TPU v7x, 128 devices: a whole 4x4x4 slice. The times are simulated.
128 devices in a mesh: blk: 64 (over y_hi, z, x, core), grp: 2 (over y_lo).
Axes of the slice: x: 4, y: 4 (y_hi: 2, y_lo: 2; y = y_hi * 2 + y_lo), z: 4, core: 2. Of those that a mesh axis runs over, the one named last changes fastest.
Arguments:
- points: float32 [3, 98304], P(None, 'blk'), may hold values from 0 to 8, as said below
- targets: float32 [16, 98304], P(None, 'blk'), may hold values from -64 to 64
- length_scales: float32 [3], replicated, may hold values from 1 to 2
- noise_levels: float32 [8], replicated, may hold values from 0.05 to 1
- noise_class: int32 [98304], P('blk'), may hold values from 0 to 7
Outputs:
- solution: float32 [16, 98304], P(None, 'blk')
- residual: float32 [16, 98304], P(None, 'blk')
Inputs may be any that keep to these rules, and one draw needn't show every extreme that they name: `points`: each coordinate of each point lies in [0, 8].
All inputs are finite; a program needn't handle non-finite values.
Results may differ from a plain program's by a relative error of at most 0.00028.
Values sent between devices are 32-bit elements; how exact they have to be, the bound alone decides.
No kernel may reach another device: no remote copies, remote signals or barrier semaphores. Data moves between devices by JAX's collectives and lax.ppermute only.
A program may use at most 64 MiB of HBM per device.

v0:
```python
import jax
import jax.numpy as jnp
from jax import lax
from jax.sharding import PartitionSpec as P


def passed_along(block, axis, distance):
    devices = range(lax.axis_size(axis))
    route = [((i - distance) % len(devices), i) for i in devices]
    return lax.ppermute(block, axis, route)


def matern(row_points, col_points, inverse_scale):
    scaled_rows = row_points * inverse_scale[:, None]
    scaled_cols = col_points * inverse_scale[:, None]
    offsets = scaled_rows[0][:, None] - scaled_cols[0][None, :]
    squared = offsets * offsets
    offsets = scaled_rows[1][:, None] - scaled_cols[1][None, :]
    squared = squared + offsets * offsets
    offsets = scaled_rows[2][:, None] - scaled_cols[2][None, :]
    squared = squared + offsets * offsets
    radius = jnp.sqrt(5.0 * squared)
    return (1.0 + radius + radius * radius / 3.0) * jnp.exp(-radius)


def rows_term(kernel_tile, far_vectors):
    return lax.dot_general(
        far_vectors,
        kernel_tile,
        (((1,), (1,)), ((), ())),
        precision=lax.Precision.HIGHEST,
        preferred_element_type=jnp.float32,
    )


def cols_term(kernel_tile, near_vectors):
    return jnp.dot(
        near_vectors,
        kernel_tile,
        precision=lax.Precision.HIGHEST,
        preferred_element_type=jnp.float32,
    )


def repeat(carried, count, advance):

    def two_steps(turn_index, inner):
        return advance(advance(inner))

    carried = lax.fori_loop(0, count // 2, two_steps, carried)
    carried = advance(carried)
    return carried


def squares(residual):
    return lax.psum(jnp.sum(residual * residual, axis=1), "blk")


def on_device(points, targets, length_scales, noise_levels, noise_class):
    inverse_scale = 1.0 / length_scales
    classes = lax.broadcasted_iota(jnp.int32, (noise_levels.shape[0], noise_class.shape[0]), 0)
    noise_diag = jnp.sum(
        jnp.where(noise_class[None, :] == classes, noise_levels[:, None], 0.0), axis=0
    )
    block_size = points.shape[1]
    row_count = block_size // lax.axis_size("grp")
    row_start = lax.axis_index("grp") * row_count
    row_points = lax.dynamic_slice_in_dim(points, row_start, row_count, 1)
    cycle_size = lax.axis_size("blk")
    half_cycle = cycle_size // 2

    def apply_kernel(vectors):
        row_vectors = lax.dynamic_slice_in_dim(vectors, row_start, row_count, 1)
        row_sums = rows_term(matern(row_points, points, inverse_scale), vectors)

        def advance_with(carried, columns):
            moved_points, moved_vectors, moved_sums, rows_now = carried
            moved_points, moved_vectors, moved_sums = passed_along(
                (moved_points, moved_vectors, moved_sums), "blk", 1
            )
            kernel_tile = matern(row_points, moved_points, inverse_scale)
            rows_now = rows_now + rows_term(kernel_tile, moved_vectors)
            if columns:
                moved_sums = moved_sums + cols_term(kernel_tile, row_vectors)
            return (moved_points, moved_vectors, moved_sums, rows_now)

        carried = (points, vectors, jnp.zeros_like(vectors), row_sums)
        carried = repeat(carried, half_cycle - 1, lambda inner: advance_with(inner, True))
        carried = advance_with(carried, False)
        returned = passed_along(carried[2], "blk", -half_cycle)
        row_sums = carried[3]
        own_part = lax.dynamic_slice_in_dim(returned, row_start, row_count, 1) + row_sums
        partial_image = lax.dynamic_update_slice_in_dim(returned, own_part, row_start, 1)
        summed = lax.psum(partial_image, "grp")
        return summed + noise_diag[None, :] * vectors

    residual = targets
    norm_now = squares(residual)
    kernel_image = apply_kernel(targets)
    curvature = lax.psum(jnp.sum(targets * kernel_image, axis=1), "blk")
    step_size = norm_now / curvature
    solution = step_size[:, None] * targets
    residual = residual - step_size[:, None] * kernel_image
    return (solution, residual)


def solution(mesh):
    return jax.shard_map(
        on_device,
        mesh=mesh,
        in_specs=(P(None, "blk"), P(None, "blk"), P(), P(), P("blk")),
        out_specs=(P(None, "blk"), P(None, "blk")),
        check_vma=False,
    )
```

profile of v0, /device:TPU:0, one launch (start us, length us, event | category | flops | bytes accessed | tf_op | source)
XLA Modules:
  0.0 1042.5 jit_solution(11664753912020013001)
XLA Ops:
  8.9 8.1 fusion.81
  17.0 770.8 %while.17 = (s32[]{:T(128)}, f32[3,1536]{1,0:T(4,128)S(1)}, f32[16,1536]{1,0:T(8,128)S(1)}, f32[16,1536]{1,0:T(8,128)S(1)}, f32[16,768]{1,0:T(8,128)S(1)}, /*ind...) while((s32[]{:T(128)}, f32[3,1536]{1,0:T(4,128)S(1)}, ...), condition=%wide.region_3.4_spmd.clone, body=%wide.region_2.3_spmd.clone.sunk | while | flops 976858368 | bytes 3096951 | solution.py:50
  47.8 8.9 collective-permute-done.1
  63.8 8.1 fusion.124
  80.1 8.1 fusion.125
  88.6 8.7 collective-permute-done
  97.3 8.9 collective-permute-done.1
  113.3 8.1 fusion.124
  129.6 8.1 fusion.125
  138.1 8.7 collective-permute-done
  146.8 8.9 collective-permute-done.1
  162.8 8.1 fusion.124
  179.1 8.1 fusion.125
  187.5 8.7 collective-permute-done
  196.3 8.9 collective-permute-done.1
  212.2 8.1 fusion.124
  228.6 8.1 fusion.125
  237.0 8.7 collective-permute-done
  245.8 8.9 collective-permute-done.1
  261.7 8.1 fusion.124
  278.1 8.1 fusion.125
  286.5 8.7 collective-permute-done
  295.2 8.9 collective-permute-done.1
  311.2 8.1 fusion.124
  327.6 8.1 fusion.125
  336.0 8.7 collective-permute-done
  344.7 8.9 collective-permute-done.1
  360.7 8.1 fusion.124
  377.1 8.1 fusion.125
  385.5 8.7 collective-permute-done
  394.2 8.9 collective-permute-done.1
  410.2 8.1 fusion.124
  426.5 8.1 fusion.125
  435.0 8.7 collective-permute-done
  443.7 8.9 collective-permute-done.1
  459.7 8.1 fusion.124
  476.0 8.1 fusion.125
  484.4 8.7 collective-permute-done
  493.2 8.9 collective-permute-done.1
  509.2 8.1 fusion.124
  525.5 8.1 fusion.125
  533.9 8.7 collective-permute-done
  542.7 8.9 collective-permute-done.1
  558.6 8.1 fusion.124
  575.0 8.1 fusion.125
  583.4 8.7 collective-permute-done
  592.2 8.9 collective-permute-done.1
  608.1 8.1 fusion.124
  624.5 8.1 fusion.125
  632.9 8.7 collective-permute-done
  641.6 8.9 collective-permute-done.1
  657.6 8.1 fusion.124
  674.0 8.1 fusion.125
  682.4 8.7 collective-permute-done
  691.1 8.9 collective-permute-done.1
  707.1 8.1 fusion.124
  731.9 8.7 collective-permute-done
  740.6 8.9 collective-permute-done.1
  756.6 8.1 fusion.124
  787.9 9.0 collective-permute-done.7
  796.9 9.0 collective-permute-done.12
  814.4 9.6 collective-permute-done.8
  842.8 22.0 %all-reduce.3.cloned.1.call-done = f32[16,1536]{1,0:T(8,128)} async-done(((f32[16,1536]{1,0:T(8,128)}), f32[16,1536]{1,0:T(8,128)}) %all-reduce.3.cloned.1.call-update) | async-done | bytes 98320 | tf_op jit(solution)/shard_map/psum | solution.py:94
  865.9 168.7 %all-reduce = (f32[16]{0:T(128)S(1)}, f32[16]{0:T(128)S(1)}) all-reduce(f32[16]{0:T(128)S(1)} %get-tuple-element.88, f32[16]{0:T(128)S(1)} %get-tuple-element.87), channel_id=1, replica_groups=mesh['blk'=64,'grp'=2] {'blk'}, use_global_device_ids=true, to_apply=%region_1.2 | all-reduce | flops 32 | bytes 256 | tf_op jit(solution)/shard_map/psum | solution.py:56
  (316 shorter events, 290.6 us)
Async XLA Ops:
  7.2 857.7 %all-reduce.3.cloned.1.call-start = ((), (), s32[]{:S(2)}) async-start(), calls=%async_computation | async-start | bytes 196608 | tf_op jit(solution)/shard_map/psum | solution.py:94
  37.8 10.0 collective-permute-start
  37.9 25.8 %collective-permute-start.2 = (f32[16,1536]{1,0:T(8,128)S(1)}, f32[16,1536]{1,0:T(8,128)S(1)}, u32[]{:S(2)}, u32[]{:S(2)}) collective-permute-start(f32[16,1536]{1,0:T(8,128)S(1)} %get-tuple-element.210), channel_id=1, source_target_pairs={{126,0},{0,2},{2,4},{4,6},{6,8},{8,10},{10,12},{12,14},{14,16},{16... | collective-permute-start | bytes 294920 | tf_op jit(solution)/shard_map/while/body/eval_jaxpr/ppermute | solution.py:10
  39.6 17.4 %collective-permute-start.4 = (f32[16,1536]{1,0:T(8,128)S(1)}, f32[16,1536]{1,0:T(8,128)S(1)}, u32[]{:S(2)}, u32[]{:S(2)}) collective-permute-start(f32[16,1536]{1,0:T(8,128)S(1)} %broadcast_select_fusion.2), channel_id=1, source_target_pairs={{126,0},{0,2},{2,4},{4,6},{6,8},{8,10},{10,12},{12,14},{14,16},{16... | collective-permute-start | bytes 294920 | tf_op jit(solution)/shard_map/while/body/eval_jaxpr/ppermute | solution.py:10
  63.6 9.8 collective-permute-start.5
  63.7 16.4 %collective-permute-start.3 = (f32[16,1536]{1,0:T(8,128)S(1)}, f32[16,1536]{1,0:T(8,128)S(1)}, u32[]{:S(2)}, u32[]{:S(2)}) collective-permute-start(f32[16,1536]{1,0:T(8,128)S(1)} %collective-permute-done.2), channel_id=1, source_target_pairs={{126,0},{0,2},{2,4},{4,6},{6,8},{8,10},{10,12},{12,14},{14,16},{16... | collective-permute-start | bytes 294920 | tf_op jit(solution)/shard_map/while/body/eval_jaxpr/ppermute | solution.py:10
  88.3 24.9 %collective-permute-start.2 = (f32[16,1536]{1,0:T(8,128)S(1)}, f32[16,1536]{1,0:T(8,128)S(1)}, u32[]{:S(2)}, u32[]{:S(2)}) collective-permute-start(f32[16,1536]{1,0:T(8,128)S(1)} %get-tuple-element.210), channel_id=1, source_target_pairs={{126,0},{0,2},{2,4},{4,6},{6,8},{8,10},{10,12},{12,14},{14,16},{16... | collective-permute-start | bytes 294920 | tf_op jit(solution)/shard_map/while/body/eval_jaxpr/ppermute | solution.py:10
  88.4 18.0 %collective-permute-start.4 = (f32[16,1536]{1,0:T(8,128)S(1)}, f32[16,1536]{1,0:T(8,128)S(1)}, u32[]{:S(2)}, u32[]{:S(2)}) collective-permute-start(f32[16,1536]{1,0:T(8,128)S(1)} %broadcast_select_fusion.2), channel_id=1, source_target_pairs={{126,0},{0,2},{2,4},{4,6},{6,8},{8,10},{10,12},{12,14},{14,16},{16... | collective-permute-start | bytes 294920 | tf_op jit(solution)/shard_map/while/body/eval_jaxpr/ppermute | solution.py:10
  113.1 9.8 collective-permute-start.5
  113.2 16.4 %collective-permute-start.3 = (f32[16,1536]{1,0:T(8,128)S(1)}, f32[16,1536]{1,0:T(8,128)S(1)}, u32[]{:S(2)}, u32[]{:S(2)}) collective-permute-start(f32[16,1536]{1,0:T(8,128)S(1)} %collective-permute-done.2), channel_id=1, source_target_pairs={{126,0},{0,2},{2,4},{4,6},{6,8},{8,10},{10,12},{12,14},{14,16},{16... | collective-permute-start | bytes 294920 | tf_op jit(solution)/shard_map/while/body/eval_jaxpr/ppermute | solution.py:10
  137.8 24.9 %collective-permute-start.2 = (f32[16,1536]{1,0:T(8,128)S(1)}, f32[16,1536]{1,0:T(8,128)S(1)}, u32[]{:S(2)}, u32[]{:S(2)}) collective-permute-start(f32[16,1536]{1,0:T(8,128)S(1)} %get-tuple-element.210), channel_id=1, source_target_pairs={{126,0},{0,2},{2,4},{4,6},{6,8},{8,10},{10,12},{12,14},{14,16},{16... | collective-permute-start | bytes 294920 | tf_op jit(solution)/shard_map/while/body/eval_jaxpr/ppermute | solution.py:10
  137.9 18.0 %collective-permute-start.4 = (f32[16,1536]{1,0:T(8,128)S(1)}, f32[16,1536]{1,0:T(8,128)S(1)}, u32[]{:S(2)}, u32[]{:S(2)}) collective-permute-start(f32[16,1536]{1,0:T(8,128)S(1)} %broadcast_select_fusion.2), channel_id=1, source_target_pairs={{126,0},{0,2},{2,4},{4,6},{6,8},{8,10},{10,12},{12,14},{14,16},{16... | collective-permute-start | bytes 294920 | tf_op jit(solution)/shard_map/while/body/eval_jaxpr/ppermute | solution.py:10
  162.6 9.8 collective-permute-start.5
  162.7 16.4 %collective-permute-start.3 = (f32[16,1536]{1,0:T(8,128)S(1)}, f32[16,1536]{1,0:T(8,128)S(1)}, u32[]{:S(2)}, u32[]{:S(2)}) collective-permute-start(f32[16,1536]{1,0:T(8,128)S(1)} %collective-permute-done.2), channel_id=1, source_target_pairs={{126,0},{0,2},{2,4},{4,6},{6,8},{8,10},{10,12},{12,14},{14,16},{16... | collective-permute-start | bytes 294920 | tf_op jit(solution)/shard_map/while/body/eval_jaxpr/ppermute | solution.py:10
  187.3 24.9 %collective-permute-start.2 = (f32[16,1536]{1,0:T(8,128)S(1)}, f32[16,1536]{1,0:T(8,128)S(1)}, u32[]{:S(2)}, u32[]{:S(2)}) collective-permute-start(f32[16,1536]{1,0:T(8,128)S(1)} %get-tuple-element.210), channel_id=1, source_target_pairs={{126,0},{0,2},{2,4},{4,6},{6,8},{8,10},{10,12},{12,14},{14,16},{16... | collective-permute-start | bytes 294920 | tf_op jit(solution)/shard_map/while/body/eval_jaxpr/ppermute | solution.py:10
  187.4 18.0 %collective-permute-start.4 = (f32[16,1536]{1,0:T(8,128)S(1)}, f32[16,1536]{1,0:T(8,128)S(1)}, u32[]{:S(2)}, u32[]{:S(2)}) collective-permute-start(f32[16,1536]{1,0:T(8,128)S(1)} %broadcast_select_fusion.2), channel_id=1, source_target_pairs={{126,0},{0,2},{2,4},{4,6},{6,8},{8,10},{10,12},{12,14},{14,16},{16... | collective-permute-start | bytes 294920 | tf_op jit(solution)/shard_map/while/body/eval_jaxpr/ppermute | solution.py:10
  212.1 9.8 collective-permute-start.5
  212.2 16.4 %collective-permute-start.3 = (f32[16,1536]{1,0:T(8,128)S(1)}, f32[16,1536]{1,0:T(8,128)S(1)}, u32[]{:S(2)}, u32[]{:S(2)}) collective-permute-start(f32[16,1536]{1,0:T(8,128)S(1)} %collective-permute-done.2), channel_id=1, source_target_pairs={{126,0},{0,2},{2,4},{4,6},{6,8},{8,10},{10,12},{12,14},{14,16},{16... | collective-permute-start | bytes 294920 | tf_op jit(solution)/shard_map/while/body/eval_jaxpr/ppermute | solution.py:10
  236.8 24.9 %collective-permute-start.2 = (f32[16,1536]{1,0:T(8,128)S(1)}, f32[16,1536]{1,0:T(8,128)S(1)}, u32[]{:S(2)}, u32[]{:S(2)}) collective-permute-start(f32[16,1536]{1,0:T(8,128)S(1)} %get-tuple-element.210), channel_id=1, source_target_pairs={{126,0},{0,2},{2,4},{4,6},{6,8},{8,10},{10,12},{12,14},{14,16},{16... | collective-permute-start | bytes 294920 | tf_op jit(solution)/shard_map/while/body/eval_jaxpr/ppermute | solution.py:10
  236.9 18.0 %collective-permute-start.4 = (f32[16,1536]{1,0:T(8,128)S(1)}, f32[16,1536]{1,0:T(8,128)S(1)}, u32[]{:S(2)}, u32[]{:S(2)}) collective-permute-start(f32[16,1536]{1,0:T(8,128)S(1)} %broadcast_select_fusion.2), channel_id=1, source_target_pairs={{126,0},{0,2},{2,4},{4,6},{6,8},{8,10},{10,12},{12,14},{14,16},{16... | collective-permute-start | bytes 294920 | tf_op jit(solution)/shard_map/while/body/eval_jaxpr/ppermute | solution.py:10
  261.6 9.8 collective-permute-start.5
  261.6 16.4 %collective-permute-start.3 = (f32[16,1536]{1,0:T(8,128)S(1)}, f32[16,1536]{1,0:T(8,128)S(1)}, u32[]{:S(2)}, u32[]{:S(2)}) collective-permute-start(f32[16,1536]{1,0:T(8,128)S(1)} %collective-permute-done.2), channel_id=1, source_target_pairs={{126,0},{0,2},{2,4},{4,6},{6,8},{8,10},{10,12},{12,14},{14,16},{16... | collective-permute-start | bytes 294920 | tf_op jit(solution)/shard_map/while/body/eval_jaxpr/ppermute | solution.py:10
  286.2 24.9 %collective-permute-start.2 = (f32[16,1536]{1,0:T(8,128)S(1)}, f32[16,1536]{1,0:T(8,128)S(1)}, u32[]{:S(2)}, u32[]{:S(2)}) collective-permute-start(f32[16,1536]{1,0:T(8,128)S(1)} %get-tuple-element.210), channel_id=1, source_target_pairs={{126,0},{0,2},{2,4},{4,6},{6,8},{8,10},{10,12},{12,14},{14,16},{16... | collective-permute-start | bytes 294920 | tf_op jit(solution)/shard_map/while/body/eval_jaxpr/ppermute | solution.py:10
  286.4 18.0 %collective-permute-start.4 = (f32[16,1536]{1,0:T(8,128)S(1)}, f32[16,1536]{1,0:T(8,128)S(1)}, u32[]{:S(2)}, u32[]{:S(2)}) collective-permute-start(f32[16,1536]{1,0:T(8,128)S(1)} %broadcast_select_fusion.2), channel_id=1, source_target_pairs={{126,0},{0,2},{2,4},{4,6},{6,8},{8,10},{10,12},{12,14},{14,16},{16... | collective-permute-start | bytes 294920 | tf_op jit(solution)/shard_map/while/body/eval_jaxpr/ppermute | solution.py:10
  311.0 9.8 collective-permute-start.5
  311.1 16.4 %collective-permute-start.3 = (f32[16,1536]{1,0:T(8,128)S(1)}, f32[16,1536]{1,0:T(8,128)S(1)}, u32[]{:S(2)}, u32[]{:S(2)}) collective-permute-start(f32[16,1536]{1,0:T(8,128)S(1)} %collective-permute-done.2), channel_id=1, source_target_pairs={{126,0},{0,2},{2,4},{4,6},{6,8},{8,10},{10,12},{12,14},{14,16},{16... | collective-permute-start | bytes 294920 | tf_op jit(solution)/shard_map/while/body/eval_jaxpr/ppermute | solution.py:10
  335.7 24.9 %collective-permute-start.2 = (f32[16,1536]{1,0:T(8,128)S(1)}, f32[16,1536]{1,0:T(8,128)S(1)}, u32[]{:S(2)}, u32[]{:S(2)}) collective-permute-start(f32[16,1536]{1,0:T(8,128)S(1)} %get-tuple-element.210), channel_id=1, source_target_pairs={{126,0},{0,2},{2,4},{4,6},{6,8},{8,10},{10,12},{12,14},{14,16},{16... | collective-permute-start | bytes 294920 | tf_op jit(solution)/shard_map/while/body/eval_jaxpr/ppermute | solution.py:10
  335.8 18.0 %collective-permute-start.4 = (f32[16,1536]{1,0:T(8,128)S(1)}, f32[16,1536]{1,0:T(8,128)S(1)}, u32[]{:S(2)}, u32[]{:S(2)}) collective-permute-start(f32[16,1536]{1,0:T(8,128)S(1)} %broadcast_select_fusion.2), channel_id=1, source_target_pairs={{126,0},{0,2},{2,4},{4,6},{6,8},{8,10},{10,12},{12,14},{14,16},{16... | collective-permute-start | bytes 294920 | tf_op jit(solution)/shard_map/while/body/eval_jaxpr/ppermute | solution.py:10
  360.5 9.8 collective-permute-start.5
  360.6 16.4 %collective-permute-start.3 = (f32[16,1536]{1,0:T(8,128)S(1)}, f32[16,1536]{1,0:T(8,128)S(1)}, u32[]{:S(2)}, u32[]{:S(2)}) collective-permute-start(f32[16,1536]{1,0:T(8,128)S(1)} %collective-permute-done.2), channel_id=1, source_target_pairs={{126,0},{0,2},{2,4},{4,6},{6,8},{8,10},{10,12},{12,14},{14,16},{16... | collective-permute-start | bytes 294920 | tf_op jit(solution)/shard_map/while/body/eval_jaxpr/ppermute | solution.py:10
  385.2 24.9 %collective-permute-start.2 = (f32[16,1536]{1,0:T(8,128)S(1)}, f32[16,1536]{1,0:T(8,128)S(1)}, u32[]{:S(2)}, u32[]{:S(2)}) collective-permute-start(f32[16,1536]{1,0:T(8,128)S(1)} %get-tuple-element.210), channel_id=1, source_target_pairs={{126,0},{0,2},{2,4},{4,6},{6,8},{8,10},{10,12},{12,14},{14,16},{16... | collective-permute-start | bytes 294920 | tf_op jit(solution)/shard_map/while/body/eval_jaxpr/ppermute | solution.py:10
  385.3 18.0 %collective-permute-start.4 = (f32[16,1536]{1,0:T(8,128)S(1)}, f32[16,1536]{1,0:T(8,128)S(1)}, u32[]{:S(2)}, u32[]{:S(2)}) collective-permute-start(f32[16,1536]{1,0:T(8,128)S(1)} %broadcast_select_fusion.2), channel_id=1, source_target_pairs={{126,0},{0,2},{2,4},{4,6},{6,8},{8,10},{10,12},{12,14},{14,16},{16... | collective-permute-start | bytes 294920 | tf_op jit(solution)/shard_map/while/body/eval_jaxpr/ppermute | solution.py:10
  410.0 9.8 collective-permute-start.5
  410.1 16.4 %collective-permute-start.3 = (f32[16,1536]{1,0:T(8,128)S(1)}, f32[16,1536]{1,0:T(8,128)S(1)}, u32[]{:S(2)}, u32[]{:S(2)}) collective-permute-start(f32[16,1536]{1,0:T(8,128)S(1)} %collective-permute-done.2), channel_id=1, source_target_pairs={{126,0},{0,2},{2,4},{4,6},{6,8},{8,10},{10,12},{12,14},{14,16},{16... | collective-permute-start | bytes 294920 | tf_op jit(solution)/shard_map/while/body/eval_jaxpr/ppermute | solution.py:10
  434.7 24.9 %collective-permute-start.2 = (f32[16,1536]{1,0:T(8,128)S(1)}, f32[16,1536]{1,0:T(8,128)S(1)}, u32[]{:S(2)}, u32[]{:S(2)}) collective-permute-start(f32[16,1536]{1,0:T(8,128)S(1)} %get-tuple-element.210), channel_id=1, source_target_pairs={{126,0},{0,2},{2,4},{4,6},{6,8},{8,10},{10,12},{12,14},{14,16},{16... | collective-permute-start | bytes 294920 | tf_op jit(solution)/shard_map/while/body/eval_jaxpr/ppermute | solution.py:10
  434.8 18.0 %collective-permute-start.4 = (f32[16,1536]{1,0:T(8,128)S(1)}, f32[16,1536]{1,0:T(8,128)S(1)}, u32[]{:S(2)}, u32[]{:S(2)}) collective-permute-start(f32[16,1536]{1,0:T(8,128)S(1)} %broadcast_select_fusion.2), channel_id=1, source_target_pairs={{126,0},{0,2},{2,4},{4,6},{6,8},{8,10},{10,12},{12,14},{14,16},{16... | collective-permute-start | bytes 294920 | tf_op jit(solution)/shard_map/while/body/eval_jaxpr/ppermute | solution.py:10
  459.5 9.8 collective-permute-start.5
  459.6 16.4 %collective-permute-start.3 = (f32[16,1536]{1,0:T(8,128)S(1)}, f32[16,1536]{1,0:T(8,128)S(1)}, u32[]{:S(2)}, u32[]{:S(2)}) collective-permute-start(f32[16,1536]{1,0:T(8,128)S(1)} %collective-permute-done.2), channel_id=1, source_target_pairs={{126,0},{0,2},{2,4},{4,6},{6,8},{8,10},{10,12},{12,14},{14,16},{16... | collective-permute-start | bytes 294920 | tf_op jit(solution)/shard_map/while/body/eval_jaxpr/ppermute | solution.py:10
  484.2 24.9 %collective-permute-start.2 = (f32[16,1536]{1,0:T(8,128)S(1)}, f32[16,1536]{1,0:T(8,128)S(1)}, u32[]{:S(2)}, u32[]{:S(2)}) collective-permute-start(f32[16,1536]{1,0:T(8,128)S(1)} %get-tuple-element.210), channel_id=1, source_target_pairs={{126,0},{0,2},{2,4},{4,6},{6,8},{8,10},{10,12},{12,14},{14,16},{16... | collective-permute-start | bytes 294920 | tf_op jit(solution)/shard_map/while/body/eval_jaxpr/ppermute | solution.py:10
  484.3 18.0 %collective-permute-start.4 = (f32[16,1536]{1,0:T(8,128)S(1)}, f32[16,1536]{1,0:T(8,128)S(1)}, u32[]{:S(2)}, u32[]{:S(2)}) collective-permute-start(f32[16,1536]{1,0:T(8,128)S(1)} %broadcast_select_fusion.2), channel_id=1, source_target_pairs={{126,0},{0,2},{2,4},{4,6},{6,8},{8,10},{10,12},{12,14},{14,16},{16... | collective-permute-start | bytes 294920 | tf_op jit(solution)/shard_map/while/body/eval_jaxpr/ppermute | solution.py:10
  509.0 9.8 collective-permute-start.5
  509.1 16.4 %collective-permute-start.3 = (f32[16,1536]{1,0:T(8,128)S(1)}, f32[16,1536]{1,0:T(8,128)S(1)}, u32[]{:S(2)}, u32[]{:S(2)}) collective-permute-start(f32[16,1536]{1,0:T(8,128)S(1)} %collective-permute-done.2), channel_id=1, source_target_pairs={{126,0},{0,2},{2,4},{4,6},{6,8},{8,10},{10,12},{12,14},{14,16},{16... | collective-permute-start | bytes 294920 | tf_op jit(solution)/shard_map/while/body/eval_jaxpr/ppermute | solution.py:10
  533.7 24.9 %collective-permute-start.2 = (f32[16,1536]{1,0:T(8,128)S(1)}, f32[16,1536]{1,0:T(8,128)S(1)}, u32[]{:S(2)}, u32[]{:S(2)}) collective-permute-start(f32[16,1536]{1,0:T(8,128)S(1)} %get-tuple-element.210), channel_id=1, source_target_pairs={{126,0},{0,2},{2,4},{4,6},{6,8},{8,10},{10,12},{12,14},{14,16},{16... | collective-permute-start | bytes 294920 | tf_op jit(solution)/shard_map/while/body/eval_jaxpr/ppermute | solution.py:10
  533.8 18.0 %collective-permute-start.4 = (f32[16,1536]{1,0:T(8,128)S(1)}, f32[16,1536]{1,0:T(8,128)S(1)}, u32[]{:S(2)}, u32[]{:S(2)}) collective-permute-start(f32[16,1536]{1,0:T(8,128)S(1)} %broadcast_select_fusion.2), channel_id=1, source_target_pairs={{126,0},{0,2},{2,4},{4,6},{6,8},{8,10},{10,12},{12,14},{14,16},{16... | collective-permute-start | bytes 294920 | tf_op jit(solution)/shard_map/while/body/eval_jaxpr/ppermute | solution.py:10
  558.5 9.8 collective-permute-start.5
  558.6 16.4 %collective-permute-start.3 = (f32[16,1536]{1,0:T(8,128)S(1)}, f32[16,1536]{1,0:T(8,128)S(1)}, u32[]{:S(2)}, u32[]{:S(2)}) collective-permute-start(f32[16,1536]{1,0:T(8,128)S(1)} %collective-permute-done.2), channel_id=1, source_target_pairs={{126,0},{0,2},{2,4},{4,6},{6,8},{8,10},{10,12},{12,14},{14,16},{16... | collective-permute-start | bytes 294920 | tf_op jit(solution)/shard_map/while/body/eval_jaxpr/ppermute | solution.py:10
  583.2 24.9 %collective-permute-start.2 = (f32[16,1536]{1,0:T(8,128)S(1)}, f32[16,1536]{1,0:T(8,128)S(1)}, u32[]{:S(2)}, u32[]{:S(2)}) collective-permute-start(f32[16,1536]{1,0:T(8,128)S(1)} %get-tuple-element.210), channel_id=1, source_target_pairs={{126,0},{0,2},{2,4},{4,6},{6,8},{8,10},{10,12},{12,14},{14,16},{16... | collective-permute-start | bytes 294920 | tf_op jit(solution)/shard_map/while/body/eval_jaxpr/ppermute | solution.py:10
  583.3 18.0 %collective-permute-start.4 = (f32[16,1536]{1,0:T(8,128)S(1)}, f32[16,1536]{1,0:T(8,128)S(1)}, u32[]{:S(2)}, u32[]{:S(2)}) collective-permute-start(f32[16,1536]{1,0:T(8,128)S(1)} %broadcast_select_fusion.2), channel_id=1, source_target_pairs={{126,0},{0,2},{2,4},{4,6},{6,8},{8,10},{10,12},{12,14},{14,16},{16... | collective-permute-start | bytes 294920 | tf_op jit(solution)/shard_map/while/body/eval_jaxpr/ppermute | solution.py:10
  607.9 9.8 collective-permute-start.5
  608.0 16.4 %collective-permute-start.3 = (f32[16,1536]{1,0:T(8,128)S(1)}, f32[16,1536]{1,0:T(8,128)S(1)}, u32[]{:S(2)}, u32[]{:S(2)}) collective-permute-start(f32[16,1536]{1,0:T(8,128)S(1)} %collective-permute-done.2), channel_id=1, source_target_pairs={{126,0},{0,2},{2,4},{4,6},{6,8},{8,10},{10,12},{12,14},{14,16},{16... | collective-permute-start | bytes 294920 | tf_op jit(solution)/shard_map/while/body/eval_jaxpr/ppermute | solution.py:10
  632.6 24.9 %collective-permute-start.2 = (f32[16,1536]{1,0:T(8,128)S(1)}, f32[16,1536]{1,0:T(8,128)S(1)}, u32[]{:S(2)}, u32[]{:S(2)}) collective-permute-start(f32[16,1536]{1,0:T(8,128)S(1)} %get-tuple-element.210), channel_id=1, source_target_pairs={{126,0},{0,2},{2,4},{4,6},{6,8},{8,10},{10,12},{12,14},{14,16},{16... | collective-permute-start | bytes 294920 | tf_op jit(solution)/shard_map/while/body/eval_jaxpr/ppermute | solution.py:10
  632.7 18.0 %collective-permute-start.4 = (f32[16,1536]{1,0:T(8,128)S(1)}, f32[16,1536]{1,0:T(8,128)S(1)}, u32[]{:S(2)}, u32[]{:S(2)}) collective-permute-start(f32[16,1536]{1,0:T(8,128)S(1)} %broadcast_select_fusion.2), channel_id=1, source_target_pairs={{126,0},{0,2},{2,4},{4,6},{6,8},{8,10},{10,12},{12,14},{14,16},{16... | collective-permute-start | bytes 294920 | tf_op jit(solution)/shard_map/while/body/eval_jaxpr/ppermute | solution.py:10
  657.5 16.4 %collective-permute-start.3 = (f32[16,1536]{1,0:T(8,128)S(1)}, f32[16,1536]{1,0:T(8,128)S(1)}, u32[]{:S(2)}, u32[]{:S(2)}) collective-permute-start(f32[16,1536]{1,0:T(8,128)S(1)} %collective-permute-done.2), channel_id=1, source_target_pairs={{126,0},{0,2},{2,4},{4,6},{6,8},{8,10},{10,12},{12,14},{14,16},{16... | collective-permute-start | bytes 294920 | tf_op jit(solution)/shard_map/while/body/eval_jaxpr/ppermute | solution.py:10
  682.1 24.9 %collective-permute-start.2 = (f32[16,1536]{1,0:T(8,128)S(1)}, f32[16,1536]{1,0:T(8,128)S(1)}, u32[]{:S(2)}, u32[]{:S(2)}) collective-permute-start(f32[16,1536]{1,0:T(8,128)S(1)} %get-tuple-element.210), channel_id=1, source_target_pairs={{126,0},{0,2},{2,4},{4,6},{6,8},{8,10},{10,12},{12,14},{14,16},{16... | collective-permute-start | bytes 294920 | tf_op jit(solution)/shard_map/while/body/eval_jaxpr/ppermute | solution.py:10
  682.2 18.0 %collective-permute-start.4 = (f32[16,1536]{1,0:T(8,128)S(1)}, f32[16,1536]{1,0:T(8,128)S(1)}, u32[]{:S(2)}, u32[]{:S(2)}) collective-permute-start(f32[16,1536]{1,0:T(8,128)S(1)} %broadcast_select_fusion.2), channel_id=1, source_target_pairs={{126,0},{0,2},{2,4},{4,6},{6,8},{8,10},{10,12},{12,14},{14,16},{16... | collective-permute-start | bytes 294920 | tf_op jit(solution)/shard_map/while/body/eval_jaxpr/ppermute | solution.py:10
  707.0 16.4 %collective-permute-start.3 = (f32[16,1536]{1,0:T(8,128)S(1)}, f32[16,1536]{1,0:T(8,128)S(1)}, u32[]{:S(2)}, u32[]{:S(2)}) collective-permute-start(f32[16,1536]{1,0:T(8,128)S(1)} %collective-permute-done.2), channel_id=1, source_target_pairs={{126,0},{0,2},{2,4},{4,6},{6,8},{8,10},{10,12},{12,14},{14,16},{16... | collective-permute-start | bytes 294920 | tf_op jit(solution)/shard_map/while/body/eval_jaxpr/ppermute | solution.py:10
  731.6 24.9 %collective-permute-start.2 = (f32[16,1536]{1,0:T(8,128)S(1)}, f32[16,1536]{1,0:T(8,128)S(1)}, u32[]{:S(2)}, u32[]{:S(2)}) collective-permute-start(f32[16,1536]{1,0:T(8,128)S(1)} %get-tuple-element.210), channel_id=1, source_target_pairs={{126,0},{0,2},{2,4},{4,6},{6,8},{8,10},{10,12},{12,14},{14,16},{16... | collective-permute-start | bytes 294920 | tf_op jit(solution)/shard_map/while/body/eval_jaxpr/ppermute | solution.py:10
  731.7 18.0 %collective-permute-start.4 = (f32[16,1536]{1,0:T(8,128)S(1)}, f32[16,1536]{1,0:T(8,128)S(1)}, u32[]{:S(2)}, u32[]{:S(2)}) collective-permute-start(f32[16,1536]{1,0:T(8,128)S(1)} %broadcast_select_fusion.2), channel_id=1, source_target_pairs={{126,0},{0,2},{2,4},{4,6},{6,8},{8,10},{10,12},{12,14},{14,16},{16... | collective-permute-start | bytes 294920 | tf_op jit(solution)/shard_map/while/body/eval_jaxpr/ppermute | solution.py:10
  756.4 9.8 collective-permute-start.5
  756.5 16.4 %collective-permute-start.3 = (f32[16,1536]{1,0:T(8,128)S(1)}, f32[16,1536]{1,0:T(8,128)S(1)}, u32[]{:S(2)}, u32[]{:S(2)}) collective-permute-start(f32[16,1536]{1,0:T(8,128)S(1)} %collective-permute-done.2), channel_id=1, source_target_pairs={{126,0},{0,2},{2,4},{4,6},{6,8},{8,10},{10,12},{12,14},{14,16},{16... | collective-permute-start | bytes 294920 | tf_op jit(solution)/shard_map/while/body/eval_jaxpr/ppermute | solution.py:10
  796.9 17.5 %collective-permute-start.10 = (f32[16,1536]{1,0:T(8,128)S(1)}, f32[16,1536]{1,0:T(8,128)S(1)}, u32[]{:S(2)}, u32[]{:S(2)}) collective-permute-start(f32[16,1536]{1,0:T(8,128)S(1)} %get-tuple-element.50), channel_id=1, source_target_pairs={{126,0},{0,2},{2,4},{4,6},{6,8},{8,10},{10,12},{12,14},{14,16},{16... | collective-permute-start | bytes 294920 | tf_op jit(solution)/shard_map/ppermute | solution.py:10
  796.9 11.1 %collective-permute-start.6 = (f32[16,1536]{1,0:T(8,128)S(1)}, f32[16,1536]{1,0:T(8,128)S(1)}, u32[]{:S(2)}, u32[]{:S(2)}) collective-permute-start(f32[16,1536]{1,0:T(8,128)S(1)} %get-tuple-element.47), channel_id=1, source_target_pairs={{126,0},{0,2},{2,4},{4,6},{6,8},{8,10},{10,12},{12,14},{14,16},{16... | collective-permute-start | bytes 294920 | tf_op jit(solution)/shard_map/ppermute | solution.py:10
  814.3 20.0 %collective-permute-start.11 = (f32[16,1536]{1,0:T(8,128)S(1)}, f32[16,1536]{1,0:T(8,128)S(1)}, u32[]{:S(2)}, u32[]{:S(2)}) collective-permute-start(f32[16,1536]{1,0:T(8,128)S(1)} %collective-permute-done.10), channel_id=1, source_target_pairs={{126,0},{0,2},{2,4},{4,6},{6,8},{8,10},{10,12},{12,14},{14,16},{16... | collective-permute-start | bytes 294920 | tf_op jit(solution)/shard_map/ppermute | solution.py:10
  824.0 10.3 collective-permute-start.9
  (40 other events, 490.3 us)
Sparse Core Ops, SparseCore 0:
  842.7 22.0 all-reduce.2
where the time goes:
time: 1050 us; the launch traced here: 1040 us
  matrix products  472 us (45%)
  waiting for transfers between devices  339 us (32%)
  blocking collectives  169 us (16%)
  loops' own time  29.5 us (3%)
  between operations  14.4 us (1%)
    ppermute x97, waiting for transfers between devices, passed_along(): return lax.ppermute(block, axis, route)  317 us
    dot_general x33, matrix products, rows_term(): lax.dot_general(far_vectors, kernel_tile, (((1,), (1,)), ((), ())), preci...  265 us
    dot_general x31, matrix products, cols_term(): jnp.dot(near_vectors, kernel_tile, precision=lax.Precision.HIGHEST, prefe...  206 us
    psum x1, blocking collectives, squares(): return lax.psum(jnp.sum(residual * residual, axis=1), 'blk')  169 us
    another operation x1, loops' own time, repeat(): carried = lax.fori_loop(0, count // 2, two_steps, carried)  29.5 us
    psum x1, waiting for transfers between devices, apply_kernel(): summed = lax.psum(partial_image, 'grp')  22 us
  transfers between devices with their start and end apart: 98, of which 50 were waited for; matrix products, arithmetic and copies ran while one was open for 33% of the time, Pallas kernels for 0%

commit v1 on v0

v1 whole, which is shorter than its diff:
```python
import math

import jax
import jax.numpy as jnp
import numpy as np
from jax import lax
from jax.experimental import pallas as pl
from jax.experimental.pallas import tpu as pltpu
from jax.sharding import PartitionSpec as P

BOTH = ("blk", "grp")
SHARD = 1536
CHUNKS = 4
SUPER = SHARD * CHUNKS
NSUPER = 16
NVEC = 16
TILE = 512
SUB = 256
LOG2E = math.log2(math.e)
SHIFT = 1.5 * LOG2E
OFFSET = 0.75 * LOG2E * LOG2E
FACTOR = 2.0**SHIFT / (3.0 * LOG2E * LOG2E)
bf16 = jnp.bfloat16
f32 = jnp.float32


def device_at(block, member):
    return (CHUNKS * block + member // 2) * 2 + member % 2


def column_route(chunk):
    route = []
    for a in range(NSUPER):
        for d in range(8):
            source = (a + (d if d else 8)) % NSUPER
            member = ((d // 2 + chunk) % CHUNKS) * 2 + d % 2
            route.append((device_at(source, member), device_at(a, d)))
    return route


def row_route(chunk):
    return [
        (device_at(a, ((d // 2 + chunk) % CHUNKS) * 2 + d % 2), device_at(a, d))
        for a in range(NSUPER)
        for d in range(8)
    ]


def backward(route):
    return [(b, a) for a, b in route]


def tile_tables():
    per = SHARD // TILE
    side = SUPER // TILE
    triangle = [(i, j) for i in range(side) for j in range(i, side)]
    cuts = [0, 20, 40, 60, 78]
    tables, counts = [], []
    for call in range(CHUNKS):
        first = SUPER // TILE
        regular = [(i, first + j, 1) for i in range(side) for j in range(per)]
        lists = [regular]
        for distances in ((0, 1), (1, 2)):
            tiles = []
            for distance in distances:
                chunk = (call - distance) % CHUNKS
                tiles += [(chunk * per + i, first + j, 1) for i in range(per) for j in range(per)]
            tiles += [(i, j, int(i != j)) for i, j in triangle[cuts[call] : cuts[call + 1]]]
            lists.append(tiles)
        longest = max(len(x) for x in lists)
        counts.append([len(x) for x in lists])
        assert all(len(x) % 2 == 0 for x in lists)
        tables.append(
            np.array(
                [[(i * TILE, j * TILE, k) for i, j, k in x + x[:1] * (longest - len(x))] for x in lists],
                np.int32,
            )
        )
    return tables, counts


def pieces(value, count):
    out = []
    for _ in range(count):
        piece = value.astype(bf16).astype(f32)
        out.append(piece)
        value = value - piece
    return out


def kernel_values(squared):
    squared = jnp.maximum(squared, 1e-12)
    shifted = -SHIFT - squared * lax.rsqrt(squared)
    return (shifted * shifted + OFFSET) * jnp.exp2(shifted)


def tile_kernel(
    table, meta, scale, x0, x1, x2, x3, y0, sums_in, curve_in,
    sums_out, column_out, curve_out,
    row_feat, col_feat, col_vec, row_vec_t, row_sum, col_sum, hi0, hi1, lo0, lo1,
):
    chunks = [x0, x1, x2, x3, y0]
    for place, chunk in enumerate(chunks):
        span = slice(place * SHARD, (place + 1) * SHARD)
        scaled = jnp.concatenate(
            [(chunk[c : c + 1, :] - 4.0) * scale[c] for c in range(3)], axis=0
        )
        a1, a2, a3 = pieces(scaled, 3)
        norm = jnp.sum(scaled * scaled, axis=0, keepdims=True)
        n1, n2, n3 = pieces(norm, 3)
        one = jnp.ones_like(norm)
        pad = jnp.zeros((8, SHARD), f32)
        columns = jnp.concatenate(
            [-2.0 * a1, -2.0 * a2, -2.0 * a1, -2.0 * a3, -2.0 * a2, -2.0 * a1,
             one, one, one, n1, n2, n3, pad], axis=0)
        col_feat[:, span] = columns.astype(bf16)
        vec_hi, vec_lo = pieces(chunk[3:19, :], 2)
        vec = jnp.concatenate([vec_hi, vec_lo], axis=0)
        col_vec[span, :] = jnp.transpose(vec).astype(bf16)
        if place < CHUNKS:
            rows = jnp.concatenate(
                [a1, a1, a2, a1, a2, a3, n1, n2, n3, one, one, one, pad], axis=0
            )
            row_feat[span, :] = jnp.transpose(rows).astype(bf16)
            row_vec_t[:, span] = vec.astype(bf16)
    for ref in (row_sum, col_sum, hi0, hi1, lo0, lo1):
        ref[...] = jnp.zeros_like(ref)
    variant = meta[0]
    count = meta[1]

    def place_of(t):
        return (
            pl.multiple_of(table[variant, t, 0], TILE),
            pl.multiple_of(table[variant, t, 1], TILE),
            table[variant, t, 2],
        )

    def produce(place, hi, lo, x):
        row, col, _ = place
        right = col_feat[:, pl.ds(pl.multiple_of(col + x, SUB), SUB)]
        for y in range(0, TILE, SUB):
            left = row_feat[pl.ds(pl.multiple_of(row + y, SUB), SUB), :]
            value = kernel_values(jnp.dot(left, right, preferred_element_type=f32))
            high = value.astype(bf16)
            hi[y : y + SUB, x : x + SUB] = high
            lo[y : y + SUB, x : x + SUB] = (value - high.astype(f32)).astype(bf16)

    def consume(place, hi, lo, x, total):
        row, col, keep = place
        span = pl.ds(pl.multiple_of(col + x, SUB), SUB)
        high, low = hi[:, x : x + SUB], lo[:, x : x + SUB]
        right = col_vec[span, :]
        part = jnp.dot(high, right, preferred_element_type=f32)
        part = part + jnp.dot(low, right, preferred_element_type=f32)
        left = row_vec_t[:, pl.ds(row, TILE)]
        column = jnp.dot(left, high, preferred_element_type=f32)
        column = column + jnp.dot(left, low, preferred_element_type=f32)
        col_sum[:, span] += column * keep.astype(f32)
        return part if total is None else total + part

    def both(ahead, ahead_hi, ahead_lo, now, hi, lo):
        total = None
        for x in range(0, TILE, SUB):
            if ahead is not None:
                produce(ahead, ahead_hi, ahead_lo, x)
            total = consume(now, hi, lo, x, total)
        row_sum[pl.ds(now[0], TILE), :] += total

    def two_tiles(u, carried):
        both(place_of(2 * u), hi0, lo0, place_of(jnp.maximum(2 * u - 1, 0)), hi1, lo1)
        both(place_of(2 * u + 1), hi1, lo1, place_of(2 * u), hi0, lo0)
        return carried

    lax.fori_loop(0, count // 2, two_tiles, 0)
    both(None, None, None, place_of(count - 1), hi1, lo1)

    curve = curve_in[...]
    for place, chunk in enumerate(chunks):
        span = slice(place * SHARD, (place + 1) * SHARD)
        total = col_sum[:, span]
        if place < CHUNKS:
            total = total + jnp.transpose(row_sum[span, :])
        total = FACTOR * (total[:NVEC] + total[NVEC:])
        product = total * chunk[3:19, :]
        for lane in range(0, SHARD, 128):
            curve = curve + product[:, lane : lane + 128]
        if place < CHUNKS:
            sums_out[:, span] = sums_in[:, span] + total
        else:
            column_out[...] = total
    curve_out[...] = curve


def run_tiles(table, meta, scale, rows, columns, sums, curve):
    vmem = pl.BlockSpec(memory_space=pltpu.VMEM)
    smem = pl.BlockSpec(memory_space=pltpu.SMEM)
    every = SUPER + SHARD
    return pl.pallas_call(
        tile_kernel,
        out_shape=[
            jax.ShapeDtypeStruct((NVEC, SUPER), f32),
            jax.ShapeDtypeStruct((NVEC, SHARD), f32),
            jax.ShapeDtypeStruct((NVEC, 128), f32),
        ],
        in_specs=[smem] * 3 + [vmem] * 7,
        out_specs=[vmem] * 3,
        scratch_shapes=[
            pltpu.VMEM((SUPER, 32), bf16),
            pltpu.VMEM((32, every), bf16),
            pltpu.VMEM((every, 32), bf16),
            pltpu.VMEM((32, SUPER), bf16),
            pltpu.VMEM((SUPER, 32), f32),
            pltpu.VMEM((32, every), f32),
        ]
        + [pltpu.VMEM((TILE, TILE), bf16)] * 4,
        compiler_params=pltpu.CompilerParams(vmem_limit_bytes=56 * 2**20),
        cost_estimate=pl.CostEstimate(
            flops=30_000_000_000, bytes_accessed=2_000_000, transcendentals=0
        ),
    )(table, meta, scale, *rows, columns, sums, curve)


def on_device(points, targets, length_scales, noise_levels, noise_class):
    shard = jnp.concatenate([points, targets], axis=0)
    columns = [lax.ppermute(shard, BOTH, column_route(c)) for c in range(CHUNKS)]
    rows = [shard] + [lax.ppermute(shard, BOTH, row_route(c)) for c in range(1, CHUNKS)]

    block = lax.axis_index("blk")
    first = (block % CHUNKS == 0) & (lax.axis_index("grp") == 0)
    variant = jnp.where(first, jnp.where(block < 32, 1, 2), 0).astype(jnp.int32)
    tables, counts = tile_tables()
    scale = (math.sqrt(5.0) * LOG2E) / length_scales

    sums = jnp.zeros((NVEC, SUPER), f32)
    curve = jnp.zeros((NVEC, 128), f32)
    returned = []
    for c in range(CHUNKS):
        count = jnp.where(variant == 0, counts[c][0], counts[c][1]).astype(jnp.int32)
        meta = jnp.stack([variant, count])
        sums, column_sums, curve = run_tiles(
            jnp.asarray(tables[c]), meta, scale, rows, columns[c], sums, curve
        )
        returned.append(lax.ppermute(column_sums, BOTH, backward(column_route(c))))
    for c in range(1, CHUNKS):
        part = sums[:, c * SHARD : (c + 1) * SHARD]
        returned.append(lax.ppermute(part, BOTH, backward(row_route(c))))

    classes = lax.broadcasted_iota(jnp.int32, (noise_levels.shape[0], noise_class.shape[0]), 0)
    noise_diag = jnp.sum(
        jnp.where(noise_class[None, :] == classes, noise_levels[:, None], 0.0), axis=0
    )
    own_noise = noise_diag[None, :] * targets
    norm = 0.5 * jnp.sum(targets * targets, axis=1)
    curvature = jnp.sum(curve, axis=1) + 0.5 * jnp.sum(targets * own_noise, axis=1)
    scalars = jnp.stack([norm, curvature])
    for k in range(6):
        scalars = scalars + lax.ppermute(scalars, "blk", [(i, i ^ (1 << k)) for i in range(64)])
    scalars = scalars + lax.ppermute(scalars, "grp", [(0, 1), (1, 0)])
    step_size = scalars[0] / scalars[1]

    own = sums[:, :SHARD]
    for part in returned:
        own = own + part
    image = own + lax.ppermute(own, "grp", [(0, 1), (1, 0)]) + own_noise
    return (step_size[:, None] * targets, targets - step_size[:, None] * image)


def solution(mesh):
    return jax.shard_map(
        on_device,
        mesh=mesh,
        in_specs=(P(None, "blk"), P(None, "blk"), P(), P(), P("blk")),
        out_specs=(P(None, "blk"), P(None, "blk")),
        check_vma=False,
    )
```

time: 1050 us -> 209 us (0.20)
  matrix products: 472 us -> 0 us
  waiting for transfers between devices: 339 us -> 22.7 us
  blocking collectives: 169 us -> 0 us
  Pallas kernels: 0 us -> 136 us
  loops' own time: 29.5 us -> 0 us
  starting transfers between devices: 10 us -> 34.9 us
  between operations: 14.4 us -> 0.79 us
    dot_general x64 -> x0, matrix products: 472 us -> none  [the longest x33 265 us: rows_term(): lax.dot_general(far_vectors, kernel_tile, (((1,), (1,)), ((), ())), preci...]
    ppermute x97 -> x22, waiting for transfers between devices: 317 us -> 22.7 us  [the longest x6 12.3 us: on_device(): lax.ppermute(scalars, 'blk', [(i, i ^ 1 << k) for i in range(64)])]
    psum x1 -> x0, blocking collectives: 169 us -> none  [squares(): return lax.psum(jnp.sum(residual * residual, axis=1), 'blk')]
    pallas_call x0 -> x4, Pallas kernels: none -> 136 us  [run_tiles(): pl.pallas_call(tile_kernel, out_shape=[jax.ShapeDtypeStruct((NVEC, SUPER)...]
    another operation x1 -> x0, loops' own time: 29.5 us -> none  [repeat(): carried = lax.fori_loop(0, count // 2, two_steps, carried)]
    ppermute x97 -> x22, starting transfers between devices: 10 us -> 34.9 us  [the longest x4 10 us: on_device(): lax.ppermute(shard, BOTH, column_route(c))]
    psum x1 -> x0, waiting for transfers between devices: 22 us -> none  [apply_kernel(): summed = lax.psum(partial_image, 'grp')]
  transfers between devices with their start and end apart: 98 -> 22, of which waited for: 50 -> 9; matrix products, arithmetic and copies ran while one was open for 33% -> 2% of each run, Pallas kernels for 0% -> 50%
where the time goes in v1:
time: 209 us; the launch traced here: 206 us
  Pallas kernels  136 us (65%)
  starting transfers between devices  34.9 us (17%)
  waiting for transfers between devices  22.7 us (11%)
  other arithmetic  5.52 us (3%)
  local copies, waits for them, and re-layouts  5.41 us (3%)
    pallas_call x4, Pallas kernels, run_tiles(): pl.pallas_call(tile_kernel, out_shape=[jax.ShapeDtypeStruct((NVEC, SUPER)...  136 us
    ppermute x6, waiting for transfers between devices, on_device(): lax.ppermute(scalars, 'blk', [(i, i ^ 1 << k) for i in range(64)])  12.3 us
    ppermute x4, starting transfers between devices, on_device(): lax.ppermute(shard, BOTH, column_route(c))  10 us
    ppermute x6, starting transfers between devices, on_device(): lax.ppermute(scalars, 'blk', [(i, i ^ 1 << k) for i in range(64)])  8.26 us
    ppermute x4, waiting for transfers between devices, on_device(): returned.append(lax.ppermute(column_sums, BOTH, backward(column_route(c))))  6.27 us
    ppermute x1, starting transfers between devices, on_device(): image = own + lax.ppermute(own, 'grp', [(0, 1), (1, 0)]) + own_noise  4.28 us
    ppermute x4, starting transfers between devices, on_device(): returned.append(lax.ppermute(column_sums, BOTH, backward(column_route(c))))  4.19 us
  transfers between devices with their start and end apart: 22, of which 9 were waited for; matrix products, arithmetic and copies ran while one was open for 2% of the time, Pallas kernels for 50%

profile of v1, /device:TPU:0, one launch (start us, length us, event | category | flops | bytes accessed | tf_op | source)
XLA Modules:
  0.0 205.7 jit_solution(15840826018413461669)
XLA Ops:
  0.6 1.0 pad_maximum_fusion.x0
  1.6 1.1 collective-permute-start
  2.7 0.7 collective-permute-start.1
  3.4 0.2 collective-permute-start.2
  3.5 3.2 %collective-permute-start.6 = (f32[19,1536]{1,0:T(8,128)S(1)}, f32[19,1536]{1,0:T(8,128)S(1)}, u32[]{:S(2)}, u32[]{:S(2)}) collective-permute-start(f32[19,1536]{1,0:T(8,128)S(1)} %pad_maximum_fusion.x0), channel_id=1, source_target_pairs={{64,0},{9,1},{18,2},{27,3},{36,4},{45,5},{54,6},{63,7},{72,8},{17,... | collective-permute-start | bytes 350216 | tf_op jit(solution)/shard_map/ppermute | solution.py:225
  6.7 3.8 %collective-permute-start.5 = (f32[19,1536]{1,0:T(8,128)S(1)}, f32[19,1536]{1,0:T(8,128)S(1)}, u32[]{:S(2)}, u32[]{:S(2)}) collective-permute-start(f32[19,1536]{1,0:T(8,128)S(1)} %pad_maximum_fusion.x0), channel_id=1, source_target_pairs={{66,0},{11,1},{20,2},{29,3},{38,4},{47,5},{48,6},{57,7},{74,8},{19... | collective-permute-start | bytes 350216 | tf_op jit(solution)/shard_map/ppermute | solution.py:225
  10.5 0.7 copy-done.15
  11.2 0.5 broadcast_divide_fusion.scale
  11.7 0.2 copy-done.3
  11.8 0.1 select_reduce_fusion
  11.9 0.1 multiply_reduce_fusion
  12.1 0.7 pad_add_fusion.1.meta
  12.7 0.6 pad_add_fusion.meta
  13.3 0.0 collective-permute-done.x1
  13.4 1.5 collective-permute-start.4
  14.8 0.0 collective-permute-done.1.x2
  14.8 1.5 collective-permute-start.3
  16.4 0.0 collective-permute-done.2.x3
  16.4 0.0 collective-permute-done.6.y0
  16.4 0.8 broadcast_in_dim.23.sums_in
  17.3 0.6 broadcast_in_dim.24.curve_in
  17.9 34.4 %shard_map.104 = (f32[16,6144]{1,0:T(8,128)}, f32[16,1536]{1,0:T(8,128)}, f32[16,128]{1,0:T(8,128)}) custom-call(s32[3,38,3]{2,1,0:T(8,128)} %constant.50.clone.table, s32[2]{0:T(128)} %pad_add_fusion.1.meta, f32[3]{0:T(128)} %broadcast_divide_fusion.scale, f32[19,1536]{1,0:T(8,128)} %copy-done.1, f32[19,1536]{1,0:T(8,128)} %copy-done.4, ...), custom_call_target="tpu_custom_call" | custom-call | flops 30000001024 | bytes 2000000 | tf_op jit(solution)/shard_map/pallas_call | solution.py:198
  52.3 0.0 collective-permute-done.5.y0
  52.3 0.7 copy-done.7
  52.9 34.6 %shard_map.105 = (f32[16,6144]{1,0:T(8,128)}, f32[16,1536]{1,0:T(8,128)}, f32[16,128]{1,0:T(8,128)}) custom-call(s32[3,38,3]{2,1,0:T(8,128)} %constant.51.clone.table, s32[2]{0:T(128)} %pad_add_fusion.1.meta, f32[3]{0:T(128)} %broadcast_divide_fusion.scale, f32[19,1536]{1,0:T(8,128)} %copy-done.1, f32[19,1536]{1,0:T(8,128)} %copy-done.4, ...), custom_call_target="tpu_custom_call" | custom-call | flops 30000001024 | bytes 2000000 | tf_op jit(solution)/shard_map/pallas_call | solution.py:198
  87.5 0.0 collective-permute-done.4.y0
  87.5 0.7 copy-done.10
  88.2 34.4 %shard_map.106 = (f32[16,6144]{1,0:T(8,128)}, f32[16,1536]{1,0:T(8,128)}, f32[16,128]{1,0:T(8,128)}) custom-call(s32[3,38,3]{2,1,0:T(8,128)} %constant.52.clone.table, s32[2]{0:T(128)} %pad_add_fusion.1.meta, f32[3]{0:T(128)} %broadcast_divide_fusion.scale, f32[19,1536]{1,0:T(8,128)} %copy-done.1, f32[19,1536]{1,0:T(8,128)} %copy-done.4, ...), custom_call_target="tpu_custom_call" | custom-call | flops 30000001024 | bytes 2000000 | tf_op jit(solution)/shard_map/pallas_call | solution.py:198
  122.6 0.0 collective-permute-done.3.y0
  122.6 0.7 copy-done.9
  123.3 32.9 %shard_map.107 = (f32[16,6144]{1,0:T(8,128)}, f32[16,1536]{1,0:T(8,128)}, f32[16,128]{1,0:T(8,128)}) custom-call(s32[3,36,3]{2,1,0:T(8,128)} %constant.53.clone.table, s32[2]{0:T(128)} %pad_add_fusion.meta, f32[3]{0:T(128)} %broadcast_divide_fusion.scale, f32[19,1536]{1,0:T(8,128)} %copy-done.1, f32[19,1536]{1,0:T(8,128)} %copy-done.4, ...), custom_call_target="tpu_custom_call" | custom-call | flops 30000001024 | bytes 2000000 | tf_op jit(solution)/shard_map/pallas_call | solution.py:198
  156.2 0.8 reduce_sum.37
  157.0 0.1 collective-permute-start.7
  157.1 0.0 copy-start.12
  157.1 0.0 copy-start.11
  157.1 1.1 fusion.5
  158.2 0.5 collective-permute-start.18
  158.7 0.0 collective-permute-done.7
  158.8 0.1 collective-permute-start.8
  158.9 2.0 collective-permute-start.19
  160.9 1.5 collective-permute-done.8
  162.4 2.8 %collective-permute-start.9 = (f32[2,16]{1,0:T(2,128)S(1)}, f32[2,16]{1,0:T(2,128)S(1)}, u32[]{:S(2)}, u32[]{:S(2)}) collective-permute-start(f32[2,16]{1,0:T(2,128)S(1)} %fusion.6), channel_id=1, source_target_pairs={{0,8},{2,10},{4,12},{6,14},{8,0},{10,2},{12,4},{14,6},{16,24},{18,... | collective-permute-start | bytes 392 | tf_op jit(solution)/shard_map/ppermute | solution.py:257
  165.3 2.3 %collective-permute-done.9 = f32[2,16]{1,0:T(2,128)S(1)} collective-permute-done((f32[2,16]{1,0:T(2,128)S(1)}, f32[2,16]{1,0:T(2,128)S(1)}, u32[]{:S(2)}, u32[]{:S(2)}) %collective-permute-start.9) | collective-permute-done | bytes 160 | tf_op jit(solution)/shard_map/ppermute | solution.py:257
  167.6 0.0 collective-permute-start.10
  167.6 3.6 %collective-permute-done.10 = f32[2,16]{1,0:T(2,128)S(1)} collective-permute-done((f32[2,16]{1,0:T(2,128)S(1)}, f32[2,16]{1,0:T(2,128)S(1)}, u32[]{:S(2)}, u32[]{:S(2)}) %collective-permute-start.10) | collective-permute-done | bytes 160 | tf_op jit(solution)/shard_map/ppermute | solution.py:257
  171.2 2.4 %collective-permute-start.11 = (f32[2,16]{1,0:T(2,128)S(1)}, f32[2,16]{1,0:T(2,128)S(1)}, u32[]{:S(2)}, u32[]{:S(2)}) collective-permute-start(f32[2,16]{1,0:T(2,128)S(1)} %add.71), channel_id=1, source_target_pairs={{0,32},{2,34},{4,36},{6,38},{8,40},{10,42},{12,44},{14,46},{16,48}... | collective-permute-start | bytes 392 | tf_op jit(solution)/shard_map/ppermute | solution.py:257
  173.6 2.7 %collective-permute-done.11 = f32[2,16]{1,0:T(2,128)S(1)} collective-permute-done((f32[2,16]{1,0:T(2,128)S(1)}, f32[2,16]{1,0:T(2,128)S(1)}, u32[]{:S(2)}, u32[]{:S(2)}) %collective-permute-start.11) | collective-permute-done | bytes 160 | tf_op jit(solution)/shard_map/ppermute | solution.py:257
  176.2 2.8 %collective-permute-start.12 = (f32[2,16]{1,0:T(2,128)S(1)}, f32[2,16]{1,0:T(2,128)S(1)}, u32[]{:S(2)}, u32[]{:S(2)}) collective-permute-start(f32[2,16]{1,0:T(2,128)S(1)} %add.72), channel_id=1, source_target_pairs={{0,64},{2,66},{4,68},{6,70},{8,72},{10,74},{12,76},{14,78},{16,80}... | collective-permute-start | bytes 392 | tf_op jit(solution)/shard_map/ppermute | solution.py:257
  179.1 0.0 collective-permute-start.20
  179.1 2.2 %collective-permute-done.12 = f32[2,16]{1,0:T(2,128)S(1)} collective-permute-done((f32[2,16]{1,0:T(2,128)S(1)}, f32[2,16]{1,0:T(2,128)S(1)}, u32[]{:S(2)}, u32[]{:S(2)}) %collective-permute-start.12) | collective-permute-done | bytes 160 | tf_op jit(solution)/shard_map/ppermute | solution.py:257
  181.3 3.8 %collective-permute-start.13 = (f32[2,16]{1,0:T(2,128)S(1)}, f32[2,16]{1,0:T(2,128)S(1)}, u32[]{:S(2)}, u32[]{:S(2)}) collective-permute-start(f32[2,16]{1,0:T(2,128)S(1)} %add.73), channel_id=1, source_target_pairs={{0,1},{1,0},{2,3},{3,2},{4,5},{5,4},{6,7},{7,6},{8,9},{9,8},{10,11... | collective-permute-start | bytes 392 | tf_op jit(solution)/shard_map/ppermute | solution.py:258
  185.1 0.0 collective-permute-start.17
  185.1 1.5 collective-permute-done.13
  186.6 1.3 collective-permute-start.16
  187.9 0.0 collective-permute-done.18
  187.9 1.1 collective-permute-start.15
  189.0 1.8 collective-permute-start.14
  190.8 1.9 collective-permute-done.17
  192.8 4.3 %collective-permute-done.16 = f32[16,1536]{1,0:T(8,128)S(1)} collective-permute-done((f32[16,1536]{1,0:T(8,128)S(1)}, f32[16,1536]{1,0:T(8,128)S(1)}, u32[]{:S(2)}, u32[]{:S(2)}) %collective-permute-start.16) | collective-permute-done | bytes 98336 | tf_op jit(solution)/shard_map/ppermute | solution.py:243
  197.1 0.0 collective-permute-done.14
  197.1 0.9 add_add_fusion
  198.0 4.3 %collective-permute-start.21 = (f32[16,1536]{1,0:T(8,128)S(1)}, f32[16,1536]{1,0:T(8,128)S(1)}, u32[]{:S(2)}, u32[]{:S(2)}) collective-permute-start(f32[16,1536]{1,0:T(8,128)S(1)} %add_add_fusion), channel_id=1, source_target_pairs={{0,1},{1,0},{2,3},{3,2},{4,5},{5,4},{6,7},{7,6},{8,9},{9,8},{10,11... | collective-permute-start | bytes 294920 | tf_op jit(solution)/shard_map/ppermute | solution.py:264
  202.3 2.6 %collective-permute-done.21 = f32[16,1536]{1,0:T(8,128)S(1)} collective-permute-done((f32[16,1536]{1,0:T(8,128)S(1)}, f32[16,1536]{1,0:T(8,128)S(1)}, u32[]{:S(2)}, u32[]{:S(2)}) %collective-permute-start.21) | collective-permute-done | bytes 98336 | tf_op jit(solution)/shard_map/ppermute | solution.py:264
  204.9 0.8 fusion.2
  (39 shorter events, 0.1 us)
Async XLA Ops:
  0.6 11.3 %copy-start = (f32[16,1536]{1,0:T(8,128)S(1)}, f32[16,1536]{1,0:T(8,128)}, u32[]{:S(2)}) copy-start(f32[16,1536]{1,0:T(8,128)} %param.10) | copy-start | bytes 294916
  1.6 15.6 %copy-start.1 = (f32[19,1536]{1,0:T(8,128)}, f32[19,1536]{1,0:T(8,128)S(1)}, u32[]{:S(2)}) copy-start(f32[19,1536]{1,0:T(8,128)S(1)} %pad_maximum_fusion.x0) | copy-start | bytes 350212
  1.6 11.7 %collective-permute-start = (f32[19,1536]{1,0:T(8,128)S(1)}, f32[19,1536]{1,0:T(8,128)S(1)}, u32[]{:S(2)}, u32[]{:S(2)}) collective-permute-start(f32[19,1536]{1,0:T(8,128)S(1)} %pad_maximum_fusion.x0), channel_id=1, source_target_pairs={{2,0},{3,1},{4,2},{5,3},{6,4},{7,5},{0,6},{1,7},{10,8},{11,9},{12,... | collective-permute-start | bytes 350216 | tf_op jit(solution)/shard_map/ppermute | solution.py:226
  2.7 12.1 %collective-permute-start.1 = (f32[19,1536]{1,0:T(8,128)S(1)}, f32[19,1536]{1,0:T(8,128)S(1)}, u32[]{:S(2)}, u32[]{:S(2)}) collective-permute-start(f32[19,1536]{1,0:T(8,128)S(1)} %pad_maximum_fusion.x0), channel_id=1, source_target_pairs={{4,0},{5,1},{6,2},{7,3},{0,4},{1,5},{2,6},{3,7},{12,8},{13,9},{14,... | collective-permute-start | bytes 350216 | tf_op jit(solution)/shard_map/ppermute | solution.py:226
  3.4 13.0 %collective-permute-start.2 = (f32[19,1536]{1,0:T(8,128)S(1)}, f32[19,1536]{1,0:T(8,128)S(1)}, u32[]{:S(2)}, u32[]{:S(2)}) collective-permute-start(f32[19,1536]{1,0:T(8,128)S(1)} %pad_maximum_fusion.x0), channel_id=1, source_target_pairs={{6,0},{7,1},{0,2},{1,3},{2,4},{3,5},{4,6},{5,7},{14,8},{15,9},{8,1... | collective-permute-start | bytes 350216 | tf_op jit(solution)/shard_map/ppermute | solution.py:226
  3.5 12.9 %collective-permute-start.6 = (f32[19,1536]{1,0:T(8,128)S(1)}, f32[19,1536]{1,0:T(8,128)S(1)}, u32[]{:S(2)}, u32[]{:S(2)}) collective-permute-start(f32[19,1536]{1,0:T(8,128)S(1)} %pad_maximum_fusion.x0), channel_id=1, source_target_pairs={{64,0},{9,1},{18,2},{27,3},{36,4},{45,5},{54,6},{63,7},{72,8},{17,... | collective-permute-start | bytes 350216 | tf_op jit(solution)/shard_map/ppermute | solution.py:225
  6.7 45.6 %collective-permute-start.5 = (f32[19,1536]{1,0:T(8,128)S(1)}, f32[19,1536]{1,0:T(8,128)S(1)}, u32[]{:S(2)}, u32[]{:S(2)}) collective-permute-start(f32[19,1536]{1,0:T(8,128)S(1)} %pad_maximum_fusion.x0), channel_id=1, source_target_pairs={{66,0},{11,1},{20,2},{29,3},{38,4},{47,5},{48,6},{57,7},{74,8},{19... | collective-permute-start | bytes 350216 | tf_op jit(solution)/shard_map/ppermute | solution.py:225
  10.5 1.2 copy-start.2
  10.5 0.7 copy-start.15
  11.2 0.7 copy-start.3
  13.4 3.9 %copy-start.4 = (f32[19,1536]{1,0:T(8,128)}, f32[19,1536]{1,0:T(8,128)S(1)}, u32[]{:S(2)}) copy-start(f32[19,1536]{1,0:T(8,128)S(1)} %collective-permute-done.x1) | copy-start | bytes 350212
  13.4 74.1 %collective-permute-start.4 = (f32[19,1536]{1,0:T(8,128)S(1)}, f32[19,1536]{1,0:T(8,128)S(1)}, u32[]{:S(2)}, u32[]{:S(2)}) collective-permute-start(f32[19,1536]{1,0:T(8,128)S(1)} %pad_maximum_fusion.x0), channel_id=1, source_target_pairs={{68,0},{13,1},{22,2},{31,3},{32,4},{41,5},{50,6},{59,7},{76,8},{21... | collective-permute-start | bytes 350216 | tf_op jit(solution)/shard_map/ppermute | solution.py:225
  14.8 2.4 %copy-start.5 = (f32[19,1536]{1,0:T(8,128)}, f32[19,1536]{1,0:T(8,128)S(1)}, u32[]{:S(2)}) copy-start(f32[19,1536]{1,0:T(8,128)S(1)} %collective-permute-done.1.x2) | copy-start | bytes 350212
  14.8 107.8 %collective-permute-start.3 = (f32[19,1536]{1,0:T(8,128)S(1)}, f32[19,1536]{1,0:T(8,128)S(1)}, u32[]{:S(2)}, u32[]{:S(2)}) collective-permute-start(f32[19,1536]{1,0:T(8,128)S(1)} %pad_maximum_fusion.x0), channel_id=1, source_target_pairs={{70,0},{15,1},{16,2},{25,3},{34,4},{43,5},{52,6},{61,7},{78,8},{23... | collective-permute-start | bytes 350216 | tf_op jit(solution)/shard_map/ppermute | solution.py:225
  16.4 1.5 copy-start.6
  16.4 1.5 copy-start.8
  52.3 0.7 copy-start.7
  87.5 0.7 copy-start.10
  122.6 0.7 copy-start.9
  157.0 1.7 collective-permute-start.7
  157.1 28.0 %copy-start.14 = (f32[16,1536]{1,0:T(8,128)S(1)}, f32[16,1536]{1,0:T(8,128)}, u32[]{:S(2)}) copy-start(f32[16,1536]{1,0:T(8,128)} %get-tuple-element.25) | copy-start | bytes 294916
  157.1 29.5 %copy-start.13 = (f32[16,1536]{1,0:T(8,128)S(1)}, f32[16,1536]{1,0:T(8,128)}, u32[]{:S(2)}) copy-start(f32[16,1536]{1,0:T(8,128)} %get-tuple-element.24) | copy-start | bytes 294916
  157.1 30.8 %copy-start.12 = (f32[16,1536]{1,0:T(8,128)S(1)}, f32[16,1536]{1,0:T(8,128)}, u32[]{:S(2)}) copy-start(f32[16,1536]{1,0:T(8,128)} %get-tuple-element.23) | copy-start | bytes 294916
  157.1 31.8 %copy-start.11 = (f32[16,1536]{1,0:T(8,128)S(1)}, f32[16,1536]{1,0:T(8,128)}, u32[]{:S(2)}) copy-start(f32[16,1536]{1,0:T(8,128)} %get-tuple-element.22) | copy-start | bytes 294916
  158.2 29.7 %collective-permute-start.18 = (f32[16,1536]{1,0:T(8,128)S(1)}, f32[16,1536]{1,0:T(8,128)S(1)}, u32[]{:S(2)}, u32[]{:S(2)}) collective-permute-start(f32[16,1536]{1,0:T(8,128)S(1)} %get-tuple-element.28), channel_id=1, source_target_pairs={{0,2},{1,3},{2,4},{3,5},{4,6},{5,7},{6,0},{7,1},{8,10},{9,11},{10,... | collective-permute-start | bytes 294920 | tf_op jit(solution)/shard_map/ppermute | solution.py:246
  158.8 3.6 %collective-permute-start.8 = (f32[2,16]{1,0:T(2,128)S(1)}, f32[2,16]{1,0:T(2,128)S(1)}, u32[]{:S(2)}, u32[]{:S(2)}) collective-permute-start(f32[2,16]{1,0:T(2,128)S(1)} %fusion.4), channel_id=1, source_target_pairs={{0,4},{2,6},{4,0},{6,2},{8,12},{10,14},{12,8},{14,10},{16,20},{18,... | collective-permute-start | bytes 392 | tf_op jit(solution)/shard_map/ppermute | solution.py:257
  158.9 30.1 %collective-permute-start.19 = (f32[16,1536]{1,0:T(8,128)S(1)}, f32[16,1536]{1,0:T(8,128)S(1)}, u32[]{:S(2)}, u32[]{:S(2)}) collective-permute-start(f32[16,1536]{1,0:T(8,128)S(1)} %get-tuple-element.30), channel_id=1, source_target_pairs={{0,4},{1,5},{2,6},{3,7},{4,0},{5,1},{6,2},{7,3},{8,12},{9,13},{10,... | collective-permute-start | bytes 294920 | tf_op jit(solution)/shard_map/ppermute | solution.py:246
  162.4 5.2 %collective-permute-start.9 = (f32[2,16]{1,0:T(2,128)S(1)}, f32[2,16]{1,0:T(2,128)S(1)}, u32[]{:S(2)}, u32[]{:S(2)}) collective-permute-start(f32[2,16]{1,0:T(2,128)S(1)} %fusion.6), channel_id=1, source_target_pairs={{0,8},{2,10},{4,12},{6,14},{8,0},{10,2},{12,4},{14,6},{16,24},{18,... | collective-permute-start | bytes 392 | tf_op jit(solution)/shard_map/ppermute | solution.py:257
  167.6 3.6 %collective-permute-start.10 = (f32[2,16]{1,0:T(2,128)S(1)}, f32[2,16]{1,0:T(2,128)S(1)}, u32[]{:S(2)}, u32[]{:S(2)}) collective-permute-start(f32[2,16]{1,0:T(2,128)S(1)} %add.70), channel_id=1, source_target_pairs={{0,16},{2,18},{4,20},{6,22},{8,24},{10,26},{12,28},{14,30},{16,0},... | collective-permute-start | bytes 392 | tf_op jit(solution)/shard_map/ppermute | solution.py:257
  171.2 5.1 %collective-permute-start.11 = (f32[2,16]{1,0:T(2,128)S(1)}, f32[2,16]{1,0:T(2,128)S(1)}, u32[]{:S(2)}, u32[]{:S(2)}) collective-permute-start(f32[2,16]{1,0:T(2,128)S(1)} %add.71), channel_id=1, source_target_pairs={{0,32},{2,34},{4,36},{6,38},{8,40},{10,42},{12,44},{14,46},{16,48}... | collective-permute-start | bytes 392 | tf_op jit(solution)/shard_map/ppermute | solution.py:257
  176.2 5.1 %collective-permute-start.12 = (f32[2,16]{1,0:T(2,128)S(1)}, f32[2,16]{1,0:T(2,128)S(1)}, u32[]{:S(2)}, u32[]{:S(2)}) collective-permute-start(f32[2,16]{1,0:T(2,128)S(1)} %add.72), channel_id=1, source_target_pairs={{0,64},{2,66},{4,68},{6,70},{8,72},{10,74},{12,76},{14,78},{16,80}... | collective-permute-start | bytes 392 | tf_op jit(solution)/shard_map/ppermute | solution.py:257
  179.1 11.8 %collective-permute-start.20 = (f32[16,1536]{1,0:T(8,128)S(1)}, f32[16,1536]{1,0:T(8,128)S(1)}, u32[]{:S(2)}, u32[]{:S(2)}) collective-permute-start(f32[16,1536]{1,0:T(8,128)S(1)} %get-tuple-element.29), channel_id=1, source_target_pairs={{0,6},{1,7},{2,0},{3,1},{4,2},{5,3},{6,4},{7,5},{8,14},{9,15},{10,... | collective-permute-start | bytes 294920 | tf_op jit(solution)/shard_map/ppermute | solution.py:246
  181.3 5.3 %collective-permute-start.13 = (f32[2,16]{1,0:T(2,128)S(1)}, f32[2,16]{1,0:T(2,128)S(1)}, u32[]{:S(2)}, u32[]{:S(2)}) collective-permute-start(f32[2,16]{1,0:T(2,128)S(1)} %add.73), channel_id=1, source_target_pairs={{0,1},{1,0},{2,3},{3,2},{4,5},{5,4},{6,7},{7,6},{8,9},{9,8},{10,11... | collective-permute-start | bytes 392 | tf_op jit(solution)/shard_map/ppermute | solution.py:258
  185.1 7.7 %collective-permute-start.17 = (f32[16,1536]{1,0:T(8,128)S(1)}, f32[16,1536]{1,0:T(8,128)S(1)}, u32[]{:S(2)}, u32[]{:S(2)}) collective-permute-start(f32[16,1536]{1,0:T(8,128)S(1)} %copy-done.14), channel_id=1, source_target_pairs={{0,70},{1,15},{2,16},{3,25},{4,34},{5,43},{6,52},{7,61},{8,78},{9,... | collective-permute-start | bytes 294920 | tf_op jit(solution)/shard_map/ppermute | solution.py:243
  186.6 10.5 %collective-permute-start.16 = (f32[16,1536]{1,0:T(8,128)S(1)}, f32[16,1536]{1,0:T(8,128)S(1)}, u32[]{:S(2)}, u32[]{:S(2)}) collective-permute-start(f32[16,1536]{1,0:T(8,128)S(1)} %copy-done.13), channel_id=1, source_target_pairs={{0,68},{1,13},{2,22},{3,31},{4,32},{5,41},{6,50},{7,59},{8,76},{9,... | collective-permute-start | bytes 294920 | tf_op jit(solution)/shard_map/ppermute | solution.py:243
  187.9 9.2 %collective-permute-start.15 = (f32[16,1536]{1,0:T(8,128)S(1)}, f32[16,1536]{1,0:T(8,128)S(1)}, u32[]{:S(2)}, u32[]{:S(2)}) collective-permute-start(f32[16,1536]{1,0:T(8,128)S(1)} %copy-done.12), channel_id=1, source_target_pairs={{0,66},{1,11},{2,20},{3,29},{4,38},{5,47},{6,48},{7,57},{8,74},{9,... | collective-permute-start | bytes 294920 | tf_op jit(solution)/shard_map/ppermute | solution.py:243
  189.0 8.1 %collective-permute-start.14 = (f32[16,1536]{1,0:T(8,128)S(1)}, f32[16,1536]{1,0:T(8,128)S(1)}, u32[]{:S(2)}, u32[]{:S(2)}) collective-permute-start(f32[16,1536]{1,0:T(8,128)S(1)} %copy-done.11), channel_id=1, source_target_pairs={{0,64},{1,9},{2,18},{3,27},{4,36},{5,45},{6,54},{7,63},{8,72},{9,1... | collective-permute-start | bytes 294920 | tf_op jit(solution)/shard_map/ppermute | solution.py:243
  198.0 6.9 %collective-permute-start.21 = (f32[16,1536]{1,0:T(8,128)S(1)}, f32[16,1536]{1,0:T(8,128)S(1)}, u32[]{:S(2)}, u32[]{:S(2)}) collective-permute-start(f32[16,1536]{1,0:T(8,128)S(1)} %add_add_fusion), channel_id=1, source_target_pairs={{0,1},{1,0},{2,3},{3,2},{4,5},{5,4},{6,7},{7,6},{8,9},{9,8},{10,11... | collective-permute-start | bytes 294920 | tf_op jit(solution)/shard_map/ppermute | solution.py:264

commit v2 on v1

v2 whole, which is shorter than its diff:
```python
import functools
import math

import jax
import jax.numpy as jnp
import numpy as np
from jax import lax
from jax.experimental import pallas as pl
from jax.experimental.pallas import tpu as pltpu
from jax.sharding import PartitionSpec as P

BOTH = ("blk", "grp")
SHARD = 1536
CHUNKS = 4
SUPER = SHARD * CHUNKS
NSUPER = 16
NVEC = 16
TILE = 512
SUB = 256
LOG2E = math.log2(math.e)
SHIFT = 1.5 * LOG2E
OFFSET = 0.75 * LOG2E * LOG2E
FACTOR = 2.0**SHIFT / (3.0 * LOG2E * LOG2E)
bf16 = jnp.bfloat16
f32 = jnp.float32


def device_at(block, member):
    return (CHUNKS * block + member // 2) * 2 + member % 2


def column_route(chunk):
    route = []
    for a in range(NSUPER):
        for d in range(8):
            source = (a + (d if d else 8)) % NSUPER
            member = ((d // 2 + chunk) % CHUNKS) * 2 + d % 2
            route.append((device_at(source, member), device_at(a, d)))
    return route


def row_route(chunk):
    return [
        (device_at(a, ((d // 2 + chunk) % CHUNKS) * 2 + d % 2), device_at(a, d))
        for a in range(NSUPER)
        for d in range(8)
    ]


def backward(route):
    return [(b, a) for a, b in route]


CALLS = [((0, 1, 2, 3), (0,)), ((0, 1, 2, 3), (1,)), ((1, 2, 3), (2, 3)), ((0,), (2, 3))]
OFF = [(1, 0), (2, 1), (3, 1), (0, 2), (0, 3), (2, 3)]
ON = [[(0, 0), (1, 1)], [(2, 2), (3, 3)]]
FILL = [[20, 11, 47, 0], [29, 20, 29, 0]]


def tile_tables():
    per = SHARD // TILE
    side = SUPER // TILE
    triangle = [(i, j) for i in range(side) for j in range(i, side)]
    used = [0, 0]
    tables, counts = [], []
    for call, (rows, columns) in enumerate(CALLS):
        held = (0, 1, 2, 3) if len(rows) > 1 else rows

        def pair(i, j):
            first = (len(held) + columns.index(j)) * per
            return [
                (held.index(i) * per + y, first + x, 1) for y in range(per) for x in range(per)
            ]

        lists = [[t for i in rows for j in columns for t in pair(i, j)]]
        for half in range(2):
            chunks = [(i, j) for i, j in OFF + ON[half] if i in rows and j in columns]
            tiles = [t for i, j in chunks for t in pair(i, j)]
            part = triangle[used[half] : used[half] + FILL[half][call]]
            used[half] += len(part)
            tiles += [(i, j, int(i != j)) for i, j in part]
            lists.append(tiles)
        longest = max(len(x) for x in lists)
        counts.append([len(x) for x in lists])
        assert all(len(x) % 2 == 0 for x in lists)
        tables.append(
            np.array(
                [
                    [(i * TILE, j * TILE, k) for i, j, k in x + x[:1] * (longest - len(x))]
                    for x in lists
                ],
                np.int32,
            )
        )
    assert used == [len(triangle)] * 2
    return tables, counts


def pieces(value, count):
    out = []
    for _ in range(count):
        piece = value.astype(bf16).astype(f32)
        out.append(piece)
        value = value - piece
    return out


def kernel_values(squared):
    squared = jnp.maximum(squared, 1e-12)
    shifted = -SHIFT - squared * lax.rsqrt(squared)
    return (shifted * shifted + OFFSET) * jnp.exp2(shifted)


def tile_kernel(x_count, y_count, chained, *refs):
    refs = list(refs)
    table, meta, scale = refs[:3]
    chunks = refs[3 : 3 + x_count + y_count]
    rest = refs[3 + x_count + y_count :]
    if chained:
        sums_in, curve_in, rest = rest[:x_count], rest[x_count], rest[x_count + 1 :]
    sums_out, rest = rest[: x_count + y_count], rest[x_count + y_count :]
    curve_out, row_feat, col_feat, vectors, row_sum, col_sum, hi0, hi1, lo0, lo1 = rest

    for place, chunk in enumerate(chunks):
        span = slice(place * SHARD, (place + 1) * SHARD)
        scaled = jnp.concatenate(
            [(chunk[c : c + 1, :] - 4.0) * scale[c] for c in range(3)], axis=0
        )
        a1, a2, a3 = pieces(scaled, 3)
        norm = jnp.sum(scaled * scaled, axis=0, keepdims=True)
        n1, n2, n3 = pieces(norm, 3)
        one = jnp.ones_like(norm)
        pad = jnp.zeros((8, SHARD), f32)
        columns = jnp.concatenate(
            [-2.0 * a1, -2.0 * a2, -2.0 * a1, -2.0 * a3, -2.0 * a2, -2.0 * a1,
             one, one, one, n1, n2, n3, pad], axis=0)
        col_feat[:, span] = columns.astype(bf16)
        vectors[:, span] = jnp.concatenate(pieces(chunk[3:19, :], 2), axis=0).astype(bf16)
        if place < x_count:
            rows = jnp.concatenate(
                [a1, a1, a2, a1, a2, a3, n1, n2, n3, one, one, one, pad], axis=0
            )
            row_feat[span, :] = jnp.transpose(rows).astype(bf16)
    for ref in (row_sum, col_sum, hi1, lo1):
        ref[...] = jnp.zeros_like(ref)
    variant = meta[0]
    count = meta[1]

    def place_of(t):
        return (
            pl.multiple_of(table[variant, t, 0], TILE),
            pl.multiple_of(table[variant, t, 1], TILE),
            table[variant, t, 2],
        )

    def produce(place, hi, lo, x):
        row, col, _ = place
        right = col_feat[:, pl.ds(pl.multiple_of(col + x, SUB), SUB)]
        for y in range(0, TILE, SUB):
            left = row_feat[pl.ds(pl.multiple_of(row + y, SUB), SUB), :]
            value = kernel_values(jnp.dot(left, right, preferred_element_type=f32))
            high = value.astype(bf16)
            hi[y : y + SUB, x : x + SUB] = high
            lo[y : y + SUB, x : x + SUB] = (value - high.astype(f32)).astype(bf16)

    def consume(place, hi, lo, x):
        row, col, keep = place
        across = (((1,), (1,)), ((), ()))
        span = pl.ds(pl.multiple_of(col + x, SUB), SUB)
        high, low = hi[:, x : x + SUB], lo[:, x : x + SUB]
        far, near = vectors[:, span], vectors[:, pl.ds(row, TILE)]
        part = lax.dot_general(far, high, across, preferred_element_type=f32)
        part = part + lax.dot_general(far, low, across, preferred_element_type=f32)
        row_sum[:, pl.ds(row, TILE)] += part
        part = jnp.dot(near, high, preferred_element_type=f32)
        part = part + jnp.dot(near, low, preferred_element_type=f32)
        col_sum[:, span] += part * keep.astype(f32)

    def both(ahead, ahead_hi, ahead_lo, now, hi, lo):
        for x in range(0, TILE, SUB):
            if ahead is not None:
                produce(ahead, ahead_hi, ahead_lo, x)
            consume(now, hi, lo, x)

    def two_tiles(u, carried):
        both(place_of(2 * u), hi0, lo0, place_of(jnp.maximum(2 * u - 1, 0)), hi1, lo1)
        both(place_of(2 * u + 1), hi1, lo1, place_of(2 * u), hi0, lo0)
        return carried

    lax.fori_loop(0, count // 2, two_tiles, 0)
    both(None, None, None, place_of(count - 1), hi1, lo1)

    curve = curve_in[...] if chained else jnp.zeros((NVEC, 128), f32)
    for place, chunk in enumerate(chunks):
        span = slice(place * SHARD, (place + 1) * SHARD)
        total = col_sum[:, span]
        if place < x_count:
            total = total + row_sum[:, span]
        total = FACTOR * (total[:NVEC] + total[NVEC:])
        product = total * chunk[3:19, :]
        for lane in range(0, SHARD, 128):
            curve = curve + product[:, lane : lane + 128]
        if chained and place < x_count:
            total = total + sums_in[place][...]
        sums_out[place][...] = total
    curve_out[...] = curve


def run_tiles(table, meta, scale, rows, columns, sums, curve):
    vmem = pl.BlockSpec(memory_space=pltpu.VMEM)
    smem = pl.BlockSpec(memory_space=pltpu.SMEM)
    count = len(rows) + len(columns)
    wide = len(rows) * SHARD
    every = count * SHARD
    chained = curve is not None
    passed = [*rows, *columns, *sums, curve] if chained else [*rows, *columns]
    out = pl.pallas_call(
        functools.partial(tile_kernel, len(rows), len(columns), chained),
        out_shape=[jax.ShapeDtypeStruct((NVEC, SHARD), f32)] * count
        + [jax.ShapeDtypeStruct((NVEC, 128), f32)],
        in_specs=[smem] * 3 + [vmem] * len(passed),
        out_specs=[vmem] * (count + 1),
        scratch_shapes=[
            pltpu.VMEM((wide, 32), bf16),
            pltpu.VMEM((32, every), bf16),
            pltpu.VMEM((32, every), bf16),
            pltpu.VMEM((32, wide), f32),
            pltpu.VMEM((32, every), f32),
        ]
        + [pltpu.VMEM((TILE, TILE), bf16)] * 4,
        compiler_params=pltpu.CompilerParams(vmem_limit_bytes=48 * 2**20),
        cost_estimate=pl.CostEstimate(
            flops=800_000_000 * table.shape[1], bytes_accessed=2_000_000, transcendentals=0
        ),
    )(table, meta, scale, *passed)
    return out[: len(rows)], out[len(rows) : count], out[count]


def summed_over_devices(value, own):
    def along(value, axis, size, masks):
        routes = [[(i, i ^ mask) for i in range(size)] for mask in masks]
        parts = [lax.ppermute(value, axis, route) for route in routes]
        return value, parts

    def added(value, parts):
        if len(parts) == 1:
            return value + parts[0]
        return (value + parts[0]) + (parts[1] + parts[2])

    value = added(*along(value, "blk", 64, [1]))
    value = added(*along(value, "blk", 64, [2, 4, 6]))
    value, own = lax.optimization_barrier((value, own))
    value = added(*along(value, "blk", 64, [8, 16, 24]))
    value = added(*along(value, BOTH, 128, [1, 64, 65]))
    return value, own


def on_device(points, targets, length_scales, noise_levels, noise_class):
    shard = jnp.concatenate([points, targets], axis=0)
    columns = [lax.ppermute(shard, BOTH, column_route(c)) for c in range(CHUNKS)]
    rows = [shard] + [lax.ppermute(shard, BOTH, row_route(c)) for c in range(1, CHUNKS)]

    block = lax.axis_index("blk")
    first = (block % CHUNKS == 0) & (lax.axis_index("grp") == 0)
    variant = jnp.where(first, jnp.where(block < 32, 1, 2), 0).astype(jnp.int32)
    tables, counts = tile_tables()
    scale = (math.sqrt(5.0) * LOG2E) / length_scales

    sums, curve = None, None
    column_sums = {}
    returned = []
    for call, (row_chunks, column_chunks) in enumerate(CALLS):
        count = jnp.where(variant == 0, counts[call][0], counts[call][1]).astype(jnp.int32)
        meta = jnp.stack([variant, count])
        held = rows if len(row_chunks) > 1 else [rows[c] for c in row_chunks]
        before = sums if len(row_chunks) > 1 else [sums[c] for c in row_chunks]
        after, column_part, curve = run_tiles(
            jnp.asarray(tables[call]), meta, scale, held, [columns[c] for c in column_chunks],
            before, curve,
        )
        if len(row_chunks) > 1:
            sums = after
        for c, part in zip(column_chunks, column_part):
            column_sums[c] = column_sums[c] + part if c in column_sums else part
        if call == 2:
            for c in range(1, CHUNKS):
                returned.append(lax.ppermute(sums[c], BOTH, backward(row_route(c))))
        if call < 2:
            c = column_chunks[0]
            returned.append(lax.ppermute(column_sums[c], BOTH, backward(column_route(c))))
    last = [lax.ppermute(column_sums[c], BOTH, backward(column_route(c))) for c in (2, 3)]

    classes = lax.broadcasted_iota(jnp.int32, (noise_levels.shape[0], noise_class.shape[0]), 0)
    noise_diag = jnp.sum(
        jnp.where(noise_class[None, :] == classes, noise_levels[:, None], 0.0), axis=0
    )
    own_noise = noise_diag[None, :] * targets
    norm = 0.5 * jnp.sum(targets * targets, axis=1)
    curvature = jnp.sum(curve, axis=1) + 0.5 * jnp.sum(targets * own_noise, axis=1)

    own = after[0]
    for part in returned + last:
        own = own + part
    scalars, own = summed_over_devices(jnp.stack([norm, curvature]), own)
    step_size = scalars[0] / scalars[1]
    image = own + lax.ppermute(own, "grp", [(0, 1), (1, 0)]) + own_noise
    return (step_size[:, None] * targets, targets - step_size[:, None] * image)


def solution(mesh):
    return jax.shard_map(
        on_device,
        mesh=mesh,
        in_specs=(P(None, "blk"), P(None, "blk"), P(), P(), P("blk")),
        out_specs=(P(None, "blk"), P(None, "blk")),
        check_vma=False,
    )
```

time: 209 us -> 178 us (0.85)
  Pallas kernels: 136 us -> 115 us
  waiting for transfers between devices: 22.7 us -> 10.2 us
  starting transfers between devices: 34.9 us -> 45.1 us
  local copies, waits for them, and re-layouts: 5.41 us -> 1.27 us
  other arithmetic: 5.52 us -> 2.43 us
    pallas_call x4, Pallas kernels: 136 us -> 115 us  [run_tiles(): pl.pallas_call(functools.partial(tile_kernel, len(rows), len(columns), ch...]
    ppermute x14 -> x17, waiting for transfers between devices: 20.1 us -> 10.2 us  [the longest x10 6.43 us: along(): parts = [lax.ppermute(value, axis, route) for route in routes]]
    ppermute x14 -> x17, starting transfers between devices: 18.7 us -> 26.8 us  [the longest x10 14.9 us: along(): parts = [lax.ppermute(value, axis, route) for route in routes]]
    ppermute x1, waiting for transfers between devices: 2.59 us -> 0.01 us  [on_device(): image = own + lax.ppermute(own, 'grp', [(0, 1), (1, 0)]) + own_noise]
    ppermute x1, starting transfers between devices: 4.28 us -> 6.38 us  [on_device(): image = own + lax.ppermute(own, 'grp', [(0, 1), (1, 0)]) + own_noise]
  transfers between devices with their start and end apart: 22 -> 25, of which waited for: 9 -> 6; matrix products, arithmetic and copies ran while one was open for 2% -> 0% of each run, Pallas kernels for 50% -> 33%
where the time goes in v2:
time: 178 us; the launch traced here: 175 us
  Pallas kernels  115 us (65%)
  starting transfers between devices  45.1 us (25%)
  waiting for transfers between devices  10.2 us (6%)
  other arithmetic  2.43 us (1%)
    pallas_call x4, Pallas kernels, run_tiles(): pl.pallas_call(functools.partial(tile_kernel, len(rows), len(columns), ch...  115 us
    ppermute x10, starting transfers between devices, along(): parts = [lax.ppermute(value, axis, route) for route in routes]  14.9 us
    ppermute x4, starting transfers between devices, on_device(): lax.ppermute(shard, BOTH, column_route(c))  10.1 us
    ppermute x4, starting transfers between devices, on_device(): lax.ppermute(column_sums[c], BOTH, backward(column_route(c)))  9.9 us
    ppermute x10, waiting for transfers between devices, along(): parts = [lax.ppermute(value, axis, route) for route in routes]  6.43 us
    ppermute x1, starting transfers between devices, on_device(): image = own + lax.ppermute(own, 'grp', [(0, 1), (1, 0)]) + own_noise  6.38 us
    ppermute x4, waiting for transfers between devices, on_device(): lax.ppermute(column_sums[c], BOTH, backward(column_route(c)))  3.75 us
  transfers between devices with their start and end apart: 25, of which 6 were waited for; matrix products, arithmetic and copies ran while one was open for 0% of the time, Pallas kernels for 33%

profile of v2, /device:TPU:0, one launch (start us, length us, event | category | flops | bytes accessed | tf_op | source)
XLA Modules:
  0.0 175.0 jit_solution(15879860984954094461)
XLA Ops:
  0.6 1.0 pad_maximum_fusion.refs_3_
  1.6 1.1 collective-permute-start.2
  2.7 0.7 collective-permute-start.3
  3.4 0.2 collective-permute-start.4
  3.5 3.2 %collective-permute-start.6 = (f32[19,1536]{1,0:T(8,128)S(1)}, f32[19,1536]{1,0:T(8,128)S(1)}, u32[]{:S(2)}, u32[]{:S(2)}) collective-permute-start(f32[19,1536]{1,0:T(8,128)S(1)} %pad_maximum_fusion.refs_3_), channel_id=1, source_target_pairs={{64,0},{9,1},{18,2},{27,3},{36,4},{45,5},{54,6},{63,7},{72,8},{17,... | collective-permute-start | bytes 350216 | tf_op jit(solution)/shard_map/ppermute | solution.py:260
  6.7 3.8 %collective-permute-start.5 = (f32[19,1536]{1,0:T(8,128)S(1)}, f32[19,1536]{1,0:T(8,128)S(1)}, u32[]{:S(2)}, u32[]{:S(2)}) collective-permute-start(f32[19,1536]{1,0:T(8,128)S(1)} %pad_maximum_fusion.refs_3_), channel_id=1, source_target_pairs={{66,0},{11,1},{20,2},{29,3},{38,4},{47,5},{48,6},{57,7},{74,8},{19... | collective-permute-start | bytes 350216 | tf_op jit(solution)/shard_map/ppermute | solution.py:260
  10.5 0.7 copy-done.7
  11.2 0.1 pad_add_fusion.2.refs_1_
  11.2 0.1 pad_add_fusion.1.refs_1_
  11.3 0.1 pad_add_fusion.refs_1_
  11.4 0.5 copy-done.5
  11.9 0.1 copy-done.6
  12.0 0.1 select_reduce_fusion
  12.1 0.1 multiply_reduce_fusion
  12.2 0.0 copy-start.1
  12.2 0.0 collective-permute-done.2.refs_4_
  12.2 1.5 collective-permute-start
  13.8 0.0 collective-permute-done.3.refs_5_
  13.8 1.5 collective-permute-start.1
  15.3 0.0 collective-permute-done.4.refs_6_
  15.3 0.0 collective-permute-done.6.refs_7_
  15.3 29.2 %shard_map.104 = (f32[16,1536]{1,0:T(8,128)S(1)}, f32[16,1536]{1,0:T(8,128)S(1)}, f32[16,1536]{1,0:T(8,128)S(1)}, f32[16,1536]{1,0:T(8,128)S(1)}, f32[16,1536]{1,0:T(8,128)S(1)}, /*index=5*/f32[16,128]{1,0:T(8,128)S(1)}) custom-call(s32[3,38,3]{2,1,0:T(8,128)S(1)} %copy-done.2, s32[2]{0:T(128)S(1)} %pad_add_fusion.2.refs_1_, ...), custom_call_target="tpu_custom_call" | custom-call | flops 30400000000 | bytes 2000000 | tf_op jit(solution)/shard_map/pallas_call | solution.py:217
  44.5 0.0 collective-permute-done.5.refs_7_
  44.5 0.0 copy-start
  44.5 29.2 %shard_map.105 = (f32[16,1536]{1,0:T(8,128)S(1)}, f32[16,1536]{1,0:T(8,128)S(1)}, f32[16,1536]{1,0:T(8,128)S(1)}, f32[16,1536]{1,0:T(8,128)S(1)}, f32[16,1536]{1,0:T(8,128)S(1)}, /*index=5*/f32[16,128]{1,0:T(8,128)S(1)}) custom-call(s32[3,38,3]{2,1,0:T(8,128)S(1)} %copy-done.1, s32[2]{0:T(128)S(1)} %pad_add_fusion.2.refs_1_, ...), custom_call_target="tpu_custom_call" | custom-call | flops 30400000000 | bytes 2000000 | tf_op jit(solution)/shard_map/pallas_call | solution.py:217
  73.7 0.0 collective-permute-done.refs_7_.refs_4_
  73.8 0.0 collective-permute-done.1.refs_8_.refs_5_
  73.8 0.0 copy-start.3
  73.8 42.1 %shard_map.106 = (f32[16,1536]{1,0:T(8,128)S(1)}, f32[16,1536]{1,0:T(8,128)S(1)}, f32[16,1536]{1,0:T(8,128)S(1)}, f32[16,1536]{1,0:T(8,128)S(1)}, f32[16,1536]{1...) custom-call(s32[3,56,3]{2,1,0:T(8,128)S(1)} %copy-done, s32[2]{0:T(128)S(1)} %pad_add_fusion.1.refs_1_, ...), custom_call_target="tpu_custom_call" | custom-call | flops 44800000000 | bytes 2000000 | tf_op jit(solution)/shard_map/pallas_call | solution.py:217
  115.9 14.6 %shard_map.107 = (f32[16,1536]{1,0:T(8,128)S(1)}, f32[16,1536]{1,0:T(8,128)S(1)}, f32[16,1536]{1,0:T(8,128)S(1)}, f32[16,128]{1,0:T(8,128)S(1)}) custom-call(s32[3,18,3]{2,1,0:T(8,128)S(1)} %copy-done.3, s32[2]{0:T(128)S(1)} %pad_add_fusion.refs_1_, f32[3]{0:T(128)S(1)} %broadcast_divide_fusion.refs_2_, f32[19,1536]{1,0:T(8,128)S(1)} %pad_maximum_fusion.refs_3_, ...), custom_call_target="tpu_custom_call" | custom-call | flops 14400000000 | bytes 2000000 | tf_op jit(solution)/shard_map/pallas_call | solution.py:217
  130.6 0.1 collective-permute-start.16
  130.7 0.1 reduce_sum.37
  130.8 0.1 collective-permute-start.7
  130.9 6.2 %collective-permute-start.17 = (f32[16,1536]{1,0:T(8,128)S(1)}, f32[16,1536]{1,0:T(8,128)S(1)}, u32[]{:S(2)}, u32[]{:S(2)}) collective-permute-start(f32[16,1536]{1,0:T(8,128)S(1)} %add.94), channel_id=1, source_target_pairs={{0,70},{1,15},{2,16},{3,25},{4,34},{5,43},{6,52},{7,61},{8,78},{9,... | collective-permute-start | bytes 294920 | tf_op jit(solution)/shard_map/ppermute | solution.py:291
  137.1 0.0 collective-permute-done.7
  137.1 4.3 %collective-permute-start.10 = (f32[2,16]{1,0:T(2,128)S(1)}, f32[2,16]{1,0:T(2,128)S(1)}, u32[]{:S(2)}, u32[]{:S(2)}) collective-permute-start(f32[2,16]{1,0:T(2,128)S(1)} %fusion.4), channel_id=1, source_target_pairs={{0,12},{2,14},{4,8},{6,10},{8,4},{10,6},{12,0},{14,2},{16,28},{18,... | collective-permute-start | bytes 392 | tf_op jit(solution)/shard_map/ppermute | solution.py:242
  141.4 0.0 collective-permute-start.13
  141.4 0.0 collective-permute-start.8
  141.4 1.5 collective-permute-done.10
  142.9 0.7 collective-permute-start.9
  143.6 1.4 collective-permute-done.8
  145.0 2.0 %collective-permute-start.14 = (f32[16,1536]{1,0:T(8,128)S(1)}, f32[16,1536]{1,0:T(8,128)S(1)}, u32[]{:S(2)}, u32[]{:S(2)}) collective-permute-start(f32[16,1536]{1,0:T(8,128)S(1)} %get-tuple-element.44), channel_id=1, source_target_pairs={{0,4},{1,5},{2,6},{3,7},{4,0},{5,1},{6,2},{7,3},{8,12},{9,13},{10,... | collective-permute-start | bytes 294920 | tf_op jit(solution)/shard_map/ppermute | solution.py:287
  147.0 1.0 collective-permute-done.9
  148.0 0.0 collective-permute-start.15
  148.0 0.0 collective-permute-done.16
  148.0 0.0 collective-permute-start.12
  148.0 0.0 collective-permute-done.17
  148.1 3.6 %collective-permute-start.11 = (f32[16,1536]{1,0:T(8,128)S(1)}, f32[16,1536]{1,0:T(8,128)S(1)}, u32[]{:S(2)}, u32[]{:S(2)}) collective-permute-start(f32[16,1536]{1,0:T(8,128)S(1)} %get-tuple-element.41), channel_id=1, source_target_pairs={{0,64},{1,9},{2,18},{3,27},{4,36},{5,45},{6,54},{7,63},{8,72},{9,1... | collective-permute-start | bytes 294920 | tf_op jit(solution)/shard_map/ppermute | solution.py:290
  151.7 0.0 collective-permute-done.13
  151.7 0.0 collective-permute-done.15
  151.7 3.7 %collective-permute-done.12 = f32[16,1536]{1,0:T(8,128)S(1)} collective-permute-done((f32[16,1536]{1,0:T(8,128)S(1)}, f32[16,1536]{1,0:T(8,128)S(1)}, u32[]{:S(2)}, u32[]{:S(2)}) %collective-permute-start.12) | collective-permute-done | bytes 98336 | tf_op jit(solution)/shard_map/ppermute | solution.py:290
  155.5 2.0 %collective-permute-start.18 = (f32[2,16]{1,0:T(2,128)S(1)}, f32[2,16]{1,0:T(2,128)S(1)}, u32[]{:S(2)}, u32[]{:S(2)}) collective-permute-start(f32[2,16]{1,0:T(2,128)S(1)} %add_add_fusion.3), channel_id=1, source_target_pairs={{0,16},{2,18},{4,20},{6,22},{8,24},{10,26},{12,28},{14,30},{16,0},... | collective-permute-start | bytes 392 | tf_op jit(solution)/shard_map/ppermute | solution.py:242
  157.5 3.1 %collective-permute-start.19 = (f32[2,16]{1,0:T(2,128)S(1)}, f32[2,16]{1,0:T(2,128)S(1)}, u32[]{:S(2)}, u32[]{:S(2)}) collective-permute-start(f32[2,16]{1,0:T(2,128)S(1)} %add_add_fusion.3), channel_id=1, source_target_pairs={{0,32},{2,34},{4,36},{6,38},{8,40},{10,42},{12,44},{14,46},{16,48}... | collective-permute-start | bytes 392 | tf_op jit(solution)/shard_map/ppermute | solution.py:242
  160.6 6.4 %collective-permute-start.24 = (f32[16,1536]{1,0:T(8,128)S(1)}, f32[16,1536]{1,0:T(8,128)S(1)}, u32[]{:S(2)}, u32[]{:S(2)}) collective-permute-start(f32[16,1536]{1,0:T(8,128)S(1)} %add_add_fusion), channel_id=1, source_target_pairs={{0,1},{1,0},{2,3},{3,2},{4,5},{5,4},{6,7},{7,6},{8,9},{9,8},{10,11... | collective-permute-start | bytes 294920 | tf_op jit(solution)/shard_map/ppermute | solution.py:306
  166.9 0.0 collective-permute-done.19
  166.9 0.0 collective-permute-done.20
  167.0 1.5 collective-permute-start.21
  168.5 1.0 collective-permute-start.22
  169.5 2.3 %collective-permute-start.23 = (f32[2,16]{1,0:T(2,128)S(1)}, f32[2,16]{1,0:T(2,128)S(1)}, u32[]{:S(2)}, u32[]{:S(2)}) collective-permute-start(f32[2,16]{1,0:T(2,128)S(1)} %add_add_fusion.2), channel_id=1, source_target_pairs={{0,65},{1,64},{2,67},{3,66},{4,69},{5,68},{6,71},{7,70},{8,73},{9,... | collective-permute-start | bytes 392 | tf_op jit(solution)/shard_map/ppermute | solution.py:242
  171.7 0.0 collective-permute-done.21
  171.7 1.8 %collective-permute-done.22 = f32[2,16]{1,0:T(2,128)S(1)} collective-permute-done((f32[2,16]{1,0:T(2,128)S(1)}, f32[2,16]{1,0:T(2,128)S(1)}, u32[]{:S(2)}, u32[]{:S(2)}) %collective-permute-start.22) | collective-permute-done | bytes 160 | tf_op jit(solution)/shard_map/ppermute | solution.py:242
  173.6 0.7 collective-permute-done.23
  174.3 0.0 collective-permute-done.24
  174.3 0.8 fusion.2
  (25 shorter events, 0.2 us)
Async XLA Ops:
  0.6 11.4 %copy-start.4 = (f32[16,1536]{1,0:T(8,128)S(1)}, f32[16,1536]{1,0:T(8,128)}, u32[]{:S(2)}) copy-start(f32[16,1536]{1,0:T(8,128)} %param.10) | copy-start | bytes 294916
  1.6 10.6 %collective-permute-start.2 = (f32[19,1536]{1,0:T(8,128)S(1)}, f32[19,1536]{1,0:T(8,128)S(1)}, u32[]{:S(2)}, u32[]{:S(2)}) collective-permute-start(f32[19,1536]{1,0:T(8,128)S(1)} %pad_maximum_fusion.refs_3_), channel_id=1, source_target_pairs={{2,0},{3,1},{4,2},{5,3},{6,4},{7,5},{0,6},{1,7},{10,8},{11,9},{12,... | collective-permute-start | bytes 350216 | tf_op jit(solution)/shard_map/ppermute | solution.py:261
  2.7 11.1 %collective-permute-start.3 = (f32[19,1536]{1,0:T(8,128)S(1)}, f32[19,1536]{1,0:T(8,128)S(1)}, u32[]{:S(2)}, u32[]{:S(2)}) collective-permute-start(f32[19,1536]{1,0:T(8,128)S(1)} %pad_maximum_fusion.refs_3_), channel_id=1, source_target_pairs={{4,0},{5,1},{6,2},{7,3},{0,4},{1,5},{2,6},{3,7},{12,8},{13,9},{14,... | collective-permute-start | bytes 350216 | tf_op jit(solution)/shard_map/ppermute | solution.py:261
  3.4 12.0 %collective-permute-start.4 = (f32[19,1536]{1,0:T(8,128)S(1)}, f32[19,1536]{1,0:T(8,128)S(1)}, u32[]{:S(2)}, u32[]{:S(2)}) collective-permute-start(f32[19,1536]{1,0:T(8,128)S(1)} %pad_maximum_fusion.refs_3_), channel_id=1, source_target_pairs={{6,0},{7,1},{0,2},{1,3},{2,4},{3,5},{4,6},{5,7},{14,8},{15,9},{8,1... | collective-permute-start | bytes 350216 | tf_op jit(solution)/shard_map/ppermute | solution.py:261
  3.5 11.8 %collective-permute-start.6 = (f32[19,1536]{1,0:T(8,128)S(1)}, f32[19,1536]{1,0:T(8,128)S(1)}, u32[]{:S(2)}, u32[]{:S(2)}) collective-permute-start(f32[19,1536]{1,0:T(8,128)S(1)} %pad_maximum_fusion.refs_3_), channel_id=1, source_target_pairs={{64,0},{9,1},{18,2},{27,3},{36,4},{45,5},{54,6},{63,7},{72,8},{17,... | collective-permute-start | bytes 350216 | tf_op jit(solution)/shard_map/ppermute | solution.py:260
  6.7 37.8 %collective-permute-start.5 = (f32[19,1536]{1,0:T(8,128)S(1)}, f32[19,1536]{1,0:T(8,128)S(1)}, u32[]{:S(2)}, u32[]{:S(2)}) collective-permute-start(f32[19,1536]{1,0:T(8,128)S(1)} %pad_maximum_fusion.refs_3_), channel_id=1, source_target_pairs={{66,0},{11,1},{20,2},{29,3},{38,4},{47,5},{48,6},{57,7},{74,8},{19... | collective-permute-start | bytes 350216 | tf_op jit(solution)/shard_map/ppermute | solution.py:260
  10.5 0.7 copy-start.7
  11.2 0.7 copy-start.5
  11.3 0.7 copy-start.6
  12.0 3.4 %copy-start.2 = (s32[3,38,3]{2,1,0:T(8,128)S(1)}, s32[3,38,3]{2,1,0:T(8,128)}, u32[]{:S(2)}) copy-start(s32[3,38,3]{2,1,0:T(8,128)} %constant.53.clone.refs_0_) | copy-start | bytes 4108
  12.2 32.3 %copy-start.1 = (s32[3,38,3]{2,1,0:T(8,128)S(1)}, s32[3,38,3]{2,1,0:T(8,128)}, u32[]{:S(2)}) copy-start(s32[3,38,3]{2,1,0:T(8,128)} %constant.54.clone.refs_0_) | copy-start | bytes 4108
  12.2 61.5 %collective-permute-start = (f32[19,1536]{1,0:T(8,128)S(1)}, f32[19,1536]{1,0:T(8,128)S(1)}, u32[]{:S(2)}, u32[]{:S(2)}) collective-permute-start(f32[19,1536]{1,0:T(8,128)S(1)} %pad_maximum_fusion.refs_3_), channel_id=1, source_target_pairs={{68,0},{13,1},{22,2},{31,3},{32,4},{41,5},{50,6},{59,7},{76,8},{21... | collective-permute-start | bytes 350216 | tf_op jit(solution)/shard_map/ppermute | solution.py:260
  13.8 60.0 %collective-permute-start.1 = (f32[19,1536]{1,0:T(8,128)S(1)}, f32[19,1536]{1,0:T(8,128)S(1)}, u32[]{:S(2)}, u32[]{:S(2)}) collective-permute-start(f32[19,1536]{1,0:T(8,128)S(1)} %pad_maximum_fusion.refs_3_), channel_id=1, source_target_pairs={{70,0},{15,1},{16,2},{25,3},{34,4},{43,5},{52,6},{61,7},{78,8},{23... | collective-permute-start | bytes 350216 | tf_op jit(solution)/shard_map/ppermute | solution.py:260
  44.5 29.2 %copy-start = (s32[3,56,3]{2,1,0:T(8,128)S(1)}, s32[3,56,3]{2,1,0:T(8,128)}, u32[]{:S(2)}) copy-start(s32[3,56,3]{2,1,0:T(8,128)} %constant.55.clone.refs_0_) | copy-start | bytes 6052
  73.8 42.2 %copy-start.3 = (s32[3,18,3]{2,1,0:T(8,128)S(1)}, s32[3,18,3]{2,1,0:T(8,128)}, u32[]{:S(2)}) copy-start(s32[3,18,3]{2,1,0:T(8,128)} %constant.56.clone.refs_0_) | copy-start | bytes 1948
  130.6 17.4 %collective-permute-start.16 = (f32[16,1536]{1,0:T(8,128)S(1)}, f32[16,1536]{1,0:T(8,128)S(1)}, u32[]{:S(2)}, u32[]{:S(2)}) collective-permute-start(f32[16,1536]{1,0:T(8,128)S(1)} %add.92), channel_id=1, source_target_pairs={{0,68},{1,13},{2,22},{3,31},{4,32},{5,41},{6,50},{7,59},{8,76},{9,... | collective-permute-start | bytes 294920 | tf_op jit(solution)/shard_map/ppermute | solution.py:291
  130.8 6.3 %collective-permute-start.7 = (f32[2,16]{1,0:T(2,128)S(1)}, f32[2,16]{1,0:T(2,128)S(1)}, u32[]{:S(2)}, u32[]{:S(2)}) collective-permute-start(f32[2,16]{1,0:T(2,128)S(1)} %pad_maximum_fusion.1), channel_id=1, source_target_pairs={{0,2},{2,0},{4,6},{6,4},{8,10},{10,8},{12,14},{14,12},{16,18},{18,... | collective-permute-start | bytes 392 | tf_op jit(solution)/shard_map/ppermute | solution.py:242
  130.9 17.1 %collective-permute-start.17 = (f32[16,1536]{1,0:T(8,128)S(1)}, f32[16,1536]{1,0:T(8,128)S(1)}, u32[]{:S(2)}, u32[]{:S(2)}) collective-permute-start(f32[16,1536]{1,0:T(8,128)S(1)} %add.94), channel_id=1, source_target_pairs={{0,70},{1,15},{2,16},{3,25},{4,34},{5,43},{6,52},{7,61},{8,78},{9,... | collective-permute-start | bytes 294920 | tf_op jit(solution)/shard_map/ppermute | solution.py:291
  137.1 5.8 %collective-permute-start.10 = (f32[2,16]{1,0:T(2,128)S(1)}, f32[2,16]{1,0:T(2,128)S(1)}, u32[]{:S(2)}, u32[]{:S(2)}) collective-permute-start(f32[2,16]{1,0:T(2,128)S(1)} %fusion.4), channel_id=1, source_target_pairs={{0,12},{2,14},{4,8},{6,10},{8,4},{10,6},{12,0},{14,2},{16,28},{18,... | collective-permute-start | bytes 392 | tf_op jit(solution)/shard_map/ppermute | solution.py:242
  141.4 10.3 %collective-permute-start.13 = (f32[16,1536]{1,0:T(8,128)S(1)}, f32[16,1536]{1,0:T(8,128)S(1)}, u32[]{:S(2)}, u32[]{:S(2)}) collective-permute-start(f32[16,1536]{1,0:T(8,128)S(1)} %get-tuple-element.43), channel_id=1, source_target_pairs={{0,2},{1,3},{2,4},{3,5},{4,6},{5,7},{6,0},{7,1},{8,10},{9,11},{10,... | collective-permute-start | bytes 294920 | tf_op jit(solution)/shard_map/ppermute | solution.py:287
  141.4 3.6 %collective-permute-start.8 = (f32[2,16]{1,0:T(2,128)S(1)}, f32[2,16]{1,0:T(2,128)S(1)}, u32[]{:S(2)}, u32[]{:S(2)}) collective-permute-start(f32[2,16]{1,0:T(2,128)S(1)} %fusion.4), channel_id=1, source_target_pairs={{0,4},{2,6},{4,0},{6,2},{8,12},{10,14},{12,8},{14,10},{16,20},{18,... | collective-permute-start | bytes 392 | tf_op jit(solution)/shard_map/ppermute | solution.py:242
  142.9 5.1 %collective-permute-start.9 = (f32[2,16]{1,0:T(2,128)S(1)}, f32[2,16]{1,0:T(2,128)S(1)}, u32[]{:S(2)}, u32[]{:S(2)}) collective-permute-start(f32[2,16]{1,0:T(2,128)S(1)} %fusion.4), channel_id=1, source_target_pairs={{0,8},{2,10},{4,12},{6,14},{8,0},{10,2},{12,4},{14,6},{16,24},{18,... | collective-permute-start | bytes 392 | tf_op jit(solution)/shard_map/ppermute | solution.py:242
  145.0 6.7 %collective-permute-start.14 = (f32[16,1536]{1,0:T(8,128)S(1)}, f32[16,1536]{1,0:T(8,128)S(1)}, u32[]{:S(2)}, u32[]{:S(2)}) collective-permute-start(f32[16,1536]{1,0:T(8,128)S(1)} %get-tuple-element.44), channel_id=1, source_target_pairs={{0,4},{1,5},{2,6},{3,7},{4,0},{5,1},{6,2},{7,3},{8,12},{9,13},{10,... | collective-permute-start | bytes 294920 | tf_op jit(solution)/shard_map/ppermute | solution.py:287
  148.0 3.7 %collective-permute-start.15 = (f32[16,1536]{1,0:T(8,128)S(1)}, f32[16,1536]{1,0:T(8,128)S(1)}, u32[]{:S(2)}, u32[]{:S(2)}) collective-permute-start(f32[16,1536]{1,0:T(8,128)S(1)} %get-tuple-element.45), channel_id=1, source_target_pairs={{0,6},{1,7},{2,0},{3,1},{4,2},{5,3},{6,4},{7,5},{8,14},{9,15},{10,... | collective-permute-start | bytes 294920 | tf_op jit(solution)/shard_map/ppermute | solution.py:287
  148.0 7.4 %collective-permute-start.12 = (f32[16,1536]{1,0:T(8,128)S(1)}, f32[16,1536]{1,0:T(8,128)S(1)}, u32[]{:S(2)}, u32[]{:S(2)}) collective-permute-start(f32[16,1536]{1,0:T(8,128)S(1)} %get-tuple-element.42), channel_id=1, source_target_pairs={{0,66},{1,11},{2,20},{3,29},{4,38},{5,47},{6,48},{7,57},{8,74},{9,... | collective-permute-start | bytes 294920 | tf_op jit(solution)/shard_map/ppermute | solution.py:290
  148.1 7.4 %collective-permute-start.11 = (f32[16,1536]{1,0:T(8,128)S(1)}, f32[16,1536]{1,0:T(8,128)S(1)}, u32[]{:S(2)}, u32[]{:S(2)}) collective-permute-start(f32[16,1536]{1,0:T(8,128)S(1)} %get-tuple-element.41), channel_id=1, source_target_pairs={{0,64},{1,9},{2,18},{3,27},{4,36},{5,45},{6,54},{7,63},{8,72},{9,1... | collective-permute-start | bytes 294920 | tf_op jit(solution)/shard_map/ppermute | solution.py:290
  155.5 11.4 %collective-permute-start.18 = (f32[2,16]{1,0:T(2,128)S(1)}, f32[2,16]{1,0:T(2,128)S(1)}, u32[]{:S(2)}, u32[]{:S(2)}) collective-permute-start(f32[2,16]{1,0:T(2,128)S(1)} %add_add_fusion.3), channel_id=1, source_target_pairs={{0,16},{2,18},{4,20},{6,22},{8,24},{10,26},{12,28},{14,30},{16,0},... | collective-permute-start | bytes 392 | tf_op jit(solution)/shard_map/ppermute | solution.py:242
  157.5 9.5 %collective-permute-start.19 = (f32[2,16]{1,0:T(2,128)S(1)}, f32[2,16]{1,0:T(2,128)S(1)}, u32[]{:S(2)}, u32[]{:S(2)}) collective-permute-start(f32[2,16]{1,0:T(2,128)S(1)} %add_add_fusion.3), channel_id=1, source_target_pairs={{0,32},{2,34},{4,36},{6,38},{8,40},{10,42},{12,44},{14,46},{16,48}... | collective-permute-start | bytes 392 | tf_op jit(solution)/shard_map/ppermute | solution.py:242
  160.6 6.4 %collective-permute-start.20 = (f32[2,16]{1,0:T(2,128)S(1)}, f32[2,16]{1,0:T(2,128)S(1)}, u32[]{:S(2)}, u32[]{:S(2)}) collective-permute-start(f32[2,16]{1,0:T(2,128)S(1)} %add_add_fusion.3), channel_id=1, source_target_pairs={{0,48},{2,50},{4,52},{6,54},{8,56},{10,58},{12,60},{14,62},{16,32}... | collective-permute-start | bytes 392 | tf_op jit(solution)/shard_map/ppermute | solution.py:242
  160.6 13.7 %collective-permute-start.24 = (f32[16,1536]{1,0:T(8,128)S(1)}, f32[16,1536]{1,0:T(8,128)S(1)}, u32[]{:S(2)}, u32[]{:S(2)}) collective-permute-start(f32[16,1536]{1,0:T(8,128)S(1)} %add_add_fusion), channel_id=1, source_target_pairs={{0,1},{1,0},{2,3},{3,2},{4,5},{5,4},{6,7},{7,6},{8,9},{9,8},{10,11... | collective-permute-start | bytes 294920 | tf_op jit(solution)/shard_map/ppermute | solution.py:306
  167.0 4.8 %collective-permute-start.21 = (f32[2,16]{1,0:T(2,128)S(1)}, f32[2,16]{1,0:T(2,128)S(1)}, u32[]{:S(2)}, u32[]{:S(2)}) collective-permute-start(f32[2,16]{1,0:T(2,128)S(1)} %add_add_fusion.2), channel_id=1, source_target_pairs={{0,1},{1,0},{2,3},{3,2},{4,5},{5,4},{6,7},{7,6},{8,9},{9,8},{10,11... | collective-permute-start | bytes 392 | tf_op jit(solution)/shard_map/ppermute | solution.py:242
  168.5 5.1 %collective-permute-start.22 = (f32[2,16]{1,0:T(2,128)S(1)}, f32[2,16]{1,0:T(2,128)S(1)}, u32[]{:S(2)}, u32[]{:S(2)}) collective-permute-start(f32[2,16]{1,0:T(2,128)S(1)} %add_add_fusion.2), channel_id=1, source_target_pairs={{0,64},{1,65},{2,66},{3,67},{4,68},{5,69},{6,70},{7,71},{8,72},{9,... | collective-permute-start | bytes 392 | tf_op jit(solution)/shard_map/ppermute | solution.py:242
  169.5 4.8 %collective-permute-start.23 = (f32[2,16]{1,0:T(2,128)S(1)}, f32[2,16]{1,0:T(2,128)S(1)}, u32[]{:S(2)}, u32[]{:S(2)}) collective-permute-start(f32[2,16]{1,0:T(2,128)S(1)} %add_add_fusion.2), channel_id=1, source_target_pairs={{0,65},{1,64},{2,67},{3,66},{4,69},{5,68},{6,71},{7,70},{8,73},{9,... | collective-permute-start | bytes 392 | tf_op jit(solution)/shard_map/ppermute | solution.py:242

commit v3 on v2

--- a/solution.py
+++ b/solution.py
@@ -34,14 +34,14 @@
     for a in range(NSUPER):
         for d in range(8):
             source = (a + (d if d else 8)) % NSUPER
-            member = ((d // 2 + chunk) % CHUNKS) * 2 + d % 2
+            member = ((d // 2) ^ chunk) * 2 + d % 2
             route.append((device_at(source, member), device_at(a, d)))
     return route
 
 
 def row_route(chunk):
     return [
-        (device_at(a, ((d // 2 + chunk) % CHUNKS) * 2 + d % 2), device_at(a, d))
+        (device_at(a, ((d // 2) ^ chunk) * 2 + d % 2), device_at(a, d))
         for a in range(NSUPER)
         for d in range(8)
     ]
@@ -51,20 +51,24 @@
     return [(b, a) for a, b in route]
 
 
-CALLS = [((0, 1, 2, 3), (0,)), ((0, 1, 2, 3), (1,)), ((1, 2, 3), (2, 3)), ((0,), (2, 3))]
+CALLS = [
+    ((0, 1), (0,), [(0, 0), (1, 0)]),
+    ((0, 1, 2, 3), (0, 1), [(2, 0), (3, 0), (0, 1), (1, 1), (2, 1), (3, 1)]),
+    ((0, 1, 2, 3), (2, 3), [(i, j) for i in (1, 2, 3) for j in (2, 3)]),
+    ((0,), (2, 3), [(0, 2), (0, 3)]),
+]
 OFF = [(1, 0), (2, 1), (3, 1), (0, 2), (0, 3), (2, 3)]
 ON = [[(0, 0), (1, 1)], [(2, 2), (3, 3)]]
-FILL = [[20, 11, 47, 0], [29, 20, 29, 0]]
+FILL = [[0, 31, 47, 0], [9, 40, 29, 0]]
 
 
 def tile_tables():
     per = SHARD // TILE
     side = SUPER // TILE
-    triangle = [(i, j) for i in range(side) for j in range(i, side)]
+    triangle = [(i, j) for j in range(side) for i in range(j + 1)]
     used = [0, 0]
     tables, counts = [], []
-    for call, (rows, columns) in enumerate(CALLS):
-        held = (0, 1, 2, 3) if len(rows) > 1 else rows
+    for call, (held, columns, pairs) in enumerate(CALLS):
 
         def pair(i, j):
             first = (len(held) + columns.index(j)) * per
@@ -72,17 +76,17 @@
                 (held.index(i) * per + y, first + x, 1) for y in range(per) for x in range(per)
             ]
 
-        lists = [[t for i in rows for j in columns for t in pair(i, j)]]
+        lists = [[t for i, j in pairs for t in pair(i, j)]]
         for half in range(2):
-            chunks = [(i, j) for i, j in OFF + ON[half] if i in rows and j in columns]
-            tiles = [t for i, j in chunks for t in pair(i, j)]
+            tiles = [t for i, j in OFF + ON[half] if (i, j) in pairs for t in pair(i, j)]
             part = triangle[used[half] : used[half] + FILL[half][call]]
+            assert not part or max(j for _, j in part) < len(held) * per
             used[half] += len(part)
             tiles += [(i, j, int(i != j)) for i, j in part]
             lists.append(tiles)
         longest = max(len(x) for x in lists)
         counts.append([len(x) for x in lists])
-        assert all(len(x) % 2 == 0 for x in lists)
+        assert all(len(x) % 2 == 0 for x in lists) and counts[-1][1] == counts[-1][2]
         tables.append(
             np.array(
                 [
@@ -111,14 +115,14 @@
     return (shifted * shifted + OFFSET) * jnp.exp2(shifted)
 
 
-def tile_kernel(x_count, y_count, chained, *refs):
+def tile_kernel(x_count, every, begun, *refs):
     refs = list(refs)
     table, meta, scale = refs[:3]
-    chunks = refs[3 : 3 + x_count + y_count]
-    rest = refs[3 + x_count + y_count :]
-    if chained:
-        sums_in, curve_in, rest = rest[:x_count], rest[x_count], rest[x_count + 1 :]
-    sums_out, rest = rest[: x_count + y_count], rest[x_count + y_count :]
+    chunks, rest = refs[3 : 3 + every], refs[3 + every :]
+    sums_in, rest = dict(zip(begun, rest)), rest[len(begun) :]
+    if begun:
+        curve_in, rest = rest[0], rest[1:]
+    sums_out, rest = rest[:every], rest[every:]
     curve_out, row_feat, col_feat, vectors, row_sum, col_sum, hi0, hi1, lo0, lo1 = rest
 
     for place, chunk in enumerate(chunks):
@@ -190,7 +194,7 @@
     lax.fori_loop(0, count // 2, two_tiles, 0)
     both(None, None, None, place_of(count - 1), hi1, lo1)
 
-    curve = curve_in[...] if chained else jnp.zeros((NVEC, 128), f32)
+    curve = curve_in[...] if begun else jnp.zeros((NVEC, 128), f32)
     for place, chunk in enumerate(chunks):
         span = slice(place * SHARD, (place + 1) * SHARD)
         total = col_sum[:, span]
@@ -200,7 +204,7 @@
         product = total * chunk[3:19, :]
         for lane in range(0, SHARD, 128):
             curve = curve + product[:, lane : lane + 128]
-        if chained and place < x_count:
+        if place in sums_in:
             total = total + sums_in[place][...]
         sums_out[place][...] = total
     curve_out[...] = curve
@@ -212,10 +216,12 @@
     count = len(rows) + len(columns)
     wide = len(rows) * SHARD
     every = count * SHARD
-    chained = curve is not None
-    passed = [*rows, *columns, *sums, curve] if chained else [*rows, *columns]
+    begun = tuple(i for i, part in enumerate(sums) if part is not None)
+    passed = [*rows, *columns, *(sums[i] for i in begun)]
+    if begun:
+        passed.append(curve)
     out = pl.pallas_call(
-        functools.partial(tile_kernel, len(rows), len(columns), chained),
+        functools.partial(tile_kernel, len(rows), count, begun),
         out_shape=[jax.ShapeDtypeStruct((NVEC, SHARD), f32)] * count
         + [jax.ShapeDtypeStruct((NVEC, 128), f32)],
         in_specs=[smem] * 3 + [vmem] * len(passed),
@@ -233,7 +239,7 @@
             flops=800_000_000 * table.shape[1], bytes_accessed=2_000_000, transcendentals=0
         ),
     )(table, meta, scale, *passed)
-    return out[: len(rows)], out[len(rows) : count], out[count]
+    return out[:count], out[count]
 
 
 def summed_over_devices(value, own):
@@ -255,10 +261,19 @@
     return value, own
 
 
+def after(value, *others):
+    return lax.optimization_barrier((value, *others))[0]
+
+
 def on_device(points, targets, length_scales, noise_levels, noise_class):
     shard = jnp.concatenate([points, targets], axis=0)
-    columns = [lax.ppermute(shard, BOTH, column_route(c)) for c in range(CHUNKS)]
-    rows = [shard] + [lax.ppermute(shard, BOTH, row_route(c)) for c in range(1, CHUNKS)]
+    rows, columns = {0: shard}, {}
+    columns[0] = lax.ppermute(shard, BOTH, column_route(0))
+    rows[1] = lax.ppermute(shard, BOTH, row_route(1))
+    then = after(shard, columns[0], rows[1])
+    rows[2] = lax.ppermute(then, BOTH, row_route(2))
+    rows[3] = lax.ppermute(then, BOTH, row_route(3))
+    columns[1] = lax.ppermute(then, BOTH, column_route(1))
 
     block = lax.axis_index("blk")
     first = (block % CHUNKS == 0) & (lax.axis_index("grp") == 0)
@@ -266,29 +281,31 @@
     tables, counts = tile_tables()
     scale = (math.sqrt(5.0) * LOG2E) / length_scales
 
-    sums, curve = None, None
-    column_sums = {}
+    sums, curve = {}, None
     returned = []
-    for call, (row_chunks, column_chunks) in enumerate(CALLS):
+    for call, (held, across, _) in enumerate(CALLS):
         count = jnp.where(variant == 0, counts[call][0], counts[call][1]).astype(jnp.int32)
         meta = jnp.stack([variant, count])
-        held = rows if len(row_chunks) > 1 else [rows[c] for c in row_chunks]
-        before = sums if len(row_chunks) > 1 else [sums[c] for c in row_chunks]
-        after, column_part, curve = run_tiles(
-            jnp.asarray(tables[call]), meta, scale, held, [columns[c] for c in column_chunks],
-            before, curve,
+        names = [("x", c) for c in held] + [("y", c) for c in across]
+        if call == 3:
+            curve = after(curve, *returned[:2])
+        parts, curve = run_tiles(
+            jnp.asarray(tables[call]), meta, scale, [rows[c] for c in held],
+            [columns[c] for c in across], [sums.get(name) for name in names], curve,
         )
-        if len(row_chunks) > 1:
-            sums = after
-        for c, part in zip(column_chunks, column_part):
-            column_sums[c] = column_sums[c] + part if c in column_sums else part
+        sums.update(zip(names, parts))
+        if call == 0:
+            then = after(shard, curve)
+            for c in (2, 3):
+                columns[c] = lax.ppermute(then, BOTH, column_route(c))
+        if call == 1:
+            for c in (0, 1):
+                returned.append(lax.ppermute(sums["y", c], BOTH, backward(column_route(c))))
         if call == 2:
-            for c in range(1, CHUNKS):
-                returned.append(lax.ppermute(sums[c], BOTH, backward(row_route(c))))
-        if call < 2:
-            c = column_chunks[0]
-            returned.append(lax.ppermute(column_sums[c], BOTH, backward(column_route(c))))
-    last = [lax.ppermute(column_sums[c], BOTH, backward(column_route(c))) for c in (2, 3)]
+            for c in (1, 2, 3):
+                returned.append(lax.ppermute(sums["x", c], BOTH, backward(row_route(c))))
+    for c in (2, 3):
+        returned.append(lax.ppermute(sums["y", c], BOTH, backward(column_route(c))))
 
     classes = lax.broadcasted_iota(jnp.int32, (noise_levels.shape[0], noise_class.shape[0]), 0)
     noise_diag = jnp.sum(
@@ -297,11 +314,12 @@
     own_noise = noise_diag[None, :] * targets
     norm = 0.5 * jnp.sum(targets * targets, axis=1)
     curvature = jnp.sum(curve, axis=1) + 0.5 * jnp.sum(targets * own_noise, axis=1)
-
-    own = after[0]
-    for part in returned + last:
+    scalars = after(jnp.stack([norm, curvature]), *returned[2:5])
+
+    own = sums["x", 0]
+    for part in returned:
         own = own + part
-    scalars, own = summed_over_devices(jnp.stack([norm, curvature]), own)
+    scalars, own = summed_over_devices(scalars, own)
     step_size = scalars[0] / scalars[1]
     image = own + lax.ppermute(own, "grp", [(0, 1), (1, 0)]) + own_noise
     return (step_size[:, None] * targets, targets - step_size[:, None] * image)

time: 178 us -> 178 us (level); the launches traced: 175 us -> 178 us
  starting transfers between devices: 45.1 us -> 48.3 us
    ppermute x14, starting transfers between devices: 23.9 us -> 27.2 us  [the longest x4 8.29 us: on_device(): returned.append(lax.ppermute(sums['y', c], BOTH, backward(column_route(c))))]
    ppermute x14, waiting for transfers between devices: 3.78 us -> 1.59 us  [the longest x1 1.56 us: on_device(): columns[0] = lax.ppermute(shard, BOTH, column_route(0))]
    ppermute x10, waiting for transfers between devices: 6.43 us -> 8.31 us  [along(): parts = [lax.ppermute(value, axis, route) for route in routes]]
  transfers between devices with their start and end apart: 25 -> 25, of which waited for: 6 -> 5; matrix products, arithmetic and copies ran while one was open for 0% -> 0% of each run, Pallas kernels for 33% -> 65%
where the time goes in v3:
time: 178 us
  Pallas kernels  115 us (65%)
  starting transfers between devices  48.3 us (27%)
  waiting for transfers between devices  9.9 us (6%)
  other arithmetic  2.4 us (1%)
    pallas_call x4, Pallas kernels, run_tiles(): pl.pallas_call(functools.partial(tile_kernel, len(rows), count, begun), o...  115 us
    ppermute x10, starting transfers between devices, along(): parts = [lax.ppermute(value, axis, route) for route in routes]  16.4 us
    ppermute x10, waiting for transfers between devices, along(): parts = [lax.ppermute(value, axis, route) for route in routes]  8.31 us
    ppermute x4, starting transfers between devices, on_device(): returned.append(lax.ppermute(sums['y', c], BOTH, backward(column_route(c))))  8.29 us
    ppermute x1, starting transfers between devices, on_device(): columns[1] = lax.ppermute(then, BOTH, column_route(1))  6.28 us
    ppermute x1, starting transfers between devices, on_device(): image = own + lax.ppermute(own, 'grp', [(0, 1), (1, 0)]) + own_noise  4.71 us
    ppermute x1, starting transfers between devices, on_device(): rows[2] = lax.ppermute(then, BOTH, row_route(2))  4.11 us
  transfers between devices with their start and end apart: 25, of which 5 were waited for; matrix products, arithmetic and copies ran while one was open for 0% of the time, Pallas kernels for 65%

profile of v3, /device:TPU:0, one launch (start us, length us, event | category | flops | bytes accessed | tf_op | source)
XLA Modules:
  0.0 177.8 jit_solution(3444137371376715331)
XLA Ops:
  0.6 1.0 pad_maximum_fusion.refs_3_
  1.6 0.1 collective-permute-start
  1.7 3.3 %collective-permute-start.1 = (f32[19,1536]{1,0:T(8,128)S(1)}, f32[19,1536]{1,0:T(8,128)S(1)}, u32[]{:S(2)}, u32[]{:S(2)}) collective-permute-start(f32[19,1536]{1,0:T(8,128)S(1)} %pad_maximum_fusion.refs_3_), channel_id=1, source_target_pairs={{64,0},{9,1},{18,2},{27,3},{36,4},{45,5},{54,6},{63,7},{72,8},{17,... | collective-permute-start | bytes 350216 | tf_op jit(solution)/shard_map/ppermute | solution.py:271
  5.1 0.7 copy-done.7
  5.7 0.1 copy-done.5
  5.8 0.6 copy-done.6
  6.4 0.1 select_reduce_fusion
  6.5 0.0 copy-start.3
  6.5 0.1 multiply_reduce_fusion
  6.6 0.1 pad_add_fusion.refs_1_
  6.7 0.1 pad_add_fusion.2.refs_1_
  6.8 0.1 pad_add_fusion.1.refs_1_
  6.9 0.0 collective-permute-done.refs_4_
  6.9 1.6 collective-permute-done.1.refs_5_.refs_7_
  8.4 4.1 %collective-permute-start.4 = (f32[19,1536]{1,0:T(8,128)S(1)}, f32[19,1536]{1,0:T(8,128)S(1)}, u32[]{:S(2)}, u32[]{:S(2)}) collective-permute-start(f32[19,1536]{1,0:T(8,128)S(1)} %pad_maximum_fusion.refs_3_), channel_id=1, source_target_pairs={{4,0},{5,1},{6,2},{7,3},{0,4},{1,5},{2,6},{3,7},{12,8},{13,9},{14,... | collective-permute-start | bytes 350216 | tf_op jit(solution)/shard_map/ppermute | solution.py:274
  12.5 0.0 collective-permute-start.5
  12.5 6.3 %collective-permute-start.6 = (f32[19,1536]{1,0:T(8,128)S(1)}, f32[19,1536]{1,0:T(8,128)S(1)}, u32[]{:S(2)}, u32[]{:S(2)}) collective-permute-start(f32[19,1536]{1,0:T(8,128)S(1)} %pad_maximum_fusion.refs_3_), channel_id=1, source_target_pairs={{66,0},{11,1},{16,2},{25,3},{38,4},{47,5},{52,6},{61,7},{74,8},{19... | collective-permute-start | bytes 350216 | tf_op jit(solution)/shard_map/ppermute | solution.py:276
  18.8 14.7 %shard_map.104 = (f32[16,1536]{1,0:T(8,128)S(1)}, f32[16,1536]{1,0:T(8,128)S(1)}, f32[16,1536]{1,0:T(8,128)S(1)}, f32[16,128]{1,0:T(8,128)S(1)}) custom-call(s32[3,18,3]{2,1,0:T(8,128)S(1)} %copy-done.3, s32[2]{0:T(128)S(1)} %pad_add_fusion.refs_1_, f32[3]{0:T(128)S(1)} %broadcast_divide_fusion.refs_2_, f32[19,1536]{1,0:T(8,128)S(1)} %pad_maximum_fusion.refs_3_, ...), custom_call_target="tpu_custom_call" | custom-call | flops 14400000000 | bytes 2000000 | tf_op jit(solution)/shard_map/pallas_call | solution.py:223
  33.5 2.7 %collective-permute-start.2 = (f32[19,1536]{1,0:T(8,128)S(1)}, f32[19,1536]{1,0:T(8,128)S(1)}, u32[]{:S(2)}, u32[]{:S(2)}) collective-permute-start(f32[19,1536]{1,0:T(8,128)S(1)} %pad_maximum_fusion.refs_3_), channel_id=1, source_target_pairs={{68,0},{13,1},{22,2},{31,3},{32,4},{41,5},{50,6},{59,7},{76,8},{21... | collective-permute-start | bytes 350216 | tf_op jit(solution)/shard_map/ppermute | solution.py:300
  36.3 0.0 collective-permute-start.3
  36.3 0.0 collective-permute-done.4.refs_5_
  36.3 0.0 collective-permute-done.5.refs_6_
  36.3 0.0 collective-permute-done.6.refs_8_
  36.3 0.0 copy-start.1
  36.3 43.6 %shard_map.105 = (f32[16,1536]{1,0:T(8,128)S(1)}, f32[16,1536]{1,0:T(8,128)S(1)}, f32[16,1536]{1,0:T(8,128)S(1)}, f32[16,1536]{1,0:T(8,128)S(1)}, f32[16,1536]{1...) custom-call(s32[3,58,3]{2,1,0:T(8,128)S(1)} %copy-done, s32[2]{0:T(128)S(1)} %pad_add_fusion.2.refs_1_, ...), custom_call_target="tpu_custom_call" | custom-call | flops 46400000000 | bytes 2000000 | tf_op jit(solution)/shard_map/pallas_call | solution.py:223
  79.9 3.3 %collective-permute-start.7 = (f32[16,1536]{1,0:T(8,128)S(1)}, f32[16,1536]{1,0:T(8,128)S(1)}, u32[]{:S(2)}, u32[]{:S(2)}) collective-permute-start(f32[16,1536]{1,0:T(8,128)S(1)} %get-tuple-element.45), channel_id=1, source_target_pairs={{0,64},{1,9},{2,18},{3,27},{4,36},{5,45},{6,54},{7,63},{8,72},{9,1... | collective-permute-start | bytes 294920 | tf_op jit(solution)/shard_map/ppermute | solution.py:303
  83.2 0.0 collective-permute-start.8
  83.2 0.0 collective-permute-done.2.refs_7_.refs_4_
  83.2 0.0 collective-permute-done.3.refs_8_.refs_5_
  83.2 0.0 copy-start.2
  83.2 42.0 %shard_map.106 = (f32[16,1536]{1,0:T(8,128)S(1)}, f32[16,1536]{1,0:T(8,128)S(1)}, f32[16,1536]{1,0:T(8,128)S(1)}, f32[16,1536]{1,0:T(8,128)S(1)}, f32[16,1536]{1...) custom-call(s32[3,56,3]{2,1,0:T(8,128)S(1)} %copy-done.1, s32[2]{0:T(128)S(1)} %pad_add_fusion.1.refs_1_, ...), custom_call_target="tpu_custom_call" | custom-call | flops 44800000000 | bytes 2000000 | tf_op jit(solution)/shard_map/pallas_call | solution.py:223
  125.2 0.3 collective-permute-start.10
  125.5 0.1 collective-permute-start.11
  125.6 2.0 %collective-permute-start.9 = (f32[16,1536]{1,0:T(8,128)S(1)}, f32[16,1536]{1,0:T(8,128)S(1)}, u32[]{:S(2)}, u32[]{:S(2)}) collective-permute-start(f32[16,1536]{1,0:T(8,128)S(1)} %get-tuple-element.49), channel_id=1, source_target_pairs={{0,2},{1,3},{2,0},{3,1},{4,6},{5,7},{6,4},{7,5},{8,10},{9,11},{10,... | collective-permute-start | bytes 294920 | tf_op jit(solution)/shard_map/ppermute | solution.py:306
  127.6 0.0 collective-permute-done.7
  127.6 0.0 collective-permute-done.8
  127.6 14.6 %shard_map.107 = (f32[16,1536]{1,0:T(8,128)S(1)}, f32[16,1536]{1,0:T(8,128)S(1)}, f32[16,1536]{1,0:T(8,128)S(1)}, f32[16,128]{1,0:T(8,128)S(1)}) custom-call(s32[3,18,3]{2,1,0:T(8,128)S(1)} %copy-done.2, s32[2]{0:T(128)S(1)} %pad_add_fusion.refs_1_, f32[3]{0:T(128)S(1)} %broadcast_divide_fusion.refs_2_, f32[19,1536]{1,0:T(8,128)S(1)} %pad_maximum_fusion.refs_3_, ...), custom_call_target="tpu_custom_call" | custom-call | flops 14400000000 | bytes 2000000 | tf_op jit(solution)/shard_map/pallas_call | solution.py:223
  142.3 0.1 collective-permute-start.16
  142.4 0.1 reduce_sum.37
  142.5 0.0 collective-permute-done.10
  142.5 0.0 collective-permute-done.11
  142.5 0.0 collective-permute-done.9
  142.5 0.1 collective-permute-start.12
  142.6 4.9 %collective-permute-start.17 = (f32[16,1536]{1,0:T(8,128)S(1)}, f32[16,1536]{1,0:T(8,128)S(1)}, u32[]{:S(2)}, u32[]{:S(2)}) collective-permute-start(f32[16,1536]{1,0:T(8,128)S(1)} %get-tuple-element.55), channel_id=1, source_target_pairs={{0,70},{1,15},{2,20},{3,29},{4,34},{5,43},{6,48},{7,57},{8,78},{9,... | collective-permute-start | bytes 294920 | tf_op jit(solution)/shard_map/ppermute | solution.py:308
  147.6 0.0 collective-permute-done.12
  147.6 0.7 collective-permute-start.13
  148.3 2.7 %collective-permute-start.14 = (f32[2,16]{1,0:T(2,128)S(1)}, f32[2,16]{1,0:T(2,128)S(1)}, u32[]{:S(2)}, u32[]{:S(2)}) collective-permute-start(f32[2,16]{1,0:T(2,128)S(1)} %add.77), channel_id=1, source_target_pairs={{0,8},{2,10},{4,12},{6,14},{8,0},{10,2},{12,4},{14,6},{16,24},{18,... | collective-permute-start | bytes 392 | tf_op jit(solution)/shard_map/ppermute | solution.py:248
  151.0 1.3 collective-permute-start.15
  152.3 0.0 collective-permute-done.13
  152.3 1.1 collective-permute-done.14
  153.4 2.4 %collective-permute-done.15 = f32[2,16]{1,0:T(2,128)S(1)} collective-permute-done((f32[2,16]{1,0:T(2,128)S(1)}, f32[2,16]{1,0:T(2,128)S(1)}, u32[]{:S(2)}, u32[]{:S(2)}) %collective-permute-start.15) | collective-permute-done | bytes 160 | tf_op jit(solution)/shard_map/ppermute | solution.py:248
  155.8 0.0 collective-permute-done.16
  155.8 0.0 collective-permute-done.17
  155.8 0.1 add_add_fusion
  155.9 0.8 collective-permute-start.18
  156.7 1.3 collective-permute-start.19
  158.0 2.7 %collective-permute-start.20 = (f32[2,16]{1,0:T(2,128)S(1)}, f32[2,16]{1,0:T(2,128)S(1)}, u32[]{:S(2)}, u32[]{:S(2)}) collective-permute-start(f32[2,16]{1,0:T(2,128)S(1)} %add_add_fusion.3), channel_id=1, source_target_pairs={{0,48},{2,50},{4,52},{6,54},{8,56},{10,58},{12,60},{14,62},{16,32}... | collective-permute-start | bytes 392 | tf_op jit(solution)/shard_map/ppermute | solution.py:248
  160.6 4.7 %collective-permute-start.24 = (f32[16,1536]{1,0:T(8,128)S(1)}, f32[16,1536]{1,0:T(8,128)S(1)}, u32[]{:S(2)}, u32[]{:S(2)}) collective-permute-start(f32[16,1536]{1,0:T(8,128)S(1)} %add_add_fusion), channel_id=1, source_target_pairs={{0,1},{1,0},{2,3},{3,2},{4,5},{5,4},{6,7},{7,6},{8,9},{9,8},{10,11... | collective-permute-start | bytes 294920 | tf_op jit(solution)/shard_map/ppermute | solution.py:324
  165.4 4.0 %collective-permute-start.21 = (f32[2,16]{1,0:T(2,128)S(1)}, f32[2,16]{1,0:T(2,128)S(1)}, u32[]{:S(2)}, u32[]{:S(2)}) collective-permute-start(f32[2,16]{1,0:T(2,128)S(1)} %add_add_fusion.2), channel_id=1, source_target_pairs={{0,1},{1,0},{2,3},{3,2},{4,5},{5,4},{6,7},{7,6},{8,9},{9,8},{10,11... | collective-permute-start | bytes 392 | tf_op jit(solution)/shard_map/ppermute | solution.py:248
  169.4 2.8 %collective-permute-start.22 = (f32[2,16]{1,0:T(2,128)S(1)}, f32[2,16]{1,0:T(2,128)S(1)}, u32[]{:S(2)}, u32[]{:S(2)}) collective-permute-start(f32[2,16]{1,0:T(2,128)S(1)} %add_add_fusion.2), channel_id=1, source_target_pairs={{0,64},{1,65},{2,66},{3,67},{4,68},{5,69},{6,70},{7,71},{8,72},{9,... | collective-permute-start | bytes 392 | tf_op jit(solution)/shard_map/ppermute | solution.py:248
  172.2 2.3 %collective-permute-done.22 = f32[2,16]{1,0:T(2,128)S(1)} collective-permute-done((f32[2,16]{1,0:T(2,128)S(1)}, f32[2,16]{1,0:T(2,128)S(1)}, u32[]{:S(2)}, u32[]{:S(2)}) %collective-permute-start.22) | collective-permute-done | bytes 160 | tf_op jit(solution)/shard_map/ppermute | solution.py:248
  174.5 2.5 %collective-permute-done.23 = f32[2,16]{1,0:T(2,128)S(1)} collective-permute-done((f32[2,16]{1,0:T(2,128)S(1)}, f32[2,16]{1,0:T(2,128)S(1)}, u32[]{:S(2)}, u32[]{:S(2)}) %collective-permute-start.23) | collective-permute-done | bytes 160 | tf_op jit(solution)/shard_map/ppermute | solution.py:248
  177.0 0.0 collective-permute-done.24
  177.0 0.8 fusion.2
  (24 shorter events, 0.1 us)
Async XLA Ops:
  0.6 5.8 %copy-start.4 = (f32[16,1536]{1,0:T(8,128)S(1)}, f32[16,1536]{1,0:T(8,128)}, u32[]{:S(2)}) copy-start(f32[16,1536]{1,0:T(8,128)} %param.10) | copy-start | bytes 294916
  1.6 5.2 %collective-permute-start = (f32[19,1536]{1,0:T(8,128)S(1)}, f32[19,1536]{1,0:T(8,128)S(1)}, u32[]{:S(2)}, u32[]{:S(2)}) collective-permute-start(f32[19,1536]{1,0:T(8,128)S(1)} %pad_maximum_fusion.refs_3_), channel_id=1, source_target_pairs={{2,0},{3,1},{0,2},{1,3},{6,4},{7,5},{4,6},{5,7},{10,8},{11,9},{8,1... | collective-permute-start | bytes 350216 | tf_op jit(solution)/shard_map/ppermute | solution.py:272
  1.7 6.7 %collective-permute-start.1 = (f32[19,1536]{1,0:T(8,128)S(1)}, f32[19,1536]{1,0:T(8,128)S(1)}, u32[]{:S(2)}, u32[]{:S(2)}) collective-permute-start(f32[19,1536]{1,0:T(8,128)S(1)} %pad_maximum_fusion.refs_3_), channel_id=1, source_target_pairs={{64,0},{9,1},{18,2},{27,3},{36,4},{45,5},{54,6},{63,7},{72,8},{17,... | collective-permute-start | bytes 350216 | tf_op jit(solution)/shard_map/ppermute | solution.py:271
  5.1 0.7 copy-start.7
  5.1 0.7 copy-start.5
  5.7 0.7 copy-start.6
  6.5 12.4 %copy-start.3 = (s32[3,18,3]{2,1,0:T(8,128)S(1)}, s32[3,18,3]{2,1,0:T(8,128)}, u32[]{:S(2)}) copy-start(s32[3,18,3]{2,1,0:T(8,128)} %constant.51.clone.refs_0_) | copy-start | bytes 1948
  6.9 29.4 %copy-start = (s32[3,58,3]{2,1,0:T(8,128)S(1)}, s32[3,58,3]{2,1,0:T(8,128)}, u32[]{:S(2)}) copy-start(s32[3,58,3]{2,1,0:T(8,128)} %constant.52.clone.refs_0_) | copy-start | bytes 6268
  8.4 27.8 %collective-permute-start.4 = (f32[19,1536]{1,0:T(8,128)S(1)}, f32[19,1536]{1,0:T(8,128)S(1)}, u32[]{:S(2)}, u32[]{:S(2)}) collective-permute-start(f32[19,1536]{1,0:T(8,128)S(1)} %pad_maximum_fusion.refs_3_), channel_id=1, source_target_pairs={{4,0},{5,1},{6,2},{7,3},{0,4},{1,5},{2,6},{3,7},{12,8},{13,9},{14,... | collective-permute-start | bytes 350216 | tf_op jit(solution)/shard_map/ppermute | solution.py:274
  12.5 23.7 %collective-permute-start.5 = (f32[19,1536]{1,0:T(8,128)S(1)}, f32[19,1536]{1,0:T(8,128)S(1)}, u32[]{:S(2)}, u32[]{:S(2)}) collective-permute-start(f32[19,1536]{1,0:T(8,128)S(1)} %pad_maximum_fusion.refs_3_), channel_id=1, source_target_pairs={{6,0},{7,1},{4,2},{5,3},{2,4},{3,5},{0,6},{1,7},{14,8},{15,9},{12,... | collective-permute-start | bytes 350216 | tf_op jit(solution)/shard_map/ppermute | solution.py:275
  12.5 23.7 %collective-permute-start.6 = (f32[19,1536]{1,0:T(8,128)S(1)}, f32[19,1536]{1,0:T(8,128)S(1)}, u32[]{:S(2)}, u32[]{:S(2)}) collective-permute-start(f32[19,1536]{1,0:T(8,128)S(1)} %pad_maximum_fusion.refs_3_), channel_id=1, source_target_pairs={{66,0},{11,1},{16,2},{25,3},{38,4},{47,5},{52,6},{61,7},{74,8},{19... | collective-permute-start | bytes 350216 | tf_op jit(solution)/shard_map/ppermute | solution.py:276
  33.5 49.7 %collective-permute-start.2 = (f32[19,1536]{1,0:T(8,128)S(1)}, f32[19,1536]{1,0:T(8,128)S(1)}, u32[]{:S(2)}, u32[]{:S(2)}) collective-permute-start(f32[19,1536]{1,0:T(8,128)S(1)} %pad_maximum_fusion.refs_3_), channel_id=1, source_target_pairs={{68,0},{13,1},{22,2},{31,3},{32,4},{41,5},{50,6},{59,7},{76,8},{21... | collective-permute-start | bytes 350216 | tf_op jit(solution)/shard_map/ppermute | solution.py:300
  36.3 46.9 %collective-permute-start.3 = (f32[19,1536]{1,0:T(8,128)S(1)}, f32[19,1536]{1,0:T(8,128)S(1)}, u32[]{:S(2)}, u32[]{:S(2)}) collective-permute-start(f32[19,1536]{1,0:T(8,128)S(1)} %pad_maximum_fusion.refs_3_), channel_id=1, source_target_pairs={{70,0},{15,1},{20,2},{29,3},{34,4},{43,5},{48,6},{57,7},{78,8},{23... | collective-permute-start | bytes 350216 | tf_op jit(solution)/shard_map/ppermute | solution.py:300
  36.3 46.9 %copy-start.1 = (s32[3,56,3]{2,1,0:T(8,128)S(1)}, s32[3,56,3]{2,1,0:T(8,128)}, u32[]{:S(2)}) copy-start(s32[3,56,3]{2,1,0:T(8,128)} %constant.53.clone.refs_0_) | copy-start | bytes 6052
  79.9 47.7 %collective-permute-start.7 = (f32[16,1536]{1,0:T(8,128)S(1)}, f32[16,1536]{1,0:T(8,128)S(1)}, u32[]{:S(2)}, u32[]{:S(2)}) collective-permute-start(f32[16,1536]{1,0:T(8,128)S(1)} %get-tuple-element.45), channel_id=1, source_target_pairs={{0,64},{1,9},{2,18},{3,27},{4,36},{5,45},{6,54},{7,63},{8,72},{9,1... | collective-permute-start | bytes 294920 | tf_op jit(solution)/shard_map/ppermute | solution.py:303
  83.2 44.5 %collective-permute-start.8 = (f32[16,1536]{1,0:T(8,128)S(1)}, f32[16,1536]{1,0:T(8,128)S(1)}, u32[]{:S(2)}, u32[]{:S(2)}) collective-permute-start(f32[16,1536]{1,0:T(8,128)S(1)} %get-tuple-element.46), channel_id=1, source_target_pairs={{0,66},{1,11},{2,16},{3,25},{4,38},{5,47},{6,52},{7,61},{8,74},{9,... | collective-permute-start | bytes 294920 | tf_op jit(solution)/shard_map/ppermute | solution.py:303
  83.2 44.4 %copy-start.2 = (s32[3,18,3]{2,1,0:T(8,128)S(1)}, s32[3,18,3]{2,1,0:T(8,128)}, u32[]{:S(2)}) copy-start(s32[3,18,3]{2,1,0:T(8,128)} %constant.54.clone.refs_0_) | copy-start | bytes 1948
  125.2 17.3 %collective-permute-start.10 = (f32[16,1536]{1,0:T(8,128)S(1)}, f32[16,1536]{1,0:T(8,128)S(1)}, u32[]{:S(2)}, u32[]{:S(2)}) collective-permute-start(f32[16,1536]{1,0:T(8,128)S(1)} %get-tuple-element.50), channel_id=1, source_target_pairs={{0,4},{1,5},{2,6},{3,7},{4,0},{5,1},{6,2},{7,3},{8,12},{9,13},{10,... | collective-permute-start | bytes 294920 | tf_op jit(solution)/shard_map/ppermute | solution.py:306
  125.5 17.0 %collective-permute-start.11 = (f32[16,1536]{1,0:T(8,128)S(1)}, f32[16,1536]{1,0:T(8,128)S(1)}, u32[]{:S(2)}, u32[]{:S(2)}) collective-permute-start(f32[16,1536]{1,0:T(8,128)S(1)} %get-tuple-element.51), channel_id=1, source_target_pairs={{0,6},{1,7},{2,4},{3,5},{4,2},{5,3},{6,0},{7,1},{8,14},{9,15},{10,... | collective-permute-start | bytes 294920 | tf_op jit(solution)/shard_map/ppermute | solution.py:306
  125.6 16.9 %collective-permute-start.9 = (f32[16,1536]{1,0:T(8,128)S(1)}, f32[16,1536]{1,0:T(8,128)S(1)}, u32[]{:S(2)}, u32[]{:S(2)}) collective-permute-start(f32[16,1536]{1,0:T(8,128)S(1)} %get-tuple-element.49), channel_id=1, source_target_pairs={{0,2},{1,3},{2,0},{3,1},{4,6},{5,7},{6,4},{7,5},{8,10},{9,11},{10,... | collective-permute-start | bytes 294920 | tf_op jit(solution)/shard_map/ppermute | solution.py:306
  142.3 13.5 %collective-permute-start.16 = (f32[16,1536]{1,0:T(8,128)S(1)}, f32[16,1536]{1,0:T(8,128)S(1)}, u32[]{:S(2)}, u32[]{:S(2)}) collective-permute-start(f32[16,1536]{1,0:T(8,128)S(1)} %get-tuple-element.54), channel_id=1, source_target_pairs={{0,68},{1,13},{2,22},{3,31},{4,32},{5,41},{6,50},{7,59},{8,76},{9,... | collective-permute-start | bytes 294920 | tf_op jit(solution)/shard_map/ppermute | solution.py:308
  142.5 5.0 %collective-permute-start.12 = (f32[2,16]{1,0:T(2,128)S(1)}, f32[2,16]{1,0:T(2,128)S(1)}, u32[]{:S(2)}, u32[]{:S(2)}) collective-permute-start(f32[2,16]{1,0:T(2,128)S(1)} %pad_maximum_fusion.1), channel_id=1, source_target_pairs={{0,2},{2,0},{4,6},{6,4},{8,10},{10,8},{12,14},{14,12},{16,18},{18,... | collective-permute-start | bytes 392 | tf_op jit(solution)/shard_map/ppermute | solution.py:248
  142.6 13.2 %collective-permute-start.17 = (f32[16,1536]{1,0:T(8,128)S(1)}, f32[16,1536]{1,0:T(8,128)S(1)}, u32[]{:S(2)}, u32[]{:S(2)}) collective-permute-start(f32[16,1536]{1,0:T(8,128)S(1)} %get-tuple-element.55), channel_id=1, source_target_pairs={{0,70},{1,15},{2,20},{3,29},{4,34},{5,43},{6,48},{7,57},{8,78},{9,... | collective-permute-start | bytes 294920 | tf_op jit(solution)/shard_map/ppermute | solution.py:308
  147.6 4.7 %collective-permute-start.13 = (f32[2,16]{1,0:T(2,128)S(1)}, f32[2,16]{1,0:T(2,128)S(1)}, u32[]{:S(2)}, u32[]{:S(2)}) collective-permute-start(f32[2,16]{1,0:T(2,128)S(1)} %add.77), channel_id=1, source_target_pairs={{0,4},{2,6},{4,0},{6,2},{8,12},{10,14},{12,8},{14,10},{16,20},{18,... | collective-permute-start | bytes 392 | tf_op jit(solution)/shard_map/ppermute | solution.py:248
  148.3 5.1 %collective-permute-start.14 = (f32[2,16]{1,0:T(2,128)S(1)}, f32[2,16]{1,0:T(2,128)S(1)}, u32[]{:S(2)}, u32[]{:S(2)}) collective-permute-start(f32[2,16]{1,0:T(2,128)S(1)} %add.77), channel_id=1, source_target_pairs={{0,8},{2,10},{4,12},{6,14},{8,0},{10,2},{12,4},{14,6},{16,24},{18,... | collective-permute-start | bytes 392 | tf_op jit(solution)/shard_map/ppermute | solution.py:248
  151.0 4.8 %collective-permute-start.15 = (f32[2,16]{1,0:T(2,128)S(1)}, f32[2,16]{1,0:T(2,128)S(1)}, u32[]{:S(2)}, u32[]{:S(2)}) collective-permute-start(f32[2,16]{1,0:T(2,128)S(1)} %add.77), channel_id=1, source_target_pairs={{0,12},{2,14},{4,8},{6,10},{8,4},{10,6},{12,0},{14,2},{16,28},{18,... | collective-permute-start | bytes 392 | tf_op jit(solution)/shard_map/ppermute | solution.py:248
  155.9 9.5 %collective-permute-start.18 = (f32[2,16]{1,0:T(2,128)S(1)}, f32[2,16]{1,0:T(2,128)S(1)}, u32[]{:S(2)}, u32[]{:S(2)}) collective-permute-start(f32[2,16]{1,0:T(2,128)S(1)} %add_add_fusion.3), channel_id=1, source_target_pairs={{0,16},{2,18},{4,20},{6,22},{8,24},{10,26},{12,28},{14,30},{16,0},... | collective-permute-start | bytes 392 | tf_op jit(solution)/shard_map/ppermute | solution.py:248
  156.7 8.7 %collective-permute-start.19 = (f32[2,16]{1,0:T(2,128)S(1)}, f32[2,16]{1,0:T(2,128)S(1)}, u32[]{:S(2)}, u32[]{:S(2)}) collective-permute-start(f32[2,16]{1,0:T(2,128)S(1)} %add_add_fusion.3), channel_id=1, source_target_pairs={{0,32},{2,34},{4,36},{6,38},{8,40},{10,42},{12,44},{14,46},{16,48}... | collective-permute-start | bytes 392 | tf_op jit(solution)/shard_map/ppermute | solution.py:248
  158.0 7.4 %collective-permute-start.20 = (f32[2,16]{1,0:T(2,128)S(1)}, f32[2,16]{1,0:T(2,128)S(1)}, u32[]{:S(2)}, u32[]{:S(2)}) collective-permute-start(f32[2,16]{1,0:T(2,128)S(1)} %add_add_fusion.3), channel_id=1, source_target_pairs={{0,48},{2,50},{4,52},{6,54},{8,56},{10,58},{12,60},{14,62},{16,32}... | collective-permute-start | bytes 392 | tf_op jit(solution)/shard_map/ppermute | solution.py:248
  160.6 16.3 %collective-permute-start.24 = (f32[16,1536]{1,0:T(8,128)S(1)}, f32[16,1536]{1,0:T(8,128)S(1)}, u32[]{:S(2)}, u32[]{:S(2)}) collective-permute-start(f32[16,1536]{1,0:T(8,128)S(1)} %add_add_fusion), channel_id=1, source_target_pairs={{0,1},{1,0},{2,3},{3,2},{4,5},{5,4},{6,7},{7,6},{8,9},{9,8},{10,11... | collective-permute-start | bytes 294920 | tf_op jit(solution)/shard_map/ppermute | solution.py:324
  165.4 6.8 %collective-permute-start.21 = (f32[2,16]{1,0:T(2,128)S(1)}, f32[2,16]{1,0:T(2,128)S(1)}, u32[]{:S(2)}, u32[]{:S(2)}) collective-permute-start(f32[2,16]{1,0:T(2,128)S(1)} %add_add_fusion.2), channel_id=1, source_target_pairs={{0,1},{1,0},{2,3},{3,2},{4,5},{5,4},{6,7},{7,6},{8,9},{9,8},{10,11... | collective-permute-start | bytes 392 | tf_op jit(solution)/shard_map/ppermute | solution.py:248
  169.4 5.1 %collective-permute-start.22 = (f32[2,16]{1,0:T(2,128)S(1)}, f32[2,16]{1,0:T(2,128)S(1)}, u32[]{:S(2)}, u32[]{:S(2)}) collective-permute-start(f32[2,16]{1,0:T(2,128)S(1)} %add_add_fusion.2), channel_id=1, source_target_pairs={{0,64},{1,65},{2,66},{3,67},{4,68},{5,69},{6,70},{7,71},{8,72},{9,... | collective-permute-start | bytes 392 | tf_op jit(solution)/shard_map/ppermute | solution.py:248
  172.2 4.8 %collective-permute-start.23 = (f32[2,16]{1,0:T(2,128)S(1)}, f32[2,16]{1,0:T(2,128)S(1)}, u32[]{:S(2)}, u32[]{:S(2)}) collective-permute-start(f32[2,16]{1,0:T(2,128)S(1)} %add_add_fusion.2), channel_id=1, source_target_pairs={{0,65},{1,64},{2,67},{3,66},{4,69},{5,68},{6,71},{7,70},{8,73},{9,... | collective-permute-start | bytes 392 | tf_op jit(solution)/shard_map/ppermute | solution.py:248

commit v4 on v3

v4 whole, which is shorter than its diff:
```python
import functools
import math

import jax
import jax.numpy as jnp
import numpy as np
from jax import lax
from jax.experimental import pallas as pl
from jax.experimental.pallas import tpu as pltpu
from jax.sharding import PartitionSpec as P

BOTH = ("blk", "grp")
SHARD = 1536
ROWS = 24
CHUNKS = 4
SUPER = SHARD * CHUNKS
NSUPER = 16
NVEC = 16
TILE = 768
SUB = 256
LOG2E = math.log2(math.e)
SHIFT = 1.5 * LOG2E
OFFSET = 0.75 * LOG2E * LOG2E
FACTOR = 2.0**SHIFT / (3.0 * LOG2E * LOG2E)
bf16 = jnp.bfloat16
f32 = jnp.float32
f8 = jnp.float8_e5m2


def device_at(block, member):
    return (CHUNKS * block + member // 2) * 2 + member % 2


def column_route(chunk):
    route = []
    for a in range(NSUPER):
        for d in range(8):
            source = (a + (d if d else 8)) % NSUPER
            member = ((d // 2) ^ chunk) * 2 + d % 2
            route.append((device_at(source, member), device_at(a, d)))
    return route


def row_route(chunk):
    return [
        (device_at(a, ((d // 2) ^ chunk) * 2 + d % 2), device_at(a, d))
        for a in range(NSUPER)
        for d in range(8)
    ]


def block_route():
    return [
        (device_at((a + (d if d else 8)) % NSUPER, d), device_at(a, d))
        for a in range(NSUPER)
        for d in range(8)
    ]


def backward(route):
    return [(b, a) for a, b in route]


CALLS = [
    ((0, 1), (0,), [(0, 0), (1, 0)]),
    ((2, 3), (0,), [(2, 0), (3, 0)]),
    ((0, 1, 2, 3), (1,), [(0, 1), (1, 1), (2, 1), (3, 1)]),
    ((0, 1, 2, 3), (2, 3), [(i, j) for i in (1, 2, 3) for j in (2, 3)]),
    ((0,), (2, 3), [(0, 2), (0, 3)]),
]
OFF = [(1, 0), (2, 1), (3, 1), (0, 2), (0, 3), (2, 3)]
ON = [[(0, 0), (1, 1)], [(2, 2), (3, 3)]]
FILL = [[0, 8, 4, 20, 0], [4, 8, 8, 12, 0]]
PER = SHARD // TILE
GIVEN = [(0, 3 * PER), (1, 3 * PER), (0, 3 * PER + 1), (1, 3 * PER + 1)]


def tile_tables():
    side = SUPER // TILE
    triangles = [
        [(i, j) for j in range(side) for i in range(j + 1) if (i, j) not in GIVEN] for _ in range(2)
    ]
    tables, counts = [], []
    for call, (held, columns, pairs) in enumerate(CALLS):

        def at(i, k=0):
            return held.index((i // PER) ^ k) * PER + i % PER

        def pair(i, j):
            first = (len(held) + columns.index(j)) * PER
            return [(at(i * PER + y), first + x, 1) for y in range(PER) for x in range(PER)]

        regular = [t for i, j in pairs for t in pair(i, j)]
        lists = [regular]
        for half in range(2):
            tiles = [t for i, j in OFF + ON[half] if (i, j) in pairs for t in pair(i, j)]
            fits = [t for t in triangles[half] if all(i // PER in held for i in t)]
            part = fits[: FILL[half][call]]
            assert len(part) == FILL[half][call]
            triangles[half] = [t for t in triangles[half] if t not in part]
            tiles += [(at(i), at(j), int(i != j)) for i, j in part]
            lists.append(tiles)
        given = GIVEN if call == 3 else []
        lists.append(regular + [(at(i), at(j), 1) for i, j in given[:2]])
        lists.append(regular + [(at(i, 1), at(j, 1), 1) for i, j in given[2:]])
        longest = max(len(x) for x in lists)
        counts.append(np.array([len(x) for x in lists], np.int32))
        assert all(len(x) % 2 == 0 for x in lists)
        tables.append(
            np.array(
                [
                    [(i * TILE, j * TILE, k) for i, j, k in x + x[:1] * (longest - len(x))]
                    for x in lists
                ],
                np.int32,
            )
        )
    assert triangles == [[], []]
    return tables, counts


def pieces(value, count, dtype=bf16):
    out = []
    for _ in range(count):
        piece = value.astype(dtype).astype(f32)
        out.append(piece)
        value = value - piece
    return out


def kernel_values(squared):
    squared = jnp.maximum(squared, 1e-12)
    shifted = -SHIFT - squared * lax.rsqrt(squared)
    return (shifted * shifted + OFFSET) * jnp.exp2(shifted)


def tile_kernel(x_count, places, begun, *refs):
    refs = list(refs)
    table, meta, scale = refs[:3]
    every = len(places)
    given = 1 + max(array for array, _ in places)
    chunks = [refs[3 + array].at[pl.ds(ROWS * i, ROWS)] for array, i in places]
    rest = refs[3 + given :]
    sums_in, rest = dict(zip(begun, rest)), rest[len(begun) :]
    if begun:
        curve_in, rest = rest[0], rest[1:]
    sums_out, rest = rest[:every], rest[every:]
    curve_out, row_feat, col_feat, vectors, vectors8, row_sum, col_sum, hi0, hi1, lo0, lo1 = rest

    largest = jnp.full((NVEC, 1), 1e-30, f32)
    for chunk in chunks:
        part = jnp.max(jnp.abs(chunk[3:19, :]), axis=1, keepdims=True)
        largest = jnp.maximum(largest, part)
    upward = 1024.0 / largest
    downward = largest * (FACTOR / 1024.0)

    for place, chunk in enumerate(chunks):
        span = slice(place * SHARD, (place + 1) * SHARD)
        scaled = jnp.concatenate(
            [(chunk[c : c + 1, :] - 4.0) * scale[c] for c in range(3)], axis=0
        )
        a1, a2, a3 = pieces(scaled, 3)
        norm = jnp.sum(scaled * scaled, axis=0, keepdims=True)
        n1, n2, n3 = pieces(norm, 3)
        one = jnp.ones_like(norm)
        pad = jnp.zeros((8, SHARD), f32)
        columns = jnp.concatenate(
            [-2.0 * a1, -2.0 * a2, -2.0 * a1, -2.0 * a3, -2.0 * a2, -2.0 * a1,
             one, one, one, n1, n2, n3, pad], axis=0)
        col_feat[:, span] = columns.astype(bf16)
        vec = chunk[3:19, :] * upward
        vectors[:, span] = jnp.concatenate(pieces(vec, 2), axis=0).astype(bf16)
        vectors8[:, span] = jnp.concatenate(pieces(vec, 2, f8), axis=0).astype(f8)
        if place < x_count:
            rows = jnp.concatenate(
                [a1, a1, a2, a1, a2, a3, n1, n2, n3, one, one, one, pad], axis=0
            )
            row_feat[span, :] = jnp.transpose(rows).astype(bf16)
    for ref in (row_sum, col_sum, hi1, lo1):
        ref[...] = jnp.zeros_like(ref)
    variant = meta[0]
    count = meta[1]

    def place_of(t):
        return (
            pl.multiple_of(table[variant, t, 0], TILE),
            pl.multiple_of(table[variant, t, 1], TILE),
            table[variant, t, 2],
        )

    def produce(place, hi, lo, x, y):
        row, col, _ = place
        right = col_feat[:, pl.ds(pl.multiple_of(col + x, SUB), SUB)]
        left = row_feat[pl.ds(pl.multiple_of(row + y, SUB), SUB), :]
        value = kernel_values(jnp.dot(left, right, preferred_element_type=f32))
        high = value.astype(bf16)
        hi[y : y + SUB, x : x + SUB] = high
        lo[y : y + SUB, x : x + SUB] = (value - high.astype(f32)).astype(f8)

    def consume_rows(place, hi, lo, y):
        row, col, _ = place
        across = (((1,), (1,)), ((), ()))
        far = pl.ds(col, TILE)
        high, low = hi[y : y + SUB, :], lo[y : y + SUB, :]
        part = lax.dot_general(vectors[:, far], high, across, preferred_element_type=f32)
        part = part + lax.dot_general(vectors8[:, far], low, across, preferred_element_type=f32)
        row_sum[:, pl.ds(pl.multiple_of(row + y, SUB), SUB)] += part

    def consume_columns(place, hi, lo, x):
        row, col, keep = place
        near = pl.ds(row, TILE)
        high, low = hi[:, x : x + SUB], lo[:, x : x + SUB]
        part = jnp.dot(vectors[:, near], high, preferred_element_type=f32)
        part = part + jnp.dot(vectors8[:, near], low, preferred_element_type=f32)
        col_sum[:, pl.ds(pl.multiple_of(col + x, SUB), SUB)] += part * keep.astype(f32)

    def both(ahead, ahead_hi, ahead_lo, now, hi, lo):
        subs = [(x, y) for x in range(0, TILE, SUB) for y in range(0, TILE, SUB)]
        work = [(consume_rows, y) for y in range(0, TILE, SUB)]
        work += [(consume_columns, x) for x in range(0, TILE, SUB)]
        done = 0
        for n, (x, y) in enumerate(subs):
            if ahead is not None:
                produce(ahead, ahead_hi, ahead_lo, x, y)
            while done * len(subs) < (n + 1) * len(work) and done < len(work):
                step, offset = work[done]
                step(now, hi, lo, offset)
                done += 1

    def two_tiles(u, carried):
        both(place_of(2 * u), hi0, lo0, place_of(jnp.maximum(2 * u - 1, 0)), hi1, lo1)
        both(place_of(2 * u + 1), hi1, lo1, place_of(2 * u), hi0, lo0)
        return carried

    lax.fori_loop(0, count // 2, two_tiles, 0)
    both(None, None, None, place_of(count - 1), hi1, lo1)

    curve = curve_in[...] if begun else jnp.zeros((NVEC, 128), f32)
    for place, chunk in enumerate(chunks):
        span = slice(place * SHARD, (place + 1) * SHARD)
        total = col_sum[:, span]
        if place < x_count:
            total = total + row_sum[:, span]
        total = downward * (total[:NVEC] + total[NVEC:])
        product = total * chunk[3:19, :]
        for lane in range(0, SHARD, 128):
            curve = curve + product[:, lane : lane + 128]
        if place in sums_in:
            total = total + sums_in[place][...]
        sums_out[place][...] = total
    curve_out[...] = curve


def run_tiles(table, meta, scale, rows, columns, sums, curve):
    vmem = pl.BlockSpec(memory_space=pltpu.VMEM)
    smem = pl.BlockSpec(memory_space=pltpu.SMEM)
    count = len(rows) + len(columns)
    wide = len(rows) * SHARD
    every = count * SHARD
    arrays, places = [], []
    for array, i in [*rows, *columns]:
        found = [n for n, other in enumerate(arrays) if other is array]
        if not found:
            arrays.append(array)
        places.append((found[0] if found else len(arrays) - 1, i))
    begun = tuple(i for i, part in enumerate(sums) if part is not None)
    passed = [*arrays, *(sums[i] for i in begun)]
    if begun:
        passed.append(curve)
    out = pl.pallas_call(
        functools.partial(tile_kernel, len(rows), places, begun),
        out_shape=[jax.ShapeDtypeStruct((NVEC, SHARD), f32)] * count
        + [jax.ShapeDtypeStruct((NVEC, 128), f32)],
        in_specs=[smem] * 3 + [vmem] * len(passed),
        out_specs=[vmem] * (count + 1),
        scratch_shapes=[
            pltpu.VMEM((wide, 32), bf16),
            pltpu.VMEM((32, every), bf16),
            pltpu.VMEM((32, every), bf16),
            pltpu.VMEM((32, every), f8),
            pltpu.VMEM((32, wide), f32),
            pltpu.VMEM((32, every), f32),
        ]
        + [pltpu.VMEM((TILE, TILE), bf16)] * 2
        + [pltpu.VMEM((TILE, TILE), f8)] * 2,
        compiler_params=pltpu.CompilerParams(vmem_limit_bytes=48 * 2**20),
        cost_estimate=pl.CostEstimate(
            flops=1_500_000_000 * table.shape[1], bytes_accessed=2_000_000, transcendentals=0
        ),
    )(table, meta, scale, *passed)
    return out[:count], out[count]


def after(value, *others):
    return lax.optimization_barrier((value, *others))[0]


def on_device(points, targets, length_scales, noise_levels, noise_class):
    shard = jnp.concatenate([points, targets, jnp.zeros((ROWS - 19, SHARD), f32)], axis=0)
    first_column = lax.ppermute(shard, BOTH, column_route(0))
    partner = lax.ppermute(shard, "blk", [(i, i ^ 1) for i in range(64)])
    chip = jnp.concatenate([shard, partner], axis=0)
    beside = lax.ppermute(chip, "blk", [(i, i ^ 2) for i in range(64)])
    rows = {0: (shard, 0), 1: (partner, 0), 2: (beside, 0), 3: (beside, 1)}
    columns = {0: (first_column, 0)}

    block = lax.axis_index("blk")
    member = (block % CHUNKS) * 2 + lax.axis_index("grp")
    variant = jnp.where(member == 0, jnp.where(block < 32, 1, 2), 0)
    variant = jnp.where(member == 1, 3, jnp.where(member == 2, 4, variant)).astype(jnp.int32)
    tables, counts = tile_tables()
    scale = (math.sqrt(5.0) * LOG2E) / length_scales

    sums, curve = {}, None
    returned = []
    for call, (held, across, _) in enumerate(CALLS):
        meta = jnp.stack([variant, jnp.asarray(counts[call])[variant]])
        names = [("x", c) for c in held] + [("y", c) for c in across]
        parts, curve = run_tiles(
            jnp.asarray(tables[call]), meta, scale, [rows[c] for c in held],
            [columns[c] for c in across], [sums.get(name) for name in names], curve,
        )
        sums.update(zip(names, parts))
        if call == 0:
            others = after(jnp.concatenate([partner, beside], axis=0), curve)
            others = lax.ppermute(others, BOTH, block_route())
            columns.update({c: (others, c - 1) for c in (1, 2, 3)})
        if call == 3:
            for c in (0, 1):
                part = after(sums["y", c], curve)
                returned.append(lax.ppermute(part, BOTH, backward(column_route(c))))
            for c in (1, 2, 3):
                returned.append(lax.ppermute(sums["x", c], BOTH, backward(row_route(c))))
    for c in (2, 3):
        returned.append(lax.ppermute(sums["y", c], BOTH, backward(column_route(c))))

    classes = lax.broadcasted_iota(jnp.int32, (noise_levels.shape[0], noise_class.shape[0]), 0)
    noise_diag = jnp.sum(
        jnp.where(noise_class[None, :] == classes, noise_levels[:, None], 0.0), axis=0
    )
    own_noise = noise_diag[None, :] * targets
    norm = 0.5 * jnp.sum(targets * targets, axis=1)
    curvature = jnp.sum(curve, axis=1) + 0.5 * jnp.sum(targets * own_noise, axis=1)
    scalars = after(jnp.concatenate([norm, curvature]), *returned[:5])
    blocks = lax.axis_size("blk")
    scalars = lax.all_to_all(
        jnp.broadcast_to(scalars[None], (blocks, 2 * NVEC)), "blk", 0, 0, tiled=True
    )
    scalars = jnp.sum(scalars, axis=0)

    scalars, *returned = lax.optimization_barrier((scalars, *returned))
    own = sums["x", 0]
    for part in returned:
        own = own + part
    theirs = lax.ppermute(own, "grp", [(0, 1), (1, 0)])
    scalars = scalars + lax.ppermute(scalars, "grp", [(0, 1), (1, 0)])
    step_size = scalars[:NVEC] / scalars[NVEC:]
    image = own + theirs + own_noise
    return (step_size[:, None] * targets, targets - step_size[:, None] * image)


def solution(mesh):
    return jax.shard_map(
        on_device,
        mesh=mesh,
        in_specs=(P(None, "blk"), P(None, "blk"), P(), P(), P("blk")),
        out_specs=(P(None, "blk"), P(None, "blk")),
        check_vma=False,
    )
```

time: 178 us -> 156 us (0.88)
  Pallas kernels: 115 us -> 93.1 us
  starting transfers between devices: 48.3 us -> 31.5 us
  blocking collectives: 0 us -> 16.7 us
    pallas_call x4 -> x5, Pallas kernels: 115 us -> 93.1 us  [run_tiles(): pl.pallas_call(functools.partial(tile_kernel, len(rows), places, begun),...]
    all_to_all x0 -> x1, blocking collectives: none -> 16.7 us  [on_device(): lax.all_to_all(jnp.broadcast_to(scalars[None], (blocks, 2 * NVEC)), 'blk'...]
    ppermute x18 -> x8, starting transfers between devices: 37.6 us -> 26.9 us  [the longest x1 10.7 us: on_device(): scalars = scalars + lax.ppermute(scalars, 'grp', [(0, 1), (1, 0)])]
    ppermute x4 -> x2, starting transfers between devices: 8.29 us -> 2.62 us  [on_device(): returned.append(lax.ppermute(sums['y', c], BOTH, backward(column_route(c))))]
    ppermute x18 -> x8, waiting for transfers between devices: 9.89 us -> 6.11 us  [the longest x1 3.15 us: on_device(): theirs = lax.ppermute(own, 'grp', [(0, 1), (1, 0)])]
    ppermute x3, waiting for transfers between devices: 0.01 us -> 2.25 us  [on_device(): returned.append(lax.ppermute(sums['x', c], BOTH, backward(row_route(c))))]
  transfers between devices with their start and end apart: 25 -> 13, of which waited for: 5 -> 5; matrix products, arithmetic and copies ran while one was open for 0% -> 1% of each run, Pallas kernels for 65% -> 24%
where the time goes in v4:
time: 156 us
  Pallas kernels  93.1 us (60%)
  starting transfers between devices  31.5 us (20%)
  blocking collectives  16.7 us (11%)
  waiting for transfers between devices  8.37 us (5%)
  other arithmetic  3.17 us (2%)
  local copies, waits for them, and re-layouts  2.27 us (1%)
    pallas_call x5, Pallas kernels, run_tiles(): pl.pallas_call(functools.partial(tile_kernel, len(rows), places, begun),...  93.1 us
    all_to_all x1, blocking collectives, on_device(): lax.all_to_all(jnp.broadcast_to(scalars[None], (blocks, 2 * NVEC)), 'blk'...  16.7 us
    ppermute x1, starting transfers between devices, on_device(): scalars = scalars + lax.ppermute(scalars, 'grp', [(0, 1), (1, 0)])  10.7 us
    ppermute x2, starting transfers between devices, on_device(): returned.append(lax.ppermute(part, BOTH, backward(column_route(c))))  7.45 us
    ppermute x1, starting transfers between devices, on_device(): beside = lax.ppermute(chip, 'blk', [(i, i ^ 2) for i in range(64)])  4.88 us
    ppermute x1, starting transfers between devices, on_device(): first_column = lax.ppermute(shard, BOTH, column_route(0))  3.35 us
    ppermute x1, waiting for transfers between devices, on_device(): theirs = lax.ppermute(own, 'grp', [(0, 1), (1, 0)])  3.15 us
  transfers between devices with their start and end apart: 13, of which 5 were waited for; matrix products, arithmetic and copies ran while one was open for 1% of the time, Pallas kernels for 24%

profile of v4, /device:TPU:0, one launch (start us, length us, event | category | flops | bytes accessed | tf_op | source)
XLA Modules:
  0.0 156.0 jit_solution(14898233814182298971)
XLA Ops:
  0.6 0.0 copy-start.6
  0.7 0.7 copy-done.6
  1.4 0.0 copy-start.7
  1.4 0.0 copy-start.5
  1.4 1.0 pad_maximum_fusion.2.refs_3_
  2.4 0.0 copy-start.8
  2.4 0.1 collective-permute-start
  2.5 3.3 %collective-permute-start.2 = (f32[24,1536]{1,0:T(8,128)S(1)}, f32[24,1536]{1,0:T(8,128)S(1)}, u32[]{:S(2)}, u32[]{:S(2)}) collective-permute-start(f32[24,1536]{1,0:T(8,128)S(1)} %pad_maximum_fusion.2.refs_3_), channel_id=1, source_target_pairs={{64,0},{9,1},{18,2},{27,3},{36,4},{45,5},{54,6},{63,7},{72,8},{17,... | collective-permute-start | bytes 442376 | tf_op jit(solution)/shard_map/ppermute | solution.py:300
  5.8 0.0 copy-done.9
  5.8 0.0 copy-done.7
  5.8 0.0 copy-done.8
  5.8 0.1 select_reduce_fusion
  5.9 0.0 copy-done.5
  5.9 0.1 multiply_reduce_fusion
  6.1 0.0 copy-start.10
  6.1 0.6 copy-done.10
  6.8 0.6 dynamic_slice.17
  7.4 0.7 pad_add_fusion.refs_1_
  8.1 0.0 copy-start.4
  8.1 0.0 collective-permute-done.refs_4_
  8.1 4.9 %collective-permute-start.1 = (f32[48,1536]{1,0:T(8,128)S(1)}, f32[48,1536]{1,0:T(8,128)S(1)}, u32[]{:S(2)}, u32[]{:S(2)}) collective-permute-start(f32[48,1536]{1,0:T(8,128)S(1)} %pad_maximum_fusion.1), channel_id=1, source_target_pairs={{0,4},{2,6},{4,0},{6,2},{8,12},{10,14},{12,8},{14,10},{16,20},{18,... | collective-permute-start | bytes 884744 | tf_op jit(solution)/shard_map/ppermute | solution.py:303
  13.0 0.0 collective-permute-done.2.refs_5_.refs_4_
  13.0 0.0 copy-done.4
  13.0 12.2 %shard_map.158 = (f32[16,1536]{1,0:T(8,128)S(1)}, f32[16,1536]{1,0:T(8,128)S(1)}, f32[16,1536]{1,0:T(8,128)S(1)}, f32[16,128]{1,0:T(8,128)S(1)}) custom-call(s32[5,8,3]{2,1,0:T(8,128)S(1)} %copy-done.4, s32[2]{0:T(128)S(1)} %pad.refs_1_, f32[3]{0:T(128)S(1)} %broadcast_divide_fusion.refs_2_, f32[24,1536]{1,0:T(8,128)S(1)} %pad_maximum_fusion.2.refs_3_, ...), custom_call_target="tpu_custom_call" | custom-call | flops 12000000000 | bytes 2000000 | tf_op jit(solution)/shard_map/pallas_call | solution.py:270
  25.2 0.0 copy-start.3
  25.2 0.0 collective-permute-done.1.refs_3_.refs_5_
  25.3 0.4 collective-permute-start.3
  25.7 0.3 copy-done.3
  26.0 0.0 copy-start.1
  26.0 12.2 %shard_map.159 = (f32[16,1536]{1,0:T(8,128)S(1)}, f32[16,1536]{1,0:T(8,128)S(1)}, f32[16,1536]{1,0:T(8,128)S(1)}, f32[16,128]{1,0:T(8,128)S(1)}) custom-call(s32[5,8,3]{2,1,0:T(8,128)S(1)} %copy-done.3, s32[2]{0:T(128)S(1)} %pad.refs_1_, f32[3]{0:T(128)S(1)} %broadcast_divide_fusion.refs_2_, f32[48,1536]{1,0:T(8,128)S(1)} %collective-permute-done.1.refs_3_.refs_5_, ...), custom_call_target="tpu_custom_call" | custom-call | flops 12000000000 | bytes 2000000 | tf_op jit(solution)/shard_map/pallas_call | solution.py:270
  38.2 1.6 %collective-permute-done.3.refs_6_.refs_4_ = f32[72,1536]{1,0:T(8,128)S(1)} collective-permute-done((f32[72,1536]{1,0:T(8,128)S(1)}, f32[72,1536]{1,0:T(8,128)S(1)}, u32[]{:S(2)}, u32[]{:S(2)}) %collective-permute-start.3) | collective-permute-done | bytes 442400 | tf_op jit(solution)/shard_map/ppermute | solution.py:326
  39.8 0.0 copy-done.1
  39.8 0.0 copy-start
  39.8 22.9 %shard_map.160 = (f32[16,1536]{1,0:T(8,128)S(1)}, f32[16,1536]{1,0:T(8,128)S(1)}, f32[16,1536]{1,0:T(8,128)S(1)}, f32[16,1536]{1,0:T(8,128)S(1)}, f32[16,1536]{1,0:T(8,128)S(1)}, /*index=5*/f32[16,128]{1,0:T(8,128)S(1)}) custom-call(s32[5,16,3]{2,1,0:T(8,128)S(1)} %copy-done.1, s32[2]{0:T(128)S(1)} %pad.1.refs_1_, f32[3]{0:T(128)S(1)} %broadcast_divide_fusion.refs_2_, ...), custom_call_target="tpu_custom_call" | custom-call | flops 24000000000 | bytes 2000000 | tf_op jit(solution)/shard_map/pallas_call | solution.py:270
  62.7 0.0 copy-done
  62.7 0.0 copy-start.2
  62.7 33.5 %shard_map.161 = (f32[16,1536]{1,0:T(8,128)S(1)}, f32[16,1536]{1,0:T(8,128)S(1)}, f32[16,1536]{1,0:T(8,128)S(1)}, f32[16,1536]{1,0:T(8,128)S(1)}, f32[16,1536]{1...) custom-call(s32[5,26,3]{2,1,0:T(8,128)S(1)} %copy-done, s32[2]{0:T(128)S(1)} %pad_add_fusion.refs_1_, ...), custom_call_target="tpu_custom_call" | custom-call | flops 38999998464 | bytes 2000000 | tf_op jit(solution)/shard_map/pallas_call | solution.py:270
  96.2 4.2 %collective-permute-start.5 = (f32[16,1536]{1,0:T(8,128)S(1)}, f32[16,1536]{1,0:T(8,128)S(1)}, u32[]{:S(2)}, u32[]{:S(2)}) collective-permute-start(f32[16,1536]{1,0:T(8,128)S(1)} %get-tuple-element.60), channel_id=1, source_target_pairs={{0,66},{1,11},{2,16},{3,25},{4,38},{5,47},{6,52},{7,61},{8,74},{9,... | collective-permute-start | bytes 294920 | tf_op jit(solution)/shard_map/ppermute | solution.py:331
  100.4 3.2 %collective-permute-start.4 = (f32[16,1536]{1,0:T(8,128)S(1)}, f32[16,1536]{1,0:T(8,128)S(1)}, u32[]{:S(2)}, u32[]{:S(2)}) collective-permute-start(f32[16,1536]{1,0:T(8,128)S(1)} %get-tuple-element.58), channel_id=1, source_target_pairs={{0,64},{1,9},{2,18},{3,27},{4,36},{5,45},{6,54},{7,63},{8,72},{9,1... | collective-permute-start | bytes 294920 | tf_op jit(solution)/shard_map/ppermute | solution.py:331
  103.6 0.0 copy-done.2
  103.6 12.3 %shard_map.162 = (f32[16,1536]{1,0:T(8,128)S(1)}, f32[16,1536]{1,0:T(8,128)S(1)}, f32[16,1536]{1,0:T(8,128)S(1)}, f32[16,128]{1,0:T(8,128)S(1)}) custom-call(s32[5,8,3]{2,1,0:T(8,128)S(1)} %copy-done.2, s32[2]{0:T(128)S(1)} %pad.refs_1_, f32[3]{0:T(128)S(1)} %broadcast_divide_fusion.refs_2_, f32[24,1536]{1,0:T(8,128)S(1)} %pad_maximum_fusion.2.refs_3_, ...), custom_call_target="tpu_custom_call" | custom-call | flops 12000000000 | bytes 2000000 | tf_op jit(solution)/shard_map/pallas_call | solution.py:270
  116.0 0.1 reduce_sum.46
  116.1 0.1 collective-permute-start.6
  116.2 0.1 collective-permute-start.7
  116.3 1.8 %collective-permute-start.8 = (f32[16,1536]{1,0:T(8,128)S(1)}, f32[16,1536]{1,0:T(8,128)S(1)}, u32[]{:S(2)}, u32[]{:S(2)}) collective-permute-start(f32[16,1536]{1,0:T(8,128)S(1)} %get-tuple-element.63), channel_id=1, source_target_pairs={{0,6},{1,7},{2,4},{3,5},{4,2},{5,3},{6,0},{7,1},{8,14},{9,15},{10,... | collective-permute-start | bytes 294920 | tf_op jit(solution)/shard_map/ppermute | solution.py:333
  118.0 0.0 collective-permute-done.5
  118.0 0.0 collective-permute-start.10
  118.0 0.0 collective-permute-done.4
  118.1 2.6 %collective-permute-start.9 = (f32[16,1536]{1,0:T(8,128)S(1)}, f32[16,1536]{1,0:T(8,128)S(1)}, u32[]{:S(2)}, u32[]{:S(2)}) collective-permute-start(f32[16,1536]{1,0:T(8,128)S(1)} %get-tuple-element.65), channel_id=1, source_target_pairs={{0,68},{1,13},{2,22},{3,31},{4,32},{5,41},{6,50},{7,59},{8,76},{9,... | collective-permute-start | bytes 294920 | tf_op jit(solution)/shard_map/ppermute | solution.py:335
  120.7 0.1 pad_maximum_fusion.3
  120.8 0.0 collective-permute-done.6
  120.8 1.1 collective-permute-done.7
  121.9 1.2 collective-permute-done.8
  123.0 16.7 %all_to_all.6 = f32[64,1,32]{2,1,0:T(1,128)S(1)} all-to-all(f32[64,1,32]{2,1,0:T(1,128)S(1)} %broadcast_in_dim.29), channel_id=1, replica_groups=mesh['blk'=64,'grp'=2] {'blk'}, dimensions={0} | all-to-all | bytes 16384 | tf_op jit(solution)/shard_map/all_to_all | solution.py:346
  139.7 0.1 reduce_sum.49
  139.8 0.0 collective-permute-done.10
  139.8 0.0 collective-permute-done.9
  139.8 10.7 %collective-permute-start.11 = (f32[32]{0:T(128)S(1)}, f32[32]{0:T(128)S(1)}, u32[]{:S(2)}, u32[]{:S(2)}) collective-permute-start(f32[32]{0:T(128)S(1)} %reduce_sum.49), channel_id=1, source_target_pairs={{0,1},{1,0},{2,3},{3,2},{4,5},{5,4},{6,7},{7,6},{8,9},{9,8},{10,11... | collective-permute-start | bytes 392 | tf_op jit(solution)/shard_map/ppermute | solution.py:356
  150.5 0.1 add_add_fusion
  150.5 0.1 collective-permute-start.12
  150.6 1.4 collective-permute-done.11
  152.0 0.1 slice_divide_fusion
  152.1 3.1 %collective-permute-done.12 = f32[16,1536]{1,0:T(8,128)S(1)} collective-permute-done((f32[16,1536]{1,0:T(8,128)S(1)}, f32[16,1536]{1,0:T(8,128)S(1)}, u32[]{:S(2)}, u32[]{:S(2)}) %collective-permute-start.12) | collective-permute-done | bytes 98336 | tf_op jit(solution)/shard_map/ppermute | solution.py:355
  155.2 0.8 fusion.2
  (11 shorter events, 0.1 us)
Async XLA Ops:
  0.6 0.7 copy-start.6
  1.4 4.5 %copy-start.9 = (f32[3]{0:T(128)S(1)}, f32[3]{0:T(128)}, u32[]{:S(2)}) copy-start(f32[3]{0:T(128)} %param.17) | copy-start | bytes 40
  1.4 4.5 %copy-start.7 = (s32[1536]{0:T(1024)S(1)}, s32[1536]{0:T(1024)}, u32[]{:S(2)}) copy-start(s32[1536]{0:T(1024)} %param.19) | copy-start | bytes 18436
  1.4 4.6 %copy-start.5 = (f32[16,1536]{1,0:T(8,128)S(1)}, f32[16,1536]{1,0:T(8,128)}, u32[]{:S(2)}) copy-start(f32[16,1536]{1,0:T(8,128)} %param.16) | copy-start | bytes 294916
  2.4 3.5 %copy-start.8 = (f32[8]{0:T(128)S(1)}, f32[8]{0:T(128)}, u32[]{:S(2)}) copy-start(f32[8]{0:T(128)} %param.18) | copy-start | bytes 100
  2.4 5.7 %collective-permute-start = (f32[24,1536]{1,0:T(8,128)S(1)}, f32[24,1536]{1,0:T(8,128)S(1)}, u32[]{:S(2)}, u32[]{:S(2)}) collective-permute-start(f32[24,1536]{1,0:T(8,128)S(1)} %pad_maximum_fusion.2.refs_3_), channel_id=1, source_target_pairs={{0,2},{2,0},{4,6},{6,4},{8,10},{10,8},{12,14},{14,12},{16,18},{18,... | collective-permute-start | bytes 442376 | tf_op jit(solution)/shard_map/ppermute | solution.py:301
  2.5 10.5 %collective-permute-start.2 = (f32[24,1536]{1,0:T(8,128)S(1)}, f32[24,1536]{1,0:T(8,128)S(1)}, u32[]{:S(2)}, u32[]{:S(2)}) collective-permute-start(f32[24,1536]{1,0:T(8,128)S(1)} %pad_maximum_fusion.2.refs_3_), channel_id=1, source_target_pairs={{64,0},{9,1},{18,2},{27,3},{36,4},{45,5},{54,6},{63,7},{72,8},{17,... | collective-permute-start | bytes 442376 | tf_op jit(solution)/shard_map/ppermute | solution.py:300
  6.1 0.7 copy-start.10
  8.1 4.9 %copy-start.4 = (s32[5,8,3]{2,1,0:T(8,128)S(1)}, s32[5,8,3]{2,1,0:T(8,128)}, u32[]{:S(2)}) copy-start(s32[5,8,3]{2,1,0:T(8,128)} %constant.55.clone.refs_0_) | copy-start | bytes 1444
  8.1 17.1 %collective-permute-start.1 = (f32[48,1536]{1,0:T(8,128)S(1)}, f32[48,1536]{1,0:T(8,128)S(1)}, u32[]{:S(2)}, u32[]{:S(2)}) collective-permute-start(f32[48,1536]{1,0:T(8,128)S(1)} %pad_maximum_fusion.1), channel_id=1, source_target_pairs={{0,4},{2,6},{4,0},{6,2},{8,12},{10,14},{12,8},{14,10},{16,20},{18,... | collective-permute-start | bytes 884744 | tf_op jit(solution)/shard_map/ppermute | solution.py:303
  25.2 0.7 copy-start.3
  25.3 14.5 %collective-permute-start.3 = (f32[72,1536]{1,0:T(8,128)S(1)}, f32[72,1536]{1,0:T(8,128)S(1)}, u32[]{:S(2)}, u32[]{:S(2)}) collective-permute-start(f32[72,1536]{1,0:T(8,128)S(1)} %pad_maximum_fusion), channel_id=1, source_target_pairs={{64,0},{9,1},{18,2},{27,3},{36,4},{45,5},{54,6},{63,7},{72,8},{17,... | collective-permute-start | bytes 1327112 | tf_op jit(solution)/shard_map/ppermute | solution.py:326
  26.0 13.8 %copy-start.1 = (s32[5,16,3]{2,1,0:T(8,128)S(1)}, s32[5,16,3]{2,1,0:T(8,128)}, u32[]{:S(2)}) copy-start(s32[5,16,3]{2,1,0:T(8,128)} %constant.58.clone.refs_0_) | copy-start | bytes 2884
  39.8 22.9 %copy-start = (s32[5,26,3]{2,1,0:T(8,128)S(1)}, s32[5,26,3]{2,1,0:T(8,128)}, u32[]{:S(2)}) copy-start(s32[5,26,3]{2,1,0:T(8,128)} %constant.60.clone.refs_0_) | copy-start | bytes 4684
  62.7 40.9 %copy-start.2 = (s32[5,8,3]{2,1,0:T(8,128)S(1)}, s32[5,8,3]{2,1,0:T(8,128)}, u32[]{:S(2)}) copy-start(s32[5,8,3]{2,1,0:T(8,128)} %constant.61.clone.refs_0_) | copy-start | bytes 1444
  96.2 21.9 %collective-permute-start.5 = (f32[16,1536]{1,0:T(8,128)S(1)}, f32[16,1536]{1,0:T(8,128)S(1)}, u32[]{:S(2)}, u32[]{:S(2)}) collective-permute-start(f32[16,1536]{1,0:T(8,128)S(1)} %get-tuple-element.60), channel_id=1, source_target_pairs={{0,66},{1,11},{2,16},{3,25},{4,38},{5,47},{6,52},{7,61},{8,74},{9,... | collective-permute-start | bytes 294920 | tf_op jit(solution)/shard_map/ppermute | solution.py:331
  100.4 17.6 %collective-permute-start.4 = (f32[16,1536]{1,0:T(8,128)S(1)}, f32[16,1536]{1,0:T(8,128)S(1)}, u32[]{:S(2)}, u32[]{:S(2)}) collective-permute-start(f32[16,1536]{1,0:T(8,128)S(1)} %get-tuple-element.58), channel_id=1, source_target_pairs={{0,64},{1,9},{2,18},{3,27},{4,36},{5,45},{6,54},{7,63},{8,72},{9,1... | collective-permute-start | bytes 294920 | tf_op jit(solution)/shard_map/ppermute | solution.py:331
  116.1 4.7 %collective-permute-start.6 = (f32[16,1536]{1,0:T(8,128)S(1)}, f32[16,1536]{1,0:T(8,128)S(1)}, u32[]{:S(2)}, u32[]{:S(2)}) collective-permute-start(f32[16,1536]{1,0:T(8,128)S(1)} %get-tuple-element.61), channel_id=1, source_target_pairs={{0,2},{1,3},{2,0},{3,1},{4,6},{5,7},{6,4},{7,5},{8,10},{9,11},{10,... | collective-permute-start | bytes 294920 | tf_op jit(solution)/shard_map/ppermute | solution.py:333
  116.2 5.7 %collective-permute-start.7 = (f32[16,1536]{1,0:T(8,128)S(1)}, f32[16,1536]{1,0:T(8,128)S(1)}, u32[]{:S(2)}, u32[]{:S(2)}) collective-permute-start(f32[16,1536]{1,0:T(8,128)S(1)} %get-tuple-element.62), channel_id=1, source_target_pairs={{0,4},{1,5},{2,6},{3,7},{4,0},{5,1},{6,2},{7,3},{8,12},{9,13},{10,... | collective-permute-start | bytes 294920 | tf_op jit(solution)/shard_map/ppermute | solution.py:333
  116.3 6.7 %collective-permute-start.8 = (f32[16,1536]{1,0:T(8,128)S(1)}, f32[16,1536]{1,0:T(8,128)S(1)}, u32[]{:S(2)}, u32[]{:S(2)}) collective-permute-start(f32[16,1536]{1,0:T(8,128)S(1)} %get-tuple-element.63), channel_id=1, source_target_pairs={{0,6},{1,7},{2,4},{3,5},{4,2},{5,3},{6,0},{7,1},{8,14},{9,15},{10,... | collective-permute-start | bytes 294920 | tf_op jit(solution)/shard_map/ppermute | solution.py:333
  118.0 21.8 %collective-permute-start.10 = (f32[16,1536]{1,0:T(8,128)S(1)}, f32[16,1536]{1,0:T(8,128)S(1)}, u32[]{:S(2)}, u32[]{:S(2)}) collective-permute-start(f32[16,1536]{1,0:T(8,128)S(1)} %get-tuple-element.66), channel_id=1, source_target_pairs={{0,70},{1,15},{2,20},{3,29},{4,34},{5,43},{6,48},{7,57},{8,78},{9,... | collective-permute-start | bytes 294920 | tf_op jit(solution)/shard_map/ppermute | solution.py:335
  118.1 21.8 %collective-permute-start.9 = (f32[16,1536]{1,0:T(8,128)S(1)}, f32[16,1536]{1,0:T(8,128)S(1)}, u32[]{:S(2)}, u32[]{:S(2)}) collective-permute-start(f32[16,1536]{1,0:T(8,128)S(1)} %get-tuple-element.65), channel_id=1, source_target_pairs={{0,68},{1,13},{2,22},{3,31},{4,32},{5,41},{6,50},{7,59},{8,76},{9,... | collective-permute-start | bytes 294920 | tf_op jit(solution)/shard_map/ppermute | solution.py:335
  139.8 12.2 %collective-permute-start.11 = (f32[32]{0:T(128)S(1)}, f32[32]{0:T(128)S(1)}, u32[]{:S(2)}, u32[]{:S(2)}) collective-permute-start(f32[32]{0:T(128)S(1)} %reduce_sum.49), channel_id=1, source_target_pairs={{0,1},{1,0},{2,3},{3,2},{4,5},{5,4},{6,7},{7,6},{8,9},{9,8},{10,11... | collective-permute-start | bytes 392 | tf_op jit(solution)/shard_map/ppermute | solution.py:356
  150.5 4.7 %collective-permute-start.12 = (f32[16,1536]{1,0:T(8,128)S(1)}, f32[16,1536]{1,0:T(8,128)S(1)}, u32[]{:S(2)}, u32[]{:S(2)}) collective-permute-start(f32[16,1536]{1,0:T(8,128)S(1)} %add_add_fusion), channel_id=1, source_target_pairs={{0,1},{1,0},{2,3},{3,2},{4,5},{5,4},{6,7},{7,6},{8,9},{9,8},{10,11... | collective-permute-start | bytes 294920 | tf_op jit(solution)/shard_map/ppermute | solution.py:355

commit v5 on v4

--- a/solution.py
+++ b/solution.py
@@ -31,13 +31,25 @@
     return (CHUNKS * block + member // 2) * 2 + member % 2
 
 
+DISTANCE = [8 - 2 * (m // 2) if m % 2 == 0 else 7 - 2 * ((m // 2) ^ 2) for m in range(8)]
+
+
+def column_source(a, m):
+    s = (a + DISTANCE[m]) % NSUPER
+    k, g = m // 2, m % 2
+    k ^= 2 * ((a ^ s) & 1)
+    even = 8 - 2 * k
+    crosses = [s % 8 < even, s % 8 < even - 1]
+    return s, k, g ^ (crosses[0] and crosses[1])
+
+
 def column_route(chunk):
     route = []
     for a in range(NSUPER):
-        for d in range(8):
-            source = (a + (d if d else 8)) % NSUPER
-            member = ((d // 2) ^ chunk) * 2 + d % 2
-            route.append((device_at(source, member), device_at(a, d)))
+        for m in range(8):
+            s, k, g = column_source(a, m)
+            route.append((device_at(s, 2 * (k ^ chunk) + g), device_at(a, m)))
+    assert len({x for x, _ in route}) == len({x for _, x in route}) == 128
     return route
 
 
@@ -49,28 +61,17 @@
     ]
 
 
-def block_route():
-    return [
-        (device_at((a + (d if d else 8)) % NSUPER, d), device_at(a, d))
-        for a in range(NSUPER)
-        for d in range(8)
-    ]
-
-
 def backward(route):
     return [(b, a) for a, b in route]
 
 
 CALLS = [
-    ((0, 1), (0,), [(0, 0), (1, 0)]),
-    ((2, 3), (0,), [(2, 0), (3, 0)]),
-    ((0, 1, 2, 3), (1,), [(0, 1), (1, 1), (2, 1), (3, 1)]),
-    ((0, 1, 2, 3), (2, 3), [(i, j) for i in (1, 2, 3) for j in (2, 3)]),
-    ((0,), (2, 3), [(0, 2), (0, 3)]),
+    ((0, 1, 2, 3), (0,), [(i, 0) for i in range(4)]),
+    ((0, 1, 2, 3), (1, 2, 3), [(i, j) for j in (1, 2, 3) for i in range(4)]),
 ]
 OFF = [(1, 0), (2, 1), (3, 1), (0, 2), (0, 3), (2, 3)]
 ON = [[(0, 0), (1, 1)], [(2, 2), (3, 3)]]
-FILL = [[0, 8, 4, 20, 0], [4, 8, 8, 12, 0]]
+FILL = [[8, 24], [12, 20]]
 PER = SHARD // TILE
 GIVEN = [(0, 3 * PER), (1, 3 * PER), (0, 3 * PER + 1), (1, 3 * PER + 1)]
 
@@ -100,7 +101,7 @@
             triangles[half] = [t for t in triangles[half] if t not in part]
             tiles += [(at(i), at(j), int(i != j)) for i, j in part]
             lists.append(tiles)
-        given = GIVEN if call == 3 else []
+        given = GIVEN if call == 1 else []
         lists.append(regular + [(at(i), at(j), 1) for i, j in given[:2]])
         lists.append(regular + [(at(i, 1), at(j, 1), 1) for i, j in given[2:]])
         longest = max(len(x) for x in lists)
@@ -297,12 +298,15 @@
 
 def on_device(points, targets, length_scales, noise_levels, noise_class):
     shard = jnp.concatenate([points, targets, jnp.zeros((ROWS - 19, SHARD), f32)], axis=0)
+    swap = [(i, i ^ 1) for i in range(64)]
     first_column = lax.ppermute(shard, BOTH, column_route(0))
-    partner = lax.ppermute(shard, "blk", [(i, i ^ 1) for i in range(64)])
-    chip = jnp.concatenate([shard, partner], axis=0)
-    beside = lax.ppermute(chip, "blk", [(i, i ^ 2) for i in range(64)])
-    rows = {0: (shard, 0), 1: (partner, 0), 2: (beside, 0), 3: (beside, 1)}
-    columns = {0: (first_column, 0)}
+    beside = lax.ppermute(shard, "blk", [(i, i ^ 2) for i in range(64)])
+    partner = lax.ppermute(shard, "blk", swap)
+    across = lax.ppermute(beside, "blk", swap)
+    rest = jnp.concatenate([partner, beside, across], axis=0)
+    others = lax.ppermute(rest, BOTH, column_route(0))
+    rows = {0: (shard, 0), 1: (rest, 0), 2: (rest, 1), 3: (rest, 2)}
+    columns = {0: (first_column, 0), 1: (others, 0), 2: (others, 1), 3: (others, 2)}
 
     block = lax.axis_index("blk")
     member = (block % CHUNKS) * 2 + lax.axis_index("grp")
@@ -310,6 +314,11 @@
     variant = jnp.where(member == 1, 3, jnp.where(member == 2, 4, variant)).astype(jnp.int32)
     tables, counts = tile_tables()
     scale = (math.sqrt(5.0) * LOG2E) / length_scales
+
+    def sent_back(name):
+        kind, c = name
+        route = row_route(c) if kind == "x" else column_route(c)
+        return lax.ppermute(sums[name], BOTH, backward(route))
 
     sums, curve = {}, None
     returned = []
@@ -321,18 +330,8 @@
             [columns[c] for c in across], [sums.get(name) for name in names], curve,
         )
         sums.update(zip(names, parts))
-        if call == 0:
-            others = after(jnp.concatenate([partner, beside], axis=0), curve)
-            others = lax.ppermute(others, BOTH, block_route())
-            columns.update({c: (others, c - 1) for c in (1, 2, 3)})
-        if call == 3:
-            for c in (0, 1):
-                part = after(sums["y", c], curve)
-                returned.append(lax.ppermute(part, BOTH, backward(column_route(c))))
-            for c in (1, 2, 3):
-                returned.append(lax.ppermute(sums["x", c], BOTH, backward(row_route(c))))
-    for c in (2, 3):
-        returned.append(lax.ppermute(sums["y", c], BOTH, backward(column_route(c))))
+        done = [[("y", 0)], [("y", 1), ("y", 2), ("y", 3), ("x", 1), ("x", 2), ("x", 3)]]
+        returned += [sent_back(name) for name in done[call]]
 
     classes = lax.broadcasted_iota(jnp.int32, (noise_levels.shape[0], noise_class.shape[0]), 0)
     noise_diag = jnp.sum(
@@ -341,7 +340,7 @@
     own_noise = noise_diag[None, :] * targets
     norm = 0.5 * jnp.sum(targets * targets, axis=1)
     curvature = jnp.sum(curve, axis=1) + 0.5 * jnp.sum(targets * own_noise, axis=1)
-    scalars = after(jnp.concatenate([norm, curvature]), *returned[:5])
+    scalars = after(jnp.concatenate([norm, curvature]), *returned[:1])
     blocks = lax.axis_size("blk")
     scalars = lax.all_to_all(
         jnp.broadcast_to(scalars[None], (blocks, 2 * NVEC)), "blk", 0, 0, tiled=True

time: 156 us -> 141 us (0.904)
  Pallas kernels: 93.1 us -> 85.4 us
  starting transfers between devices: 31.5 us -> 28.1 us
  waiting for transfers between devices: 8.37 us -> 5.53 us
    ppermute x1, starting transfers between devices: 10.7 us -> 2.21 us  [on_device(): scalars = scalars + lax.ppermute(scalars, 'grp', [(0, 1), (1, 0)])]
    pallas_call x5 -> x2, Pallas kernels: 93.1 us -> 85.4 us  [run_tiles(): pl.pallas_call(functools.partial(tile_kernel, len(rows), places, begun),...]
    ppermute x10 -> x11, starting transfers between devices: 17.4 us -> 21.2 us  [the longest x7 15.5 us: sent_back(): return lax.ppermute(sums[name], BOTH, backward(route))]
    ppermute x10 -> x11, waiting for transfers between devices: 3.85 us -> 1.01 us  [the longest x1 0.98 us: on_device(): across = lax.ppermute(beside, 'blk', swap)]
  transfers between devices with their start and end apart: 13 -> 14, of which waited for: 5 -> 3; matrix products, arithmetic and copies ran while one was open for 1% -> 1% of each run, Pallas kernels for 24% -> 61%
where the time goes in v5:
time: 141 us; the launch traced here: 140 us
  Pallas kernels  85.4 us (61%)
  starting transfers between devices  28.1 us (20%)
  blocking collectives  16.1 us (11%)
  waiting for transfers between devices  5.53 us (4%)
  other arithmetic  3.16 us (2%)
    pallas_call x2, Pallas kernels, run_tiles(): pl.pallas_call(functools.partial(tile_kernel, len(rows), places, begun),...  85.4 us
    all_to_all x1, blocking collectives, on_device(): lax.all_to_all(jnp.broadcast_to(scalars[None], (blocks, 2 * NVEC)), 'blk'...  16.1 us
    ppermute x7, starting transfers between devices, sent_back(): return lax.ppermute(sums[name], BOTH, backward(route))  15.5 us
    ppermute x1, starting transfers between devices, on_device(): first_column = lax.ppermute(shard, BOTH, column_route(0))  4.55 us
    ppermute x1, waiting for transfers between devices, on_device(): theirs = lax.ppermute(own, 'grp', [(0, 1), (1, 0)])  3.15 us
  transfers between devices with their start and end apart: 14, of which 3 were waited for; matrix products, arithmetic and copies ran while one was open for 1% of the time, Pallas kernels for 61%

profile of v5, /device:TPU:0, one launch (start us, length us, event | category | flops | bytes accessed | tf_op | source)
XLA Modules:
  0.0 140.5 jit_solution(14322694497346082156)
XLA Ops:
  0.6 0.1 pad.5.clone
  0.7 0.0 copy-start.5
  0.7 0.0 copy-start.3
  0.7 0.0 copy-start.2
  0.7 1.0 maximum_maximum_fusion.refs_3_
  1.8 0.0 copy-start.4
  1.8 1.7 %collective-permute-start.1 = (f32[24,1536]{1,0:T(8,128)S(1)}, f32[24,1536]{1,0:T(8,128)S(1)}, u32[]{:S(2)}, u32[]{:S(2)}) collective-permute-start(f32[24,1536]{1,0:T(8,128)S(1)} %maximum_maximum_fusion.refs_3_), channel_id=1, source_target_pairs={{0,4},{2,6},{4,0},{6,2},{8,12},{10,14},{12,8},{14,10},{16,20},{18,... | collective-permute-start | bytes 442376 | tf_op jit(solution)/shard_map/ppermute | solution.py:303
  3.4 0.0 collective-permute-start
  3.4 4.5 %collective-permute-start.4 = (f32[24,1536]{1,0:T(8,128)S(1)}, f32[24,1536]{1,0:T(8,128)S(1)}, u32[]{:S(2)}, u32[]{:S(2)}) collective-permute-start(f32[24,1536]{1,0:T(8,128)S(1)} %maximum_maximum_fusion.refs_3_), channel_id=1, source_target_pairs={{65,0},{29,1},{50,2},{15,3},{36,4},{57,5},{22,6},{43,7},{73,8},{37... | collective-permute-start | bytes 442376 | tf_op jit(solution)/shard_map/ppermute | solution.py:302
  8.0 0.0 copy-done.5
  8.0 0.0 copy-done.3
  8.0 0.0 copy-done.4
  8.0 0.1 select_reduce_fusion
  8.1 0.0 copy-done.2
  8.1 0.1 multiply_reduce_fusion
  8.3 0.0 copy-start.6
  8.3 0.6 copy-done.6
  8.9 0.6 dynamic_slice.6
  9.5 0.7 pad_add_fusion.refs_1_
  10.2 0.0 collective-permute-done
  10.3 0.0 collective-permute-done.1
  10.3 1.7 %collective-permute-start.2 = (f32[24,1536]{1,0:T(8,128)S(1)}, f32[24,1536]{1,0:T(8,128)S(1)}, u32[]{:S(2)}, u32[]{:S(2)}) collective-permute-start(f32[24,1536]{1,0:T(8,128)S(1)} %collective-permute-done.1), channel_id=1, source_target_pairs={{0,2},{2,0},{4,6},{6,4},{8,10},{10,8},{12,14},{14,12},{16,18},{18,... | collective-permute-start | bytes 442376 | tf_op jit(solution)/shard_map/ppermute | solution.py:305
  11.9 0.0 copy-start.1
  12.0 1.0 collective-permute-done.2
  13.0 0.0 copy-start
  13.0 2.4 %collective-permute-start.3 = (f32[72,1536]{1,0:T(8,128)S(1)}, f32[72,1536]{1,0:T(8,128)S(1)}, u32[]{:S(2)}, u32[]{:S(2)}) collective-permute-start(f32[72,1536]{1,0:T(8,128)S(1)} %constant_dynamic-update-slice_fusion.refs_4_), channel_id=1, source_target_pairs={{65,0},{29,1},{50,2},{15,3},{36,4},{57,5},{22,6},{43,7},{73,8},{37... | collective-permute-start | bytes 1327112 | tf_op jit(solution)/shard_map/ppermute | solution.py:307
  15.4 0.0 collective-permute-done.4.refs_5_
  15.4 0.0 copy-done.1
  15.4 22.7 %shard_map.104 = (f32[16,1536]{1,0:T(8,128)S(1)}, f32[16,1536]{1,0:T(8,128)S(1)}, f32[16,1536]{1,0:T(8,128)S(1)}, f32[16,1536]{1,0:T(8,128)S(1)}, f32[16,1536]{1,0:T(8,128)S(1)}, /*index=5*/f32[16,128]{1,0:T(8,128)S(1)}) custom-call(s32[5,16,3]{2,1,0:T(8,128)S(1)} %copy-done.1, s32[2]{0:T(128)S(1)} %pad.refs_1_, f32[3]{0:T(128)S(1)} %broadcast_divide_fusion.refs_2_, ...), custom_call_target="tpu_custom_call" | custom-call | flops 24000000000 | bytes 2000000 | tf_op jit(solution)/shard_map/pallas_call | solution.py:271
  38.0 1.0 collective-permute-start.5
  39.0 0.0 collective-permute-done.3.refs_5_
  39.0 0.0 copy-done
  39.0 62.8 %shard_map.105 = (f32[16,1536]{1,0:T(8,128)S(1)}, f32[16,1536]{1,0:T(8,128)S(1)}, f32[16,1536]{1,0:T(8,128)S(1)}, f32[16,1536]{1,0:T(8,128)S(1)}, f32[16,1536]{1...) custom-call(s32[5,50,3]{2,1,0:T(8,128)S(1)} %copy-done, ...), custom_call_target="tpu_custom_call" | custom-call | flops 74999996416 | bytes 2000000 | tf_op jit(solution)/shard_map/pallas_call | solution.py:271
  101.8 0.1 reduce_sum.46
  101.9 3.1 %collective-permute-start.10 = (f32[16,1536]{1,0:T(8,128)S(1)}, f32[16,1536]{1,0:T(8,128)S(1)}, u32[]{:S(2)}, u32[]{:S(2)}) collective-permute-start(f32[16,1536]{1,0:T(8,128)S(1)} %get-tuple-element.37), channel_id=1, source_target_pairs={{0,4},{1,5},{2,6},{3,7},{4,0},{5,1},{6,2},{7,3},{8,12},{9,13},{10,... | collective-permute-start | bytes 294920 | tf_op jit(solution)/shard_map/ppermute | solution.py:321
  105.0 0.5 collective-permute-start.11
  105.5 3.6 %collective-permute-start.6 = (f32[16,1536]{1,0:T(8,128)S(1)}, f32[16,1536]{1,0:T(8,128)S(1)}, u32[]{:S(2)}, u32[]{:S(2)}) collective-permute-start(f32[16,1536]{1,0:T(8,128)S(1)} %get-tuple-element.33), channel_id=1, source_target_pairs={{0,67},{1,31},{2,48},{3,13},{4,38},{5,59},{6,20},{7,41},{8,75},{9,... | collective-permute-start | bytes 294920 | tf_op jit(solution)/shard_map/ppermute | solution.py:321
  109.1 5.2 %collective-permute-start.7 = (f32[16,1536]{1,0:T(8,128)S(1)}, f32[16,1536]{1,0:T(8,128)S(1)}, u32[]{:S(2)}, u32[]{:S(2)}) collective-permute-start(f32[16,1536]{1,0:T(8,128)S(1)} %get-tuple-element.34), channel_id=1, source_target_pairs={{0,69},{1,25},{2,54},{3,11},{4,32},{5,61},{6,18},{7,47},{8,77},{9,... | collective-permute-start | bytes 294920 | tf_op jit(solution)/shard_map/ppermute | solution.py:321
  114.3 0.0 collective-permute-done.5
  114.3 0.6 collective-permute-start.8
  114.9 0.0 collective-permute-done.10
  114.9 1.5 %collective-permute-start.9 = (f32[16,1536]{1,0:T(8,128)S(1)}, f32[16,1536]{1,0:T(8,128)S(1)}, u32[]{:S(2)}, u32[]{:S(2)}) collective-permute-start(f32[16,1536]{1,0:T(8,128)S(1)} %get-tuple-element.36), channel_id=1, source_target_pairs={{0,2},{1,3},{2,0},{3,1},{4,6},{5,7},{6,4},{7,5},{8,10},{9,11},{10,... | collective-permute-start | bytes 294920 | tf_op jit(solution)/shard_map/ppermute | solution.py:321
  116.5 0.1 pad_maximum_fusion
  116.6 16.1 %all_to_all.6 = f32[64,1,32]{2,1,0:T(1,128)S(1)} all-to-all(f32[64,1,32]{2,1,0:T(1,128)S(1)} %broadcast_in_dim.29), channel_id=1, replica_groups=mesh['blk'=64,'grp'=2] {'blk'}, dimensions={0} | all-to-all | bytes 16384 | tf_op jit(solution)/shard_map/all_to_all | solution.py:345
  132.6 0.1 reduce_sum.49
  132.7 0.0 collective-permute-done.11
  132.7 0.0 collective-permute-done.6
  132.7 0.0 collective-permute-done.7
  132.7 0.0 collective-permute-done.8
  132.8 0.0 collective-permute-done.9
  132.8 2.2 %collective-permute-start.12 = (f32[32]{0:T(128)S(1)}, f32[32]{0:T(128)S(1)}, u32[]{:S(2)}, u32[]{:S(2)}) collective-permute-start(f32[32]{0:T(128)S(1)} %reduce_sum.49), channel_id=1, source_target_pairs={{0,1},{1,0},{2,3},{3,2},{4,5},{5,4},{6,7},{7,6},{8,9},{9,8},{10,11... | collective-permute-start | bytes 392 | tf_op jit(solution)/shard_map/ppermute | solution.py:355
  135.0 0.1 add_add_fusion
  135.0 0.1 collective-permute-start.13
  135.1 1.4 collective-permute-done.12
  136.5 0.1 slice_divide_fusion
  136.6 3.1 %collective-permute-done.13 = f32[16,1536]{1,0:T(8,128)S(1)} collective-permute-done((f32[16,1536]{1,0:T(8,128)S(1)}, f32[16,1536]{1,0:T(8,128)S(1)}, u32[]{:S(2)}, u32[]{:S(2)}) %collective-permute-start.13) | collective-permute-done | bytes 98336 | tf_op jit(solution)/shard_map/ppermute | solution.py:354
  139.7 0.8 fusion.2
  (10 shorter events, 0.1 us)
Async XLA Ops:
  0.7 7.3 %copy-start.5 = (f32[3]{0:T(128)S(1)}, f32[3]{0:T(128)}, u32[]{:S(2)}) copy-start(f32[3]{0:T(128)} %param.11) | copy-start | bytes 40
  0.7 7.3 %copy-start.3 = (s32[1536]{0:T(1024)S(1)}, s32[1536]{0:T(1024)}, u32[]{:S(2)}) copy-start(s32[1536]{0:T(1024)} %param.13) | copy-start | bytes 18436
  0.7 7.4 %copy-start.2 = (f32[16,1536]{1,0:T(8,128)S(1)}, f32[16,1536]{1,0:T(8,128)}, u32[]{:S(2)}) copy-start(f32[16,1536]{1,0:T(8,128)} %param.10) | copy-start | bytes 294916
  1.8 6.2 %copy-start.4 = (f32[8]{0:T(128)S(1)}, f32[8]{0:T(128)}, u32[]{:S(2)}) copy-start(f32[8]{0:T(128)} %param.12) | copy-start | bytes 100
  1.8 8.5 %collective-permute-start.1 = (f32[24,1536]{1,0:T(8,128)S(1)}, f32[24,1536]{1,0:T(8,128)S(1)}, u32[]{:S(2)}, u32[]{:S(2)}) collective-permute-start(f32[24,1536]{1,0:T(8,128)S(1)} %maximum_maximum_fusion.refs_3_), channel_id=1, source_target_pairs={{0,4},{2,6},{4,0},{6,2},{8,12},{10,14},{12,8},{14,10},{16,20},{18,... | collective-permute-start | bytes 442376 | tf_op jit(solution)/shard_map/ppermute | solution.py:303
  3.4 6.8 %collective-permute-start = (f32[24,1536]{1,0:T(8,128)S(1)}, f32[24,1536]{1,0:T(8,128)S(1)}, u32[]{:S(2)}, u32[]{:S(2)}) collective-permute-start(f32[24,1536]{1,0:T(8,128)S(1)} %maximum_maximum_fusion.refs_3_), channel_id=1, source_target_pairs={{0,2},{2,0},{4,6},{6,4},{8,10},{10,8},{12,14},{14,12},{16,18},{18,... | collective-permute-start | bytes 442376 | tf_op jit(solution)/shard_map/ppermute | solution.py:304
  3.4 11.9 %collective-permute-start.4 = (f32[24,1536]{1,0:T(8,128)S(1)}, f32[24,1536]{1,0:T(8,128)S(1)}, u32[]{:S(2)}, u32[]{:S(2)}) collective-permute-start(f32[24,1536]{1,0:T(8,128)S(1)} %maximum_maximum_fusion.refs_3_), channel_id=1, source_target_pairs={{65,0},{29,1},{50,2},{15,3},{36,4},{57,5},{22,6},{43,7},{73,8},{37... | collective-permute-start | bytes 442376 | tf_op jit(solution)/shard_map/ppermute | solution.py:302
  8.3 0.7 copy-start.6
  10.3 2.7 %collective-permute-start.2 = (f32[24,1536]{1,0:T(8,128)S(1)}, f32[24,1536]{1,0:T(8,128)S(1)}, u32[]{:S(2)}, u32[]{:S(2)}) collective-permute-start(f32[24,1536]{1,0:T(8,128)S(1)} %collective-permute-done.1), channel_id=1, source_target_pairs={{0,2},{2,0},{4,6},{6,4},{8,10},{10,8},{12,14},{14,12},{16,18},{18,... | collective-permute-start | bytes 442376 | tf_op jit(solution)/shard_map/ppermute | solution.py:305
  11.9 3.4 %copy-start.1 = (s32[5,16,3]{2,1,0:T(8,128)S(1)}, s32[5,16,3]{2,1,0:T(8,128)}, u32[]{:S(2)}) copy-start(s32[5,16,3]{2,1,0:T(8,128)} %constant.47.clone.refs_0_) | copy-start | bytes 2884
  13.0 26.1 %copy-start = (s32[5,50,3]{2,1,0:T(8,128)S(1)}, s32[5,50,3]{2,1,0:T(8,128)}, u32[]{:S(2)}) copy-start(s32[5,50,3]{2,1,0:T(8,128)} %constant.49.clone.refs_0_) | copy-start | bytes 9004
  13.0 26.1 %collective-permute-start.3 = (f32[72,1536]{1,0:T(8,128)S(1)}, f32[72,1536]{1,0:T(8,128)S(1)}, u32[]{:S(2)}, u32[]{:S(2)}) collective-permute-start(f32[72,1536]{1,0:T(8,128)S(1)} %constant_dynamic-update-slice_fusion.refs_4_), channel_id=1, source_target_pairs={{65,0},{29,1},{50,2},{15,3},{36,4},{57,5},{22,6},{43,7},{73,8},{37... | collective-permute-start | bytes 1327112 | tf_op jit(solution)/shard_map/ppermute | solution.py:307
  38.0 76.3 %collective-permute-start.5 = (f32[16,1536]{1,0:T(8,128)S(1)}, f32[16,1536]{1,0:T(8,128)S(1)}, u32[]{:S(2)}, u32[]{:S(2)}) collective-permute-start(f32[16,1536]{1,0:T(8,128)S(1)} %get-tuple-element.31), channel_id=1, source_target_pairs={{0,65},{1,29},{2,50},{3,15},{4,36},{5,57},{6,22},{7,43},{8,73},{9,... | collective-permute-start | bytes 294920 | tf_op jit(solution)/shard_map/ppermute | solution.py:321
  101.9 13.0 %collective-permute-start.10 = (f32[16,1536]{1,0:T(8,128)S(1)}, f32[16,1536]{1,0:T(8,128)S(1)}, u32[]{:S(2)}, u32[]{:S(2)}) collective-permute-start(f32[16,1536]{1,0:T(8,128)S(1)} %get-tuple-element.37), channel_id=1, source_target_pairs={{0,4},{1,5},{2,6},{3,7},{4,0},{5,1},{6,2},{7,3},{8,12},{9,13},{10,... | collective-permute-start | bytes 294920 | tf_op jit(solution)/shard_map/ppermute | solution.py:321
  105.0 27.7 %collective-permute-start.11 = (f32[16,1536]{1,0:T(8,128)S(1)}, f32[16,1536]{1,0:T(8,128)S(1)}, u32[]{:S(2)}, u32[]{:S(2)}) collective-permute-start(f32[16,1536]{1,0:T(8,128)S(1)} %get-tuple-element.38), channel_id=1, source_target_pairs={{0,6},{1,7},{2,4},{3,5},{4,2},{5,3},{6,0},{7,1},{8,14},{9,15},{10,... | collective-permute-start | bytes 294920 | tf_op jit(solution)/shard_map/ppermute | solution.py:321
  105.5 27.2 %collective-permute-start.6 = (f32[16,1536]{1,0:T(8,128)S(1)}, f32[16,1536]{1,0:T(8,128)S(1)}, u32[]{:S(2)}, u32[]{:S(2)}) collective-permute-start(f32[16,1536]{1,0:T(8,128)S(1)} %get-tuple-element.33), channel_id=1, source_target_pairs={{0,67},{1,31},{2,48},{3,13},{4,38},{5,59},{6,20},{7,41},{8,75},{9,... | collective-permute-start | bytes 294920 | tf_op jit(solution)/shard_map/ppermute | solution.py:321
  109.1 23.6 %collective-permute-start.7 = (f32[16,1536]{1,0:T(8,128)S(1)}, f32[16,1536]{1,0:T(8,128)S(1)}, u32[]{:S(2)}, u32[]{:S(2)}) collective-permute-start(f32[16,1536]{1,0:T(8,128)S(1)} %get-tuple-element.34), channel_id=1, source_target_pairs={{0,69},{1,25},{2,54},{3,11},{4,32},{5,61},{6,18},{7,47},{8,77},{9,... | collective-permute-start | bytes 294920 | tf_op jit(solution)/shard_map/ppermute | solution.py:321
  114.3 18.4 %collective-permute-start.8 = (f32[16,1536]{1,0:T(8,128)S(1)}, f32[16,1536]{1,0:T(8,128)S(1)}, u32[]{:S(2)}, u32[]{:S(2)}) collective-permute-start(f32[16,1536]{1,0:T(8,128)S(1)} %get-tuple-element.35), channel_id=1, source_target_pairs={{0,71},{1,27},{2,52},{3,9},{4,34},{5,63},{6,16},{7,45},{8,79},{9,3... | collective-permute-start | bytes 294920 | tf_op jit(solution)/shard_map/ppermute | solution.py:321
  114.9 17.8 %collective-permute-start.9 = (f32[16,1536]{1,0:T(8,128)S(1)}, f32[16,1536]{1,0:T(8,128)S(1)}, u32[]{:S(2)}, u32[]{:S(2)}) collective-permute-start(f32[16,1536]{1,0:T(8,128)S(1)} %get-tuple-element.36), channel_id=1, source_target_pairs={{0,2},{1,3},{2,0},{3,1},{4,6},{5,7},{6,4},{7,5},{8,10},{9,11},{10,... | collective-permute-start | bytes 294920 | tf_op jit(solution)/shard_map/ppermute | solution.py:321
  132.8 3.7 %collective-permute-start.12 = (f32[32]{0:T(128)S(1)}, f32[32]{0:T(128)S(1)}, u32[]{:S(2)}, u32[]{:S(2)}) collective-permute-start(f32[32]{0:T(128)S(1)} %reduce_sum.49), channel_id=1, source_target_pairs={{0,1},{1,0},{2,3},{3,2},{4,5},{5,4},{6,7},{7,6},{8,9},{9,8},{10,11... | collective-permute-start | bytes 392 | tf_op jit(solution)/shard_map/ppermute | solution.py:355
  135.0 4.7 %collective-permute-start.13 = (f32[16,1536]{1,0:T(8,128)S(1)}, f32[16,1536]{1,0:T(8,128)S(1)}, u32[]{:S(2)}, u32[]{:S(2)}) collective-permute-start(f32[16,1536]{1,0:T(8,128)S(1)} %add_add_fusion), channel_id=1, source_target_pairs={{0,1},{1,0},{2,3},{3,2},{4,5},{5,4},{6,7},{7,6},{8,9},{9,8},{10,11... | collective-permute-start | bytes 294920 | tf_op jit(solution)/shard_map/ppermute | solution.py:354

commit v6 on v5

--- a/solution.py
+++ b/solution.py
@@ -321,7 +321,6 @@
         return lax.ppermute(sums[name], BOTH, backward(route))
 
     sums, curve = {}, None
-    returned = []
     for call, (held, across, _) in enumerate(CALLS):
         meta = jnp.stack([variant, jnp.asarray(counts[call])[variant]])
         names = [("x", c) for c in held] + [("y", c) for c in across]
@@ -330,8 +329,9 @@
             [columns[c] for c in across], [sums.get(name) for name in names], curve,
         )
         sums.update(zip(names, parts))
-        done = [[("y", 0)], [("y", 1), ("y", 2), ("y", 3), ("x", 1), ("x", 2), ("x", 3)]]
-        returned += [sent_back(name) for name in done[call]]
+
+    column_sums = jnp.concatenate([sums["y", c] for c in range(CHUNKS)], axis=0)
+    column_sums = lax.ppermute(column_sums, BOTH, backward(column_route(0)))
 
     classes = lax.broadcasted_iota(jnp.int32, (noise_levels.shape[0], noise_class.shape[0]), 0)
     noise_diag = jnp.sum(
@@ -340,17 +340,18 @@
     own_noise = noise_diag[None, :] * targets
     norm = 0.5 * jnp.sum(targets * targets, axis=1)
     curvature = jnp.sum(curve, axis=1) + 0.5 * jnp.sum(targets * own_noise, axis=1)
-    scalars = after(jnp.concatenate([norm, curvature]), *returned[:1])
+    scalars = jnp.concatenate([norm, curvature])
     blocks = lax.axis_size("blk")
     scalars = lax.all_to_all(
         jnp.broadcast_to(scalars[None], (blocks, 2 * NVEC)), "blk", 0, 0, tiled=True
     )
     scalars = jnp.sum(scalars, axis=0)
 
-    scalars, *returned = lax.optimization_barrier((scalars, *returned))
-    own = sums["x", 0]
-    for part in returned:
-        own = own + part
+    scalars, column_sums = lax.optimization_barrier((scalars, column_sums))
+    total = [sums["x", c] + column_sums[c * NVEC : (c + 1) * NVEC] for c in range(CHUNKS)]
+    pair = lax.ppermute(jnp.concatenate([total[1], total[3]], axis=0), "blk", swap)
+    near = lax.ppermute(total[2] + pair[NVEC:], "blk", [(i, i ^ 2) for i in range(64)])
+    own = total[0] + pair[:NVEC] + near
     theirs = lax.ppermute(own, "grp", [(0, 1), (1, 0)])
     scalars = scalars + lax.ppermute(scalars, "grp", [(0, 1), (1, 0)])
     step_size = scalars[:NVEC] / scalars[NVEC:]

time: 141 us -> 136 us (0.965)
  starting transfers between devices: 28.1 us -> 16.6 us
  waiting for transfers between devices: 5.53 us -> 9.27 us
  blocking collectives: 16.1 us -> 18.3 us
    ppermute x7 -> x3, starting transfers between devices: 15.5 us -> 4.28 us  [the longest x1 3.54 us: on_device(): column_sums = lax.ppermute(column_sums, BOTH, backward(column_route(0)))]
    all_to_all x1, blocking collectives: 16.1 us -> 18.3 us  [on_device(): lax.all_to_all(jnp.broadcast_to(scalars[None], (blocks, 2 * NVEC)), 'blk'...]
    ppermute x7 -> x3, waiting for transfers between devices: 0.02 us -> 2.15 us  [the longest x1 1.43 us: on_device(): lax.ppermute(jnp.concatenate([total[1], total[3]], axis=0), 'blk', swap)]
  transfers between devices with their start and end apart: 14 -> 10, of which waited for: 3 -> 5; matrix products, arithmetic and copies ran while one was open for 1% -> 1% of each run, Pallas kernels for 61% -> 17%
where the time goes in v6:
time: 136 us; the launch traced here: 135 us
  Pallas kernels  85.3 us (63%)
  blocking collectives  18.3 us (13%)
  starting transfers between devices  16.6 us (12%)
  waiting for transfers between devices  9.27 us (7%)
  other arithmetic  3.15 us (2%)
  local copies, waits for them, and re-layouts  2.05 us (2%)
    pallas_call x2, Pallas kernels, run_tiles(): pl.pallas_call(functools.partial(tile_kernel, len(rows), places, begun),...  85.3 us
    all_to_all x1, blocking collectives, on_device(): lax.all_to_all(jnp.broadcast_to(scalars[None], (blocks, 2 * NVEC)), 'blk'...  18.3 us
    ppermute x1, starting transfers between devices, on_device(): first_column = lax.ppermute(shard, BOTH, column_route(0))  4.55 us
    ppermute x1, waiting for transfers between devices, on_device(): theirs = lax.ppermute(own, 'grp', [(0, 1), (1, 0)])  3.56 us
    ppermute x1, starting transfers between devices, on_device(): column_sums = lax.ppermute(column_sums, BOTH, backward(column_route(0)))  3.54 us
  transfers between devices with their start and end apart: 10, of which 5 were waited for; matrix products, arithmetic and copies ran while one was open for 1% of the time, Pallas kernels for 17%

profile of v6, /device:TPU:0, one launch (start us, length us, event | category | flops | bytes accessed | tf_op | source)
XLA Modules:
  0.0 135.4 jit_solution(5749461227930563508)
XLA Ops:
  0.6 0.1 pad.11.clone
  0.7 1.0 maximum_maximum_fusion.refs_3_
  1.7 1.7 %collective-permute-start.1 = (f32[24,1536]{1,0:T(8,128)S(1)}, f32[24,1536]{1,0:T(8,128)S(1)}, u32[]{:S(2)}, u32[]{:S(2)}) collective-permute-start(f32[24,1536]{1,0:T(8,128)S(1)} %maximum_maximum_fusion.refs_3_), channel_id=1, source_target_pairs={{0,4},{2,6},{4,0},{6,2},{8,12},{10,14},{12,8},{14,10},{16,20},{18,... | collective-permute-start | bytes 442376 | tf_op jit(solution)/shard_map/ppermute | solution.py:303
  3.3 0.0 collective-permute-start
  3.3 4.5 %collective-permute-start.4 = (f32[24,1536]{1,0:T(8,128)S(1)}, f32[24,1536]{1,0:T(8,128)S(1)}, u32[]{:S(2)}, u32[]{:S(2)}) collective-permute-start(f32[24,1536]{1,0:T(8,128)S(1)} %maximum_maximum_fusion.refs_3_), channel_id=1, source_target_pairs={{65,0},{29,1},{50,2},{15,3},{36,4},{57,5},{22,6},{43,7},{73,8},{37... | collective-permute-start | bytes 442376 | tf_op jit(solution)/shard_map/ppermute | solution.py:302
  7.9 0.0 copy-start.5
  7.9 0.0 copy-start.6
  7.9 0.7 copy-done.5
  8.6 0.0 copy-start.3
  8.6 0.0 copy-done.6
  8.6 0.6 dynamic_slice.6
  9.2 0.7 pad_add_fusion.refs_1_
  9.9 0.0 copy-start.4
  9.9 0.0 copy-done.3
  9.9 0.6 copy-done.4
  10.5 0.1 select_reduce_fusion
  10.6 0.0 collective-permute-done
  10.6 0.0 collective-permute-done.1
  10.7 1.7 %collective-permute-start.2 = (f32[24,1536]{1,0:T(8,128)S(1)}, f32[24,1536]{1,0:T(8,128)S(1)}, u32[]{:S(2)}, u32[]{:S(2)}) collective-permute-start(f32[24,1536]{1,0:T(8,128)S(1)} %collective-permute-done.1), channel_id=1, source_target_pairs={{0,2},{2,0},{4,6},{6,4},{8,10},{10,8},{12,14},{14,12},{16,18},{18,... | collective-permute-start | bytes 442376 | tf_op jit(solution)/shard_map/ppermute | solution.py:305
  12.3 0.0 copy-start.1
  12.3 1.0 collective-permute-done.2
  13.3 0.0 copy-start
  13.4 2.4 %collective-permute-start.3 = (f32[72,1536]{1,0:T(8,128)S(1)}, f32[72,1536]{1,0:T(8,128)S(1)}, u32[]{:S(2)}, u32[]{:S(2)}) collective-permute-start(f32[72,1536]{1,0:T(8,128)S(1)} %constant_dynamic-update-slice_fusion.refs_4_), channel_id=1, source_target_pairs={{65,0},{29,1},{50,2},{15,3},{36,4},{57,5},{22,6},{43,7},{73,8},{37... | collective-permute-start | bytes 1327112 | tf_op jit(solution)/shard_map/ppermute | solution.py:307
  15.7 0.0 collective-permute-done.4.refs_5_
  15.7 0.0 copy-done.1
  15.7 22.7 %shard_map.104 = (f32[16,1536]{1,0:T(8,128)S(1)}, f32[16,1536]{1,0:T(8,128)S(1)}, f32[16,1536]{1,0:T(8,128)S(1)}, f32[16,1536]{1,0:T(8,128)S(1)}, f32[16,1536]{1,0:T(8,128)S(1)}, /*index=5*/f32[16,128]{1,0:T(8,128)S(1)}) custom-call(s32[5,16,3]{2,1,0:T(8,128)S(1)} %copy-done.1, s32[2]{0:T(128)S(1)} %pad.refs_1_, f32[3]{0:T(128)S(1)} %broadcast_divide_fusion.refs_2_, ...), custom_call_target="tpu_custom_call" | custom-call | flops 24000000000 | bytes 2000000 | tf_op jit(solution)/shard_map/pallas_call | solution.py:271
  38.4 0.0 collective-permute-done.3.refs_5_
  38.4 0.0 copy-done
  38.4 62.6 %shard_map.105 = (f32[16,1536]{1,0:T(8,128)S(1)}, f32[16,1536]{1,0:T(8,128)S(1)}, f32[16,1536]{1,0:T(8,128)S(1)}, f32[16,1536]{1,0:T(8,128)S(1)}, f32[16,1536]{1...) custom-call(s32[5,50,3]{2,1,0:T(8,128)S(1)} %copy-done, ...), custom_call_target="tpu_custom_call" | custom-call | flops 74999996416 | bytes 2000000 | tf_op jit(solution)/shard_map/pallas_call | solution.py:271
  101.1 0.0 copy-start.2
  101.1 3.5 %collective-permute-start.5 = (f32[64,1536]{1,0:T(8,128)S(1)}, f32[64,1536]{1,0:T(8,128)S(1)}, u32[]{:S(2)}, u32[]{:S(2)}) collective-permute-start(f32[64,1536]{1,0:T(8,128)S(1)} %pad_maximum_fusion), channel_id=1, source_target_pairs={{0,65},{1,29},{2,50},{3,15},{4,36},{5,57},{6,22},{7,43},{8,73},{9,... | collective-permute-start | bytes 1179656 | tf_op jit(solution)/shard_map/ppermute | solution.py:334
  104.7 0.0 copy-done.2
  104.7 0.1 multiply_reduce_fusion
  104.8 0.1 reduce_sum.46
  104.9 0.1 pad_maximum_fusion.2
  105.0 18.3 %all_to_all.6 = f32[64,1,32]{2,1,0:T(1,128)S(1)} all-to-all(f32[64,1,32]{2,1,0:T(1,128)S(1)} %broadcast_in_dim.29), channel_id=1, replica_groups=mesh['blk'=64,'grp'=2] {'blk'}, dimensions={0} | all-to-all | bytes 16384 | tf_op jit(solution)/shard_map/all_to_all | solution.py:345
  123.3 0.1 reduce_sum.49
  123.4 0.0 collective-permute-done.5
  123.5 0.1 collective-permute-start.7
  123.6 1.4 %collective-permute-done.7 = f32[32,1536]{1,0:T(8,128)S(1)} collective-permute-done((f32[32,1536]{1,0:T(8,128)S(1)}, f32[32,1536]{1,0:T(8,128)S(1)}, u32[]{:S(2)}, u32[]{:S(2)}) %collective-permute-start.7) | collective-permute-done | bytes 196640 | tf_op jit(solution)/shard_map/ppermute | solution.py:352
  125.0 0.7 collective-permute-start.8
  125.7 1.0 collective-permute-start.6
  126.7 2.6 %collective-permute-done.6 = f32[32]{0:T(128)S(1)} collective-permute-done((f32[32]{0:T(128)S(1)}, f32[32]{0:T(128)S(1)}, u32[]{:S(2)}, u32[]{:S(2)}) %collective-permute-start.6) | collective-permute-done | bytes 160 | tf_op jit(solution)/shard_map/ppermute | solution.py:356
  129.2 0.7 collective-permute-done.8
  130.0 1.1 collective-permute-start.9
  131.0 0.1 slice_divide_fusion
  131.1 3.6 %collective-permute-done.9 = f32[16,1536]{1,0:T(8,128)S(1)} collective-permute-done((f32[16,1536]{1,0:T(8,128)S(1)}, f32[16,1536]{1,0:T(8,128)S(1)}, u32[]{:S(2)}, u32[]{:S(2)}) %collective-permute-start.9) | collective-permute-done | bytes 98336 | tf_op jit(solution)/shard_map/ppermute | solution.py:355
  134.7 0.8 fusion.2
  (14 shorter events, 0.2 us)
Async XLA Ops:
  1.7 9.0 %collective-permute-start.1 = (f32[24,1536]{1,0:T(8,128)S(1)}, f32[24,1536]{1,0:T(8,128)S(1)}, u32[]{:S(2)}, u32[]{:S(2)}) collective-permute-start(f32[24,1536]{1,0:T(8,128)S(1)} %maximum_maximum_fusion.refs_3_), channel_id=1, source_target_pairs={{0,4},{2,6},{4,0},{6,2},{8,12},{10,14},{12,8},{14,10},{16,20},{18,... | collective-permute-start | bytes 442376 | tf_op jit(solution)/shard_map/ppermute | solution.py:303
  3.3 7.3 %collective-permute-start = (f32[24,1536]{1,0:T(8,128)S(1)}, f32[24,1536]{1,0:T(8,128)S(1)}, u32[]{:S(2)}, u32[]{:S(2)}) collective-permute-start(f32[24,1536]{1,0:T(8,128)S(1)} %maximum_maximum_fusion.refs_3_), channel_id=1, source_target_pairs={{0,2},{2,0},{4,6},{6,4},{8,10},{10,8},{12,14},{14,12},{16,18},{18,... | collective-permute-start | bytes 442376 | tf_op jit(solution)/shard_map/ppermute | solution.py:304
  3.3 12.4 %collective-permute-start.4 = (f32[24,1536]{1,0:T(8,128)S(1)}, f32[24,1536]{1,0:T(8,128)S(1)}, u32[]{:S(2)}, u32[]{:S(2)}) collective-permute-start(f32[24,1536]{1,0:T(8,128)S(1)} %maximum_maximum_fusion.refs_3_), channel_id=1, source_target_pairs={{65,0},{29,1},{50,2},{15,3},{36,4},{57,5},{22,6},{43,7},{73,8},{37... | collective-permute-start | bytes 442376 | tf_op jit(solution)/shard_map/ppermute | solution.py:302
  7.9 0.7 copy-start.5
  7.9 0.7 copy-start.6
  8.6 1.3 copy-start.3
  9.9 0.7 copy-start.4
  10.7 2.7 %collective-permute-start.2 = (f32[24,1536]{1,0:T(8,128)S(1)}, f32[24,1536]{1,0:T(8,128)S(1)}, u32[]{:S(2)}, u32[]{:S(2)}) collective-permute-start(f32[24,1536]{1,0:T(8,128)S(1)} %collective-permute-done.1), channel_id=1, source_target_pairs={{0,2},{2,0},{4,6},{6,4},{8,10},{10,8},{12,14},{14,12},{16,18},{18,... | collective-permute-start | bytes 442376 | tf_op jit(solution)/shard_map/ppermute | solution.py:305
  12.3 3.4 %copy-start.1 = (s32[5,16,3]{2,1,0:T(8,128)S(1)}, s32[5,16,3]{2,1,0:T(8,128)}, u32[]{:S(2)}) copy-start(s32[5,16,3]{2,1,0:T(8,128)} %constant.47.clone.refs_0_) | copy-start | bytes 2884
  13.3 25.1 %copy-start = (s32[5,50,3]{2,1,0:T(8,128)S(1)}, s32[5,50,3]{2,1,0:T(8,128)}, u32[]{:S(2)}) copy-start(s32[5,50,3]{2,1,0:T(8,128)} %constant.49.clone.refs_0_) | copy-start | bytes 9004
  13.4 25.1 %collective-permute-start.3 = (f32[72,1536]{1,0:T(8,128)S(1)}, f32[72,1536]{1,0:T(8,128)S(1)}, u32[]{:S(2)}, u32[]{:S(2)}) collective-permute-start(f32[72,1536]{1,0:T(8,128)S(1)} %constant_dynamic-update-slice_fusion.refs_4_), channel_id=1, source_target_pairs={{65,0},{29,1},{50,2},{15,3},{36,4},{57,5},{22,6},{43,7},{73,8},{37... | collective-permute-start | bytes 1327112 | tf_op jit(solution)/shard_map/ppermute | solution.py:307
  101.1 3.6 %copy-start.2 = (f32[16,1536]{1,0:T(8,128)S(1)}, f32[16,1536]{1,0:T(8,128)}, u32[]{:S(2)}) copy-start(f32[16,1536]{1,0:T(8,128)} %param.10) | copy-start | bytes 294916
  101.1 22.3 %collective-permute-start.5 = (f32[64,1536]{1,0:T(8,128)S(1)}, f32[64,1536]{1,0:T(8,128)S(1)}, u32[]{:S(2)}, u32[]{:S(2)}) collective-permute-start(f32[64,1536]{1,0:T(8,128)S(1)} %pad_maximum_fusion), channel_id=1, source_target_pairs={{0,65},{1,29},{2,50},{3,15},{4,36},{5,57},{6,22},{7,43},{8,73},{9,... | collective-permute-start | bytes 1179656 | tf_op jit(solution)/shard_map/ppermute | solution.py:334
  123.5 1.5 %collective-permute-start.7 = (f32[32,1536]{1,0:T(8,128)S(1)}, f32[32,1536]{1,0:T(8,128)S(1)}, u32[]{:S(2)}, u32[]{:S(2)}) collective-permute-start(f32[32,1536]{1,0:T(8,128)S(1)} %pad_maximum_fusion.1), channel_id=1, source_target_pairs={{0,2},{2,0},{4,6},{6,4},{8,10},{10,8},{12,14},{14,12},{16,18},{18,... | collective-permute-start | bytes 589832 | tf_op jit(solution)/shard_map/ppermute | solution.py:352
  125.0 4.9 %collective-permute-start.8 = (f32[16,1536]{1,0:T(8,128)S(1)}, f32[16,1536]{1,0:T(8,128)S(1)}, u32[]{:S(2)}, u32[]{:S(2)}) collective-permute-start(f32[16,1536]{1,0:T(8,128)S(1)} %slice_add_fusion), channel_id=1, source_target_pairs={{0,4},{2,6},{4,0},{6,2},{8,12},{10,14},{12,8},{14,10},{16,20},{18,... | collective-permute-start | bytes 294920 | tf_op jit(solution)/shard_map/ppermute | solution.py:353
  125.7 3.5 %collective-permute-start.6 = (f32[32]{0:T(128)S(1)}, f32[32]{0:T(128)S(1)}, u32[]{:S(2)}, u32[]{:S(2)}) collective-permute-start(f32[32]{0:T(128)S(1)} %reduce_sum.49), channel_id=1, source_target_pairs={{0,1},{1,0},{2,3},{3,2},{4,5},{5,4},{6,7},{7,6},{8,9},{9,8},{10,11... | collective-permute-start | bytes 392 | tf_op jit(solution)/shard_map/ppermute | solution.py:356
  130.0 4.7 %collective-permute-start.9 = (f32[16,1536]{1,0:T(8,128)S(1)}, f32[16,1536]{1,0:T(8,128)S(1)}, u32[]{:S(2)}, u32[]{:S(2)}) collective-permute-start(f32[16,1536]{1,0:T(8,128)S(1)} %fusion.3), channel_id=1, source_target_pairs={{0,1},{1,0},{2,3},{3,2},{4,5},{5,4},{6,7},{7,6},{8,9},{9,8},{10,11... | collective-permute-start | bytes 294920 | tf_op jit(solution)/shard_map/ppermute | solution.py:355

commit v7 on v6

--- a/solution.py
+++ b/solution.py
@@ -16,8 +16,10 @@
 SUPER = SHARD * CHUNKS
 NSUPER = 16
 NVEC = 16
-TILE = 768
+TALL = 768
+WIDE = 512
 SUB = 256
+UNROLL = 8
 LOG2E = math.log2(math.e)
 SHIFT = 1.5 * LOG2E
 OFFSET = 0.75 * LOG2E * LOG2E
@@ -71,53 +73,48 @@
 ]
 OFF = [(1, 0), (2, 1), (3, 1), (0, 2), (0, 3), (2, 3)]
 ON = [[(0, 0), (1, 1)], [(2, 2), (3, 3)]]
-FILL = [[8, 24], [12, 20]]
-PER = SHARD // TILE
-GIVEN = [(0, 3 * PER), (1, 3 * PER), (0, 3 * PER + 1), (1, 3 * PER + 1)]
+WITHIN = [(i, j) for j in range(CHUNKS) for i in range(j + 1) if (i, j) not in ((0, 2), (0, 3))]
+GIVEN = [(0, 2), (0, 3)]
+DOWN, ALONG = SHARD // TALL, SHARD // WIDE
 
 
 def tile_tables():
-    side = SUPER // TILE
-    triangles = [
-        [(i, j) for j in range(side) for i in range(j + 1) if (i, j) not in GIVEN] for _ in range(2)
-    ]
-    tables, counts = [], []
+    within = [[(i, j, y, x) for i, j in WITHIN for y in range(DOWN) for x in range(ALONG)]] * 2
+    tables = []
     for call, (held, columns, pairs) in enumerate(CALLS):
 
-        def at(i, k=0):
-            return held.index((i // PER) ^ k) * PER + i % PER
+        def tile(i, j, y, x, keep=1):
+            return ((held.index(i) * DOWN + y) * TALL, (j * ALONG + x) * WIDE, keep)
 
         def pair(i, j):
-            first = (len(held) + columns.index(j)) * PER
-            return [(at(i * PER + y), first + x, 1) for y in range(PER) for x in range(PER)]
+            first = len(held) + columns.index(j)
+            return [tile(i, first, y, x) for y in range(DOWN) for x in range(ALONG)]
 
         regular = [t for i, j in pairs for t in pair(i, j)]
         lists = [regular]
         for half in range(2):
             tiles = [t for i, j in OFF + ON[half] if (i, j) in pairs for t in pair(i, j)]
-            fits = [t for t in triangles[half] if all(i // PER in held for i in t)]
-            part = fits[: FILL[half][call]]
-            assert len(part) == FILL[half][call]
-            triangles[half] = [t for t in triangles[half] if t not in part]
-            tiles += [(at(i), at(j), int(i != j)) for i, j in part]
-            lists.append(tiles)
-        given = GIVEN if call == 1 else []
-        lists.append(regular + [(at(i), at(j), 1) for i, j in given[:2]])
-        lists.append(regular + [(at(i, 1), at(j, 1), 1) for i, j in given[2:]])
+            fill = len(regular) - len(tiles)
+            part, within[half] = within[half][:fill], within[half][fill:]
+            lists.append(tiles + [tile(i, held.index(j), y, x, int(i != j)) for i, j, y, x in part])
+        given = [(i, j, y, x) for i, j in GIVEN for y in range(DOWN) for x in range(ALONG)]
+        for m in range(1, 7):
+            k = m // 2
+            part = given[2 * m - 2 : 2 * m] if call == 1 else []
+            lists.append(regular + [tile(i ^ k, held.index(j ^ k), y, x) for i, j, y, x in part])
+        assert all(len(x) % 2 == 0 for x in lists)
         longest = max(len(x) for x in lists)
-        counts.append(np.array([len(x) for x in lists], np.int32))
-        assert all(len(x) % 2 == 0 for x in lists)
         tables.append(
             np.array(
                 [
-                    [(i * TILE, j * TILE, k) for i, j, k in x + x[:1] * (longest - len(x))]
+                    [v for t in x + x[:1] * (longest - len(x)) for v in t] + [len(x)]
                     for x in lists
                 ],
                 np.int32,
             )
         )
-    assert triangles == [[], []]
-    return tables, counts
+    assert within == [[], []]
+    return tables
 
 
 def pieces(value, count, dtype=bf16):
@@ -137,11 +134,11 @@
 
 def tile_kernel(x_count, places, begun, *refs):
     refs = list(refs)
-    table, meta, scale = refs[:3]
+    table, scale = refs[:2]
     every = len(places)
     given = 1 + max(array for array, _ in places)
-    chunks = [refs[3 + array].at[pl.ds(ROWS * i, ROWS)] for array, i in places]
-    rest = refs[3 + given :]
+    chunks = [refs[2 + array].at[pl.ds(ROWS * i, ROWS)] for array, i in places]
+    rest = refs[2 + given :]
     sums_in, rest = dict(zip(begun, rest)), rest[len(begun) :]
     if begun:
         curve_in, rest = rest[0], rest[1:]
@@ -179,14 +176,13 @@
             row_feat[span, :] = jnp.transpose(rows).astype(bf16)
     for ref in (row_sum, col_sum, hi1, lo1):
         ref[...] = jnp.zeros_like(ref)
-    variant = meta[0]
-    count = meta[1]
+    count = table[table.shape[0] - 1]
 
     def place_of(t):
         return (
-            pl.multiple_of(table[variant, t, 0], TILE),
-            pl.multiple_of(table[variant, t, 1], TILE),
-            table[variant, t, 2],
+            pl.multiple_of(table[3 * t], TALL),
+            pl.multiple_of(table[3 * t + 1], WIDE),
+            table[3 * t + 2],
         )
 
     def produce(place, hi, lo, x, y):
@@ -198,42 +194,47 @@
         hi[y : y + SUB, x : x + SUB] = high
         lo[y : y + SUB, x : x + SUB] = (value - high.astype(f32)).astype(f8)
 
-    def consume_rows(place, hi, lo, y):
+    def consume_rows(place, part, held, y):
         row, col, _ = place
         across = (((1,), (1,)), ((), ()))
-        far = pl.ds(col, TILE)
-        high, low = hi[y : y + SUB, :], lo[y : y + SUB, :]
-        part = lax.dot_general(vectors[:, far], high, across, preferred_element_type=f32)
-        part = part + lax.dot_general(vectors8[:, far], low, across, preferred_element_type=f32)
-        row_sum[:, pl.ds(pl.multiple_of(row + y, SUB), SUB)] += part
-
-    def consume_columns(place, hi, lo, x):
+        far = held[:, pl.ds(col, WIDE)]
+        row_sum[:, pl.ds(pl.multiple_of(row + y, SUB), SUB)] += lax.dot_general(
+            far, part[y : y + SUB, :], across, preferred_element_type=f32
+        )
+
+    def consume_columns(place, part, held, x):
         row, col, keep = place
-        near = pl.ds(row, TILE)
-        high, low = hi[:, x : x + SUB], lo[:, x : x + SUB]
-        part = jnp.dot(vectors[:, near], high, preferred_element_type=f32)
-        part = part + jnp.dot(vectors8[:, near], low, preferred_element_type=f32)
-        col_sum[:, pl.ds(pl.multiple_of(col + x, SUB), SUB)] += part * keep.astype(f32)
+        near = held[:, pl.ds(row, TALL)]
+        total = jnp.dot(near, part[:, x : x + SUB], preferred_element_type=f32)
+        col_sum[:, pl.ds(pl.multiple_of(col + x, SUB), SUB)] += total * keep.astype(f32)
 
     def both(ahead, ahead_hi, ahead_lo, now, hi, lo):
-        subs = [(x, y) for x in range(0, TILE, SUB) for y in range(0, TILE, SUB)]
-        work = [(consume_rows, y) for y in range(0, TILE, SUB)]
-        work += [(consume_columns, x) for x in range(0, TILE, SUB)]
+        subs = [(x, y) for x in range(0, WIDE, SUB) for y in range(0, TALL, SUB)]
+        sides = ((hi, vectors), (lo, vectors8))
+        work = [(consume_rows, *side, y) for y in range(0, TALL, SUB) for side in sides]
+        work += [(consume_columns, *side, x) for x in range(0, WIDE, SUB) for side in sides]
         done = 0
         for n, (x, y) in enumerate(subs):
             if ahead is not None:
                 produce(ahead, ahead_hi, ahead_lo, x, y)
             while done * len(subs) < (n + 1) * len(work) and done < len(work):
-                step, offset = work[done]
-                step(now, hi, lo, offset)
+                step, part, held, offset = work[done]
+                step(now, part, held, offset)
                 done += 1
 
-    def two_tiles(u, carried):
-        both(place_of(2 * u), hi0, lo0, place_of(jnp.maximum(2 * u - 1, 0)), hi1, lo1)
-        both(place_of(2 * u + 1), hi1, lo1, place_of(2 * u), hi0, lo0)
-        return carried
-
-    lax.fori_loop(0, count // 2, two_tiles, 0)
+    def two_tiles(t):
+        both(place_of(t), hi0, lo0, place_of(jnp.maximum(t - 1, 0)), hi1, lo1)
+        both(place_of(t + 1), hi1, lo1, place_of(t), hi0, lo0)
+
+    @pl.loop(0, count // UNROLL)
+    def _(u):
+        for t in range(0, UNROLL, 2):
+            two_tiles(UNROLL * u + t)
+
+    @pl.loop(0, count % UNROLL // 2)
+    def _(u):
+        two_tiles(count // UNROLL * UNROLL + 2 * u)
+
     both(None, None, None, place_of(count - 1), hi1, lo1)
 
     curve = curve_in[...] if begun else jnp.zeros((NVEC, 128), f32)
@@ -252,7 +253,7 @@
     curve_out[...] = curve
 
 
-def run_tiles(table, meta, scale, rows, columns, sums, curve):
+def run_tiles(table, scale, rows, columns, sums, curve):
     vmem = pl.BlockSpec(memory_space=pltpu.VMEM)
     smem = pl.BlockSpec(memory_space=pltpu.SMEM)
     count = len(rows) + len(columns)
@@ -272,7 +273,7 @@
         functools.partial(tile_kernel, len(rows), places, begun),
         out_shape=[jax.ShapeDtypeStruct((NVEC, SHARD), f32)] * count
         + [jax.ShapeDtypeStruct((NVEC, 128), f32)],
-        in_specs=[smem] * 3 + [vmem] * len(passed),
+        in_specs=[smem] * 2 + [vmem] * len(passed),
         out_specs=[vmem] * (count + 1),
         scratch_shapes=[
             pltpu.VMEM((wide, 32), bf16),
@@ -282,13 +283,13 @@
             pltpu.VMEM((32, wide), f32),
             pltpu.VMEM((32, every), f32),
         ]
-        + [pltpu.VMEM((TILE, TILE), bf16)] * 2
-        + [pltpu.VMEM((TILE, TILE), f8)] * 2,
+        + [pltpu.VMEM((TALL, WIDE), bf16)] * 2
+        + [pltpu.VMEM((TALL, WIDE), f8)] * 2,
         compiler_params=pltpu.CompilerParams(vmem_limit_bytes=48 * 2**20),
         cost_estimate=pl.CostEstimate(
-            flops=1_500_000_000 * table.shape[1], bytes_accessed=2_000_000, transcendentals=0
+            flops=330_000_000 * table.shape[0], bytes_accessed=2_000_000, transcendentals=0
         ),
-    )(table, meta, scale, *passed)
+    )(table, scale, *passed)
     return out[:count], out[count]
 
 
@@ -310,9 +311,8 @@
 
     block = lax.axis_index("blk")
     member = (block % CHUNKS) * 2 + lax.axis_index("grp")
-    variant = jnp.where(member == 0, jnp.where(block < 32, 1, 2), 0)
-    variant = jnp.where(member == 1, 3, jnp.where(member == 2, 4, variant)).astype(jnp.int32)
-    tables, counts = tile_tables()
+    variant = jnp.where(member == 0, jnp.where(block < 32, 1, 2), (member + 2) % 9)
+    tables = tile_tables()
     scale = (math.sqrt(5.0) * LOG2E) / length_scales
 
     def sent_back(name):
@@ -322,10 +322,9 @@
 
     sums, curve = {}, None
     for call, (held, across, _) in enumerate(CALLS):
-        meta = jnp.stack([variant, jnp.asarray(counts[call])[variant]])
         names = [("x", c) for c in held] + [("y", c) for c in across]
         parts, curve = run_tiles(
-            jnp.asarray(tables[call]), meta, scale, [rows[c] for c in held],
+            jnp.asarray(tables[call])[variant], scale, [rows[c] for c in held],
             [columns[c] for c in across], [sums.get(name) for name in names], curve,
         )
         sums.update(zip(names, parts))

time: 136 us -> 126 us (0.926)
  Pallas kernels: 85.3 us -> 76.4 us
    pallas_call x2, Pallas kernels: 85.3 us -> 76.4 us  [run_tiles(): pl.pallas_call(functools.partial(tile_kernel, len(rows), places, begun),...]
  transfers between devices with their start and end apart: 10 -> 10, of which waited for: 5 -> 5; matrix products, arithmetic and copies ran while one was open for 1% -> 2% of each run, Pallas kernels for 17% -> 16%
where the time goes in v7:
time: 126 us
  Pallas kernels  76.4 us (61%)
  blocking collectives  19.2 us (15%)
  starting transfers between devices  16.7 us (13%)
  waiting for transfers between devices  8.14 us (6%)
  other arithmetic  2.43 us (2%)
  local copies, waits for them, and re-layouts  2.21 us (2%)
    pallas_call x2, Pallas kernels, run_tiles(): pl.pallas_call(functools.partial(tile_kernel, len(rows), places, begun),...  76.4 us
    all_to_all x1, blocking collectives, on_device(): lax.all_to_all(jnp.broadcast_to(scalars[None], (blocks, 2 * NVEC)), 'blk'...  19.2 us
    ppermute x1, starting transfers between devices, on_device(): first_column = lax.ppermute(shard, BOTH, column_route(0))  4.55 us
    ppermute x1, waiting for transfers between devices, on_device(): theirs = lax.ppermute(own, 'grp', [(0, 1), (1, 0)])  3 us
    ppermute x1, starting transfers between devices, on_device(): column_sums = lax.ppermute(column_sums, BOTH, backward(column_route(0)))  2.52 us
  transfers between devices with their start and end apart: 10, of which 5 were waited for; matrix products, arithmetic and copies ran while one was open for 2% of the time, Pallas kernels for 16%

profile of v7, /device:TPU:0, one launch (start us, length us, event | category | flops | bytes accessed | tf_op | source)
XLA Modules:
  0.0 125.9 jit_solution(15860219662190150725)
XLA Ops:
  0.6 0.1 pad.10.clone
  0.7 1.0 maximum_maximum_fusion.refs_2_
  1.7 1.7 %collective-permute-start.1 = (f32[24,1536]{1,0:T(8,128)S(1)}, f32[24,1536]{1,0:T(8,128)S(1)}, u32[]{:S(2)}, u32[]{:S(2)}) collective-permute-start(f32[24,1536]{1,0:T(8,128)S(1)} %maximum_maximum_fusion.refs_2_), channel_id=1, source_target_pairs={{0,4},{2,6},{4,0},{6,2},{8,12},{10,14},{12,8},{14,10},{16,20},{18,... | collective-permute-start | bytes 442376 | tf_op jit(solution)/shard_map/ppermute | solution.py:304
  3.3 0.0 collective-permute-start
  3.3 4.5 %collective-permute-start.4 = (f32[24,1536]{1,0:T(8,128)S(1)}, f32[24,1536]{1,0:T(8,128)S(1)}, u32[]{:S(2)}, u32[]{:S(2)}) collective-permute-start(f32[24,1536]{1,0:T(8,128)S(1)} %maximum_maximum_fusion.refs_2_), channel_id=1, source_target_pairs={{65,0},{29,1},{50,2},{15,3},{36,4},{57,5},{22,6},{43,7},{73,8},{37... | collective-permute-start | bytes 442376 | tf_op jit(solution)/shard_map/ppermute | solution.py:303
  7.9 0.0 copy-start.3
  7.9 0.0 copy-start.1
  7.9 0.7 copy-done.3
  8.6 0.7 constant_dynamic-slice_fusion
  9.3 0.0 copy-start.2
  9.3 0.7 dynamic-slice_bitcast_fusion.refs_0_
  10.0 0.0 copy-done.1
  10.0 0.0 copy-done.2
  10.0 0.1 select_reduce_fusion
  10.1 0.0 collective-permute-done
  10.1 0.0 collective-permute-done.1
  10.1 1.7 %collective-permute-start.2 = (f32[24,1536]{1,0:T(8,128)S(1)}, f32[24,1536]{1,0:T(8,128)S(1)}, u32[]{:S(2)}, u32[]{:S(2)}) collective-permute-start(f32[24,1536]{1,0:T(8,128)S(1)} %collective-permute-done.1), channel_id=1, source_target_pairs={{0,2},{2,0},{4,6},{6,4},{8,10},{10,8},{12,14},{14,12},{16,18},{18,... | collective-permute-start | bytes 442376 | tf_op jit(solution)/shard_map/ppermute | solution.py:306
  11.8 1.0 collective-permute-done.2
  12.8 2.4 %collective-permute-start.3 = (f32[72,1536]{1,0:T(8,128)S(1)}, f32[72,1536]{1,0:T(8,128)S(1)}, u32[]{:S(2)}, u32[]{:S(2)}) collective-permute-start(f32[72,1536]{1,0:T(8,128)S(1)} %constant_dynamic-update-slice_fusion.refs_3_), channel_id=1, source_target_pairs={{65,0},{29,1},{50,2},{15,3},{36,4},{57,5},{22,6},{43,7},{73,8},{37... | collective-permute-start | bytes 1327112 | tf_op jit(solution)/shard_map/ppermute | solution.py:308
  15.2 0.0 collective-permute-done.4.refs_4_
  15.2 20.5 %shard_map.86 = (f32[16,1536]{1,0:T(8,128)S(1)}, f32[16,1536]{1,0:T(8,128)S(1)}, f32[16,1536]{1,0:T(8,128)S(1)}, f32[16,1536]{1,0:T(8,128)S(1)}, f32[16,1536]{1,0:T(8,128)S(1)}, /*index=5*/f32[16,128]{1,0:T(8,128)S(1)}) custom-call(s32[73]{0:T(128)S(1)} %dynamic-slice_bitcast_fusion.refs_0_, f32[3]{0:T(128)S(1)} %broadcast_divide_fusion.refs_1_, ...), custom_call_target="tpu_custom_call" | custom-call | flops 24089999360 | bytes 2000000 | tf_op jit(solution)/shard_map/pallas_call | solution.py:272
  35.7 0.0 collective-permute-done.3.refs_4_
  35.7 55.9 %shard_map.87 = (f32[16,1536]{1,0:T(8,128)S(1)}, f32[16,1536]{1,0:T(8,128)S(1)}, f32[16,1536]{1,0:T(8,128)S(1)}, f32[16,1536]{1,0:T(8,128)S(1)}, f32[16,1536]{1,...) custom-call(s32[223]{0:T(256)S(1)} %bitcast.3, ...), custom_call_target="tpu_custom_call" | custom-call | flops 73589997568 | bytes 2000000 | tf_op jit(solution)/shard_map/pallas_call | solution.py:272
  91.6 0.0 copy-start
  91.7 2.5 %collective-permute-start.5 = (f32[64,1536]{1,0:T(8,128)S(1)}, f32[64,1536]{1,0:T(8,128)S(1)}, u32[]{:S(2)}, u32[]{:S(2)}) collective-permute-start(f32[64,1536]{1,0:T(8,128)S(1)} %pad_maximum_fusion), channel_id=1, source_target_pairs={{0,65},{1,29},{2,50},{3,15},{4,36},{5,57},{6,22},{7,43},{8,73},{9,... | collective-permute-start | bytes 1179656 | tf_op jit(solution)/shard_map/ppermute | solution.py:333
  94.2 0.0 copy-done
  94.2 0.1 multiply_reduce_fusion
  94.4 0.1 reduce_sum.46
  94.5 0.1 pad_maximum_fusion.2
  94.6 19.2 %all_to_all.6 = f32[64,1,32]{2,1,0:T(1,128)S(1)} all-to-all(f32[64,1,32]{2,1,0:T(1,128)S(1)} %broadcast_in_dim.29), channel_id=1, replica_groups=mesh['blk'=64,'grp'=2] {'blk'}, dimensions={0} | all-to-all | bytes 16384 | tf_op jit(solution)/shard_map/all_to_all | solution.py:344
  113.8 0.1 reduce_sum.49
  113.9 0.0 collective-permute-done.5
  114.0 0.1 collective-permute-start.7
  114.1 1.4 %collective-permute-done.7 = f32[32,1536]{1,0:T(8,128)S(1)} collective-permute-done((f32[32,1536]{1,0:T(8,128)S(1)}, f32[32,1536]{1,0:T(8,128)S(1)}, u32[]{:S(2)}, u32[]{:S(2)}) %collective-permute-start.7) | collective-permute-done | bytes 196640 | tf_op jit(solution)/shard_map/ppermute | solution.py:351
  115.5 0.7 collective-permute-start.8
  116.2 1.5 %collective-permute-start.6 = (f32[32]{0:T(128)S(1)}, f32[32]{0:T(128)S(1)}, u32[]{:S(2)}, u32[]{:S(2)}) collective-permute-start(f32[32]{0:T(128)S(1)} %reduce_sum.49), channel_id=1, source_target_pairs={{0,1},{1,0},{2,3},{3,2},{4,5},{5,4},{6,7},{7,6},{8,9},{9,8},{10,11... | collective-permute-start | bytes 392 | tf_op jit(solution)/shard_map/ppermute | solution.py:355
  117.7 2.0 %collective-permute-done.6 = f32[32]{0:T(128)S(1)} collective-permute-done((f32[32]{0:T(128)S(1)}, f32[32]{0:T(128)S(1)}, u32[]{:S(2)}, u32[]{:S(2)}) %collective-permute-start.6) | collective-permute-done | bytes 160 | tf_op jit(solution)/shard_map/ppermute | solution.py:355
  119.7 0.7 collective-permute-done.8
  120.5 1.6 %collective-permute-start.9 = (f32[16,1536]{1,0:T(8,128)S(1)}, f32[16,1536]{1,0:T(8,128)S(1)}, u32[]{:S(2)}, u32[]{:S(2)}) collective-permute-start(f32[16,1536]{1,0:T(8,128)S(1)} %fusion.3), channel_id=1, source_target_pairs={{0,1},{1,0},{2,3},{3,2},{4,5},{5,4},{6,7},{7,6},{8,9},{9,8},{10,11... | collective-permute-start | bytes 294920 | tf_op jit(solution)/shard_map/ppermute | solution.py:354
  122.1 0.1 slice_divide_fusion
  122.2 3.0 %collective-permute-done.9 = f32[16,1536]{1,0:T(8,128)S(1)} collective-permute-done((f32[16,1536]{1,0:T(8,128)S(1)}, f32[16,1536]{1,0:T(8,128)S(1)}, u32[]{:S(2)}, u32[]{:S(2)}) %collective-permute-start.9) | collective-permute-done | bytes 98336 | tf_op jit(solution)/shard_map/ppermute | solution.py:354
  125.2 0.8 fusion.2
  (13 shorter events, 0.2 us)
Async XLA Ops:
  1.7 8.4 %collective-permute-start.1 = (f32[24,1536]{1,0:T(8,128)S(1)}, f32[24,1536]{1,0:T(8,128)S(1)}, u32[]{:S(2)}, u32[]{:S(2)}) collective-permute-start(f32[24,1536]{1,0:T(8,128)S(1)} %maximum_maximum_fusion.refs_2_), channel_id=1, source_target_pairs={{0,4},{2,6},{4,0},{6,2},{8,12},{10,14},{12,8},{14,10},{16,20},{18,... | collective-permute-start | bytes 442376 | tf_op jit(solution)/shard_map/ppermute | solution.py:304
  3.3 6.7 %collective-permute-start = (f32[24,1536]{1,0:T(8,128)S(1)}, f32[24,1536]{1,0:T(8,128)S(1)}, u32[]{:S(2)}, u32[]{:S(2)}) collective-permute-start(f32[24,1536]{1,0:T(8,128)S(1)} %maximum_maximum_fusion.refs_2_), channel_id=1, source_target_pairs={{0,2},{2,0},{4,6},{6,4},{8,10},{10,8},{12,14},{14,12},{16,18},{18,... | collective-permute-start | bytes 442376 | tf_op jit(solution)/shard_map/ppermute | solution.py:305
  3.3 11.8 %collective-permute-start.4 = (f32[24,1536]{1,0:T(8,128)S(1)}, f32[24,1536]{1,0:T(8,128)S(1)}, u32[]{:S(2)}, u32[]{:S(2)}) collective-permute-start(f32[24,1536]{1,0:T(8,128)S(1)} %maximum_maximum_fusion.refs_2_), channel_id=1, source_target_pairs={{65,0},{29,1},{50,2},{15,3},{36,4},{57,5},{22,6},{43,7},{73,8},{37... | collective-permute-start | bytes 442376 | tf_op jit(solution)/shard_map/ppermute | solution.py:303
  7.9 0.7 copy-start.3
  7.9 2.1 %copy-start.1 = (s32[1536]{0:T(1024)S(1)}, s32[1536]{0:T(1024)}, u32[]{:S(2)}) copy-start(s32[1536]{0:T(1024)} %param.11) | copy-start | bytes 18436
  9.3 0.7 copy-start.2
  10.1 2.7 %collective-permute-start.2 = (f32[24,1536]{1,0:T(8,128)S(1)}, f32[24,1536]{1,0:T(8,128)S(1)}, u32[]{:S(2)}, u32[]{:S(2)}) collective-permute-start(f32[24,1536]{1,0:T(8,128)S(1)} %collective-permute-done.1), channel_id=1, source_target_pairs={{0,2},{2,0},{4,6},{6,4},{8,10},{10,8},{12,14},{14,12},{16,18},{18,... | collective-permute-start | bytes 442376 | tf_op jit(solution)/shard_map/ppermute | solution.py:306
  12.8 22.9 %collective-permute-start.3 = (f32[72,1536]{1,0:T(8,128)S(1)}, f32[72,1536]{1,0:T(8,128)S(1)}, u32[]{:S(2)}, u32[]{:S(2)}) collective-permute-start(f32[72,1536]{1,0:T(8,128)S(1)} %constant_dynamic-update-slice_fusion.refs_3_), channel_id=1, source_target_pairs={{65,0},{29,1},{50,2},{15,3},{36,4},{57,5},{22,6},{43,7},{73,8},{37... | collective-permute-start | bytes 1327112 | tf_op jit(solution)/shard_map/ppermute | solution.py:308
  91.6 2.6 %copy-start = (f32[16,1536]{1,0:T(8,128)S(1)}, f32[16,1536]{1,0:T(8,128)}, u32[]{:S(2)}) copy-start(f32[16,1536]{1,0:T(8,128)} %param.8) | copy-start | bytes 294916
  91.7 22.2 %collective-permute-start.5 = (f32[64,1536]{1,0:T(8,128)S(1)}, f32[64,1536]{1,0:T(8,128)S(1)}, u32[]{:S(2)}, u32[]{:S(2)}) collective-permute-start(f32[64,1536]{1,0:T(8,128)S(1)} %pad_maximum_fusion), channel_id=1, source_target_pairs={{0,65},{1,29},{2,50},{3,15},{4,36},{5,57},{6,22},{7,43},{8,73},{9,... | collective-permute-start | bytes 1179656 | tf_op jit(solution)/shard_map/ppermute | solution.py:333
  114.0 1.5 %collective-permute-start.7 = (f32[32,1536]{1,0:T(8,128)S(1)}, f32[32,1536]{1,0:T(8,128)S(1)}, u32[]{:S(2)}, u32[]{:S(2)}) collective-permute-start(f32[32,1536]{1,0:T(8,128)S(1)} %pad_maximum_fusion.1), channel_id=1, source_target_pairs={{0,2},{2,0},{4,6},{6,4},{8,10},{10,8},{12,14},{14,12},{16,18},{18,... | collective-permute-start | bytes 589832 | tf_op jit(solution)/shard_map/ppermute | solution.py:351
  115.5 4.9 %collective-permute-start.8 = (f32[16,1536]{1,0:T(8,128)S(1)}, f32[16,1536]{1,0:T(8,128)S(1)}, u32[]{:S(2)}, u32[]{:S(2)}) collective-permute-start(f32[16,1536]{1,0:T(8,128)S(1)} %slice_add_fusion), channel_id=1, source_target_pairs={{0,4},{2,6},{4,0},{6,2},{8,12},{10,14},{12,8},{14,10},{16,20},{18,... | collective-permute-start | bytes 294920 | tf_op jit(solution)/shard_map/ppermute | solution.py:352
  116.2 3.5 %collective-permute-start.6 = (f32[32]{0:T(128)S(1)}, f32[32]{0:T(128)S(1)}, u32[]{:S(2)}, u32[]{:S(2)}) collective-permute-start(f32[32]{0:T(128)S(1)} %reduce_sum.49), channel_id=1, source_target_pairs={{0,1},{1,0},{2,3},{3,2},{4,5},{5,4},{6,7},{7,6},{8,9},{9,8},{10,11... | collective-permute-start | bytes 392 | tf_op jit(solution)/shard_map/ppermute | solution.py:355
  120.5 4.7 %collective-permute-start.9 = (f32[16,1536]{1,0:T(8,128)S(1)}, f32[16,1536]{1,0:T(8,128)S(1)}, u32[]{:S(2)}, u32[]{:S(2)}) collective-permute-start(f32[16,1536]{1,0:T(8,128)S(1)} %fusion.3), channel_id=1, source_target_pairs={{0,1},{1,0},{2,3},{3,2},{4,5},{5,4},{6,7},{7,6},{8,9},{9,8},{10,11... | collective-permute-start | bytes 294920 | tf_op jit(solution)/shard_map/ppermute | solution.py:354

commit v8 on v7

--- a/solution.py
+++ b/solution.py
@@ -12,6 +12,7 @@
 BOTH = ("blk", "grp")
 SHARD = 1536
 ROWS = 24
+DEPTH = 64
 CHUNKS = 4
 SUPER = SHARD * CHUNKS
 NSUPER = 16
@@ -147,32 +148,34 @@
 
     largest = jnp.full((NVEC, 1), 1e-30, f32)
     for chunk in chunks:
-        part = jnp.max(jnp.abs(chunk[3:19, :]), axis=1, keepdims=True)
+        part = jnp.max(jnp.abs(chunk[:NVEC, :]), axis=1, keepdims=True)
         largest = jnp.maximum(largest, part)
     upward = 1024.0 / largest
     downward = largest * (FACTOR / 1024.0)
 
+    line = lax.broadcasted_iota(jnp.int32, (8, SHARD), 0)
+    factors = jnp.where(line == 0, scale[0], jnp.where(line == 1, scale[1], scale[2]))
+
     for place, chunk in enumerate(chunks):
         span = slice(place * SHARD, (place + 1) * SHARD)
-        scaled = jnp.concatenate(
-            [(chunk[c : c + 1, :] - 4.0) * scale[c] for c in range(3)], axis=0
-        )
+        scaled = jnp.where(line < 3, (chunk[NVEC:, :] - 4.0) * factors, 0.0)
         a1, a2, a3 = pieces(scaled, 3)
         norm = jnp.sum(scaled * scaled, axis=0, keepdims=True)
         n1, n2, n3 = pieces(norm, 3)
-        one = jnp.ones_like(norm)
-        pad = jnp.zeros((8, SHARD), f32)
+        norms = jnp.where(line == 0, n1, jnp.where(line == 1, n2, n3))
+        pad = jnp.zeros_like(scaled)
+        late = jnp.where(line == 3, n1, jnp.where(line == 4, n2, n3))
+        tail = jnp.where(line < 3, 1.0, jnp.where(line < 6, late, 0.0))
         columns = jnp.concatenate(
-            [-2.0 * a1, -2.0 * a2, -2.0 * a1, -2.0 * a3, -2.0 * a2, -2.0 * a1,
-             one, one, one, n1, n2, n3, pad], axis=0)
+            [-2.0 * a1, -2.0 * a2, -2.0 * a1, -2.0 * a3, -2.0 * a2, -2.0 * a1, tail, pad], axis=0
+        )
         col_feat[:, span] = columns.astype(bf16)
-        vec = chunk[3:19, :] * upward
+        vec = chunk[:NVEC, :] * upward
         vectors[:, span] = jnp.concatenate(pieces(vec, 2), axis=0).astype(bf16)
         vectors8[:, span] = jnp.concatenate(pieces(vec, 2, f8), axis=0).astype(f8)
         if place < x_count:
-            rows = jnp.concatenate(
-                [a1, a1, a2, a1, a2, a3, n1, n2, n3, one, one, one, pad], axis=0
-            )
+            tail = jnp.where(line < 3, norms, jnp.where(line < 6, 1.0, 0.0))
+            rows = jnp.concatenate([a1, a1, a2, a1, a2, a3, tail, pad], axis=0)
             row_feat[span, :] = jnp.transpose(rows).astype(bf16)
     for ref in (row_sum, col_sum, hi1, lo1):
         ref[...] = jnp.zeros_like(ref)
@@ -244,7 +247,7 @@
         if place < x_count:
             total = total + row_sum[:, span]
         total = downward * (total[:NVEC] + total[NVEC:])
-        product = total * chunk[3:19, :]
+        product = total * chunk[:NVEC, :]
         for lane in range(0, SHARD, 128):
             curve = curve + product[:, lane : lane + 128]
         if place in sums_in:
@@ -276,8 +279,8 @@
         in_specs=[smem] * 2 + [vmem] * len(passed),
         out_specs=[vmem] * (count + 1),
         scratch_shapes=[
-            pltpu.VMEM((wide, 32), bf16),
-            pltpu.VMEM((32, every), bf16),
+            pltpu.VMEM((wide, DEPTH), bf16),
+            pltpu.VMEM((DEPTH, every), bf16),
             pltpu.VMEM((32, every), bf16),
             pltpu.VMEM((32, every), f8),
             pltpu.VMEM((32, wide), f32),
@@ -298,7 +301,7 @@
 
 
 def on_device(points, targets, length_scales, noise_levels, noise_class):
-    shard = jnp.concatenate([points, targets, jnp.zeros((ROWS - 19, SHARD), f32)], axis=0)
+    shard = jnp.concatenate([targets, points, jnp.zeros((ROWS - 19, SHARD), f32)], axis=0)
     swap = [(i, i ^ 1) for i in range(64)]
     first_column = lax.ppermute(shard, BOTH, column_route(0))
     beside = lax.ppermute(shard, "blk", [(i, i ^ 2) for i in range(64)])

time: 126 us -> 125 us (level)
  no operation moved by 1% of the time
where the time goes in v8:
time: 125 us
  Pallas kernels  75.4 us (60%)
  blocking collectives  19.2 us (15%)
  starting transfers between devices  16.7 us (13%)
  waiting for transfers between devices  8.14 us (7%)
  other arithmetic  2.45 us (2%)
  local copies, waits for them, and re-layouts  2.21 us (2%)
    pallas_call x2, Pallas kernels, run_tiles(): pl.pallas_call(functools.partial(tile_kernel, len(rows), places, begun),...  75.4 us
    all_to_all x1, blocking collectives, on_device(): lax.all_to_all(jnp.broadcast_to(scalars[None], (blocks, 2 * NVEC)), 'blk'...  19.2 us
    ppermute x1, starting transfers between devices, on_device(): first_column = lax.ppermute(shard, BOTH, column_route(0))  4.55 us
    ppermute x1, waiting for transfers between devices, on_device(): theirs = lax.ppermute(own, 'grp', [(0, 1), (1, 0)])  3 us
    ppermute x1, starting transfers between devices, on_device(): column_sums = lax.ppermute(column_sums, BOTH, backward(column_route(0)))  2.56 us
  transfers between devices with their start and end apart: 10, of which 5 were waited for; matrix products, arithmetic and copies ran while one was open for 2% of the time, Pallas kernels for 16%

profile of v8, /device:TPU:0, one launch (start us, length us, event | category | flops | bytes accessed | tf_op | source)
XLA Modules:
  0.0 124.9 jit_solution(1726954320298594968)
XLA Ops:
  0.6 0.1 pad.10.clone
  0.7 1.0 maximum_maximum_fusion.refs_2_
  1.7 1.7 %collective-permute-start.1 = (f32[24,1536]{1,0:T(8,128)S(1)}, f32[24,1536]{1,0:T(8,128)S(1)}, u32[]{:S(2)}, u32[]{:S(2)}) collective-permute-start(f32[24,1536]{1,0:T(8,128)S(1)} %maximum_maximum_fusion.refs_2_), channel_id=1, source_target_pairs={{0,4},{2,6},{4,0},{6,2},{8,12},{10,14},{12,8},{14,10},{16,20},{18,... | collective-permute-start | bytes 442376 | tf_op jit(solution)/shard_map/ppermute | solution.py:307
  3.4 0.0 collective-permute-start
  3.4 4.5 %collective-permute-start.4 = (f32[24,1536]{1,0:T(8,128)S(1)}, f32[24,1536]{1,0:T(8,128)S(1)}, u32[]{:S(2)}, u32[]{:S(2)}) collective-permute-start(f32[24,1536]{1,0:T(8,128)S(1)} %maximum_maximum_fusion.refs_2_), channel_id=1, source_target_pairs={{65,0},{29,1},{50,2},{15,3},{36,4},{57,5},{22,6},{43,7},{73,8},{37... | collective-permute-start | bytes 442376 | tf_op jit(solution)/shard_map/ppermute | solution.py:306
  7.9 0.0 copy-start.3
  7.9 0.0 copy-start.1
  7.9 0.7 copy-done.3
  8.6 0.7 constant_dynamic-slice_fusion
  9.3 0.0 copy-start.2
  9.3 0.7 dynamic-slice_bitcast_fusion.refs_0_
  10.0 0.0 copy-done.1
  10.0 0.0 copy-done.2
  10.0 0.1 select_reduce_fusion
  10.1 0.0 collective-permute-done
  10.1 0.0 collective-permute-done.1
  10.1 1.7 %collective-permute-start.2 = (f32[24,1536]{1,0:T(8,128)S(1)}, f32[24,1536]{1,0:T(8,128)S(1)}, u32[]{:S(2)}, u32[]{:S(2)}) collective-permute-start(f32[24,1536]{1,0:T(8,128)S(1)} %collective-permute-done.1), channel_id=1, source_target_pairs={{0,2},{2,0},{4,6},{6,4},{8,10},{10,8},{12,14},{14,12},{16,18},{18,... | collective-permute-start | bytes 442376 | tf_op jit(solution)/shard_map/ppermute | solution.py:309
  11.8 1.0 collective-permute-done.2
  12.8 2.4 %collective-permute-start.3 = (f32[72,1536]{1,0:T(8,128)S(1)}, f32[72,1536]{1,0:T(8,128)S(1)}, u32[]{:S(2)}, u32[]{:S(2)}) collective-permute-start(f32[72,1536]{1,0:T(8,128)S(1)} %constant_dynamic-update-slice_fusion.refs_3_), channel_id=1, source_target_pairs={{65,0},{29,1},{50,2},{15,3},{36,4},{57,5},{22,6},{43,7},{73,8},{37... | collective-permute-start | bytes 1327112 | tf_op jit(solution)/shard_map/ppermute | solution.py:311
  15.2 0.0 collective-permute-done.4.refs_4_
  15.2 20.1 %shard_map.86 = (f32[16,1536]{1,0:T(8,128)S(1)}, f32[16,1536]{1,0:T(8,128)S(1)}, f32[16,1536]{1,0:T(8,128)S(1)}, f32[16,1536]{1,0:T(8,128)S(1)}, f32[16,1536]{1,0:T(8,128)S(1)}, /*index=5*/f32[16,128]{1,0:T(8,128)S(1)}) custom-call(s32[73]{0:T(128)S(1)} %dynamic-slice_bitcast_fusion.refs_0_, f32[3]{0:T(128)S(1)} %broadcast_divide_fusion.refs_1_, ...), custom_call_target="tpu_custom_call" | custom-call | flops 24089999360 | bytes 2000000 | tf_op jit(solution)/shard_map/pallas_call | solution.py:275
  35.3 0.0 collective-permute-done.3.refs_4_
  35.3 55.3 %shard_map.87 = (f32[16,1536]{1,0:T(8,128)S(1)}, f32[16,1536]{1,0:T(8,128)S(1)}, f32[16,1536]{1,0:T(8,128)S(1)}, f32[16,1536]{1,0:T(8,128)S(1)}, f32[16,1536]{1,...) custom-call(s32[223]{0:T(256)S(1)} %bitcast.3, ...), custom_call_target="tpu_custom_call" | custom-call | flops 73589997568 | bytes 2000000 | tf_op jit(solution)/shard_map/pallas_call | solution.py:275
  90.6 0.0 copy-start
  90.6 2.6 %collective-permute-start.5 = (f32[64,1536]{1,0:T(8,128)S(1)}, f32[64,1536]{1,0:T(8,128)S(1)}, u32[]{:S(2)}, u32[]{:S(2)}) collective-permute-start(f32[64,1536]{1,0:T(8,128)S(1)} %pad_maximum_fusion), channel_id=1, source_target_pairs={{0,65},{1,29},{2,50},{3,15},{4,36},{5,57},{6,22},{7,43},{8,73},{9,... | collective-permute-start | bytes 1179656 | tf_op jit(solution)/shard_map/ppermute | solution.py:336
  93.2 0.0 copy-done
  93.2 0.1 multiply_reduce_fusion
  93.3 0.1 reduce_sum.46
  93.4 0.1 pad_maximum_fusion.2
  93.6 19.2 %all_to_all.6 = f32[64,1,32]{2,1,0:T(1,128)S(1)} all-to-all(f32[64,1,32]{2,1,0:T(1,128)S(1)} %broadcast_in_dim.29), channel_id=1, replica_groups=mesh['blk'=64,'grp'=2] {'blk'}, dimensions={0} | all-to-all | bytes 16384 | tf_op jit(solution)/shard_map/all_to_all | solution.py:347
  112.8 0.1 reduce_sum.49
  112.9 0.0 collective-permute-done.5
  112.9 0.1 collective-permute-start.7
  113.0 1.4 %collective-permute-done.7 = f32[32,1536]{1,0:T(8,128)S(1)} collective-permute-done((f32[32,1536]{1,0:T(8,128)S(1)}, f32[32,1536]{1,0:T(8,128)S(1)}, u32[]{:S(2)}, u32[]{:S(2)}) %collective-permute-start.7) | collective-permute-done | bytes 196640 | tf_op jit(solution)/shard_map/ppermute | solution.py:354
  114.5 0.7 collective-permute-start.8
  115.1 1.5 %collective-permute-start.6 = (f32[32]{0:T(128)S(1)}, f32[32]{0:T(128)S(1)}, u32[]{:S(2)}, u32[]{:S(2)}) collective-permute-start(f32[32]{0:T(128)S(1)} %reduce_sum.49), channel_id=1, source_target_pairs={{0,1},{1,0},{2,3},{3,2},{4,5},{5,4},{6,7},{7,6},{8,9},{9,8},{10,11... | collective-permute-start | bytes 392 | tf_op jit(solution)/shard_map/ppermute | solution.py:358
  116.7 2.0 %collective-permute-done.6 = f32[32]{0:T(128)S(1)} collective-permute-done((f32[32]{0:T(128)S(1)}, f32[32]{0:T(128)S(1)}, u32[]{:S(2)}, u32[]{:S(2)}) %collective-permute-start.6) | collective-permute-done | bytes 160 | tf_op jit(solution)/shard_map/ppermute | solution.py:358
  118.7 0.7 collective-permute-done.8
  119.4 1.6 %collective-permute-start.9 = (f32[16,1536]{1,0:T(8,128)S(1)}, f32[16,1536]{1,0:T(8,128)S(1)}, u32[]{:S(2)}, u32[]{:S(2)}) collective-permute-start(f32[16,1536]{1,0:T(8,128)S(1)} %fusion.3), channel_id=1, source_target_pairs={{0,1},{1,0},{2,3},{3,2},{4,5},{5,4},{6,7},{7,6},{8,9},{9,8},{10,11... | collective-permute-start | bytes 294920 | tf_op jit(solution)/shard_map/ppermute | solution.py:357
  121.1 0.1 slice_divide_fusion
  121.1 3.0 %collective-permute-done.9 = f32[16,1536]{1,0:T(8,128)S(1)} collective-permute-done((f32[16,1536]{1,0:T(8,128)S(1)}, f32[16,1536]{1,0:T(8,128)S(1)}, u32[]{:S(2)}, u32[]{:S(2)}) %collective-permute-start.9) | collective-permute-done | bytes 98336 | tf_op jit(solution)/shard_map/ppermute | solution.py:357
  124.1 0.8 fusion.2
  (13 shorter events, 0.2 us)
Async XLA Ops:
  1.7 8.4 %collective-permute-start.1 = (f32[24,1536]{1,0:T(8,128)S(1)}, f32[24,1536]{1,0:T(8,128)S(1)}, u32[]{:S(2)}, u32[]{:S(2)}) collective-permute-start(f32[24,1536]{1,0:T(8,128)S(1)} %maximum_maximum_fusion.refs_2_), channel_id=1, source_target_pairs={{0,4},{2,6},{4,0},{6,2},{8,12},{10,14},{12,8},{14,10},{16,20},{18,... | collective-permute-start | bytes 442376 | tf_op jit(solution)/shard_map/ppermute | solution.py:307
  3.4 6.7 %collective-permute-start = (f32[24,1536]{1,0:T(8,128)S(1)}, f32[24,1536]{1,0:T(8,128)S(1)}, u32[]{:S(2)}, u32[]{:S(2)}) collective-permute-start(f32[24,1536]{1,0:T(8,128)S(1)} %maximum_maximum_fusion.refs_2_), channel_id=1, source_target_pairs={{0,2},{2,0},{4,6},{6,4},{8,10},{10,8},{12,14},{14,12},{16,18},{18,... | collective-permute-start | bytes 442376 | tf_op jit(solution)/shard_map/ppermute | solution.py:308
  3.4 11.8 %collective-permute-start.4 = (f32[24,1536]{1,0:T(8,128)S(1)}, f32[24,1536]{1,0:T(8,128)S(1)}, u32[]{:S(2)}, u32[]{:S(2)}) collective-permute-start(f32[24,1536]{1,0:T(8,128)S(1)} %maximum_maximum_fusion.refs_2_), channel_id=1, source_target_pairs={{65,0},{29,1},{50,2},{15,3},{36,4},{57,5},{22,6},{43,7},{73,8},{37... | collective-permute-start | bytes 442376 | tf_op jit(solution)/shard_map/ppermute | solution.py:306
  7.9 0.7 copy-start.3
  7.9 2.1 %copy-start.1 = (s32[1536]{0:T(1024)S(1)}, s32[1536]{0:T(1024)}, u32[]{:S(2)}) copy-start(s32[1536]{0:T(1024)} %param.11) | copy-start | bytes 18436
  9.3 0.7 copy-start.2
  10.1 2.7 %collective-permute-start.2 = (f32[24,1536]{1,0:T(8,128)S(1)}, f32[24,1536]{1,0:T(8,128)S(1)}, u32[]{:S(2)}, u32[]{:S(2)}) collective-permute-start(f32[24,1536]{1,0:T(8,128)S(1)} %collective-permute-done.1), channel_id=1, source_target_pairs={{0,2},{2,0},{4,6},{6,4},{8,10},{10,8},{12,14},{14,12},{16,18},{18,... | collective-permute-start | bytes 442376 | tf_op jit(solution)/shard_map/ppermute | solution.py:309
  12.8 22.5 %collective-permute-start.3 = (f32[72,1536]{1,0:T(8,128)S(1)}, f32[72,1536]{1,0:T(8,128)S(1)}, u32[]{:S(2)}, u32[]{:S(2)}) collective-permute-start(f32[72,1536]{1,0:T(8,128)S(1)} %constant_dynamic-update-slice_fusion.refs_3_), channel_id=1, source_target_pairs={{65,0},{29,1},{50,2},{15,3},{36,4},{57,5},{22,6},{43,7},{73,8},{37... | collective-permute-start | bytes 1327112 | tf_op jit(solution)/shard_map/ppermute | solution.py:311
  90.6 2.6 %copy-start = (f32[16,1536]{1,0:T(8,128)S(1)}, f32[16,1536]{1,0:T(8,128)}, u32[]{:S(2)}) copy-start(f32[16,1536]{1,0:T(8,128)} %param.8) | copy-start | bytes 294916
  90.6 22.2 %collective-permute-start.5 = (f32[64,1536]{1,0:T(8,128)S(1)}, f32[64,1536]{1,0:T(8,128)S(1)}, u32[]{:S(2)}, u32[]{:S(2)}) collective-permute-start(f32[64,1536]{1,0:T(8,128)S(1)} %pad_maximum_fusion), channel_id=1, source_target_pairs={{0,65},{1,29},{2,50},{3,15},{4,36},{5,57},{6,22},{7,43},{8,73},{9,... | collective-permute-start | bytes 1179656 | tf_op jit(solution)/shard_map/ppermute | solution.py:336
  112.9 1.5 %collective-permute-start.7 = (f32[32,1536]{1,0:T(8,128)S(1)}, f32[32,1536]{1,0:T(8,128)S(1)}, u32[]{:S(2)}, u32[]{:S(2)}) collective-permute-start(f32[32,1536]{1,0:T(8,128)S(1)} %pad_maximum_fusion.1), channel_id=1, source_target_pairs={{0,2},{2,0},{4,6},{6,4},{8,10},{10,8},{12,14},{14,12},{16,18},{18,... | collective-permute-start | bytes 589832 | tf_op jit(solution)/shard_map/ppermute | solution.py:354
  114.5 4.9 %collective-permute-start.8 = (f32[16,1536]{1,0:T(8,128)S(1)}, f32[16,1536]{1,0:T(8,128)S(1)}, u32[]{:S(2)}, u32[]{:S(2)}) collective-permute-start(f32[16,1536]{1,0:T(8,128)S(1)} %slice_add_fusion), channel_id=1, source_target_pairs={{0,4},{2,6},{4,0},{6,2},{8,12},{10,14},{12,8},{14,10},{16,20},{18,... | collective-permute-start | bytes 294920 | tf_op jit(solution)/shard_map/ppermute | solution.py:355
  115.1 3.5 %collective-permute-start.6 = (f32[32]{0:T(128)S(1)}, f32[32]{0:T(128)S(1)}, u32[]{:S(2)}, u32[]{:S(2)}) collective-permute-start(f32[32]{0:T(128)S(1)} %reduce_sum.49), channel_id=1, source_target_pairs={{0,1},{1,0},{2,3},{3,2},{4,5},{5,4},{6,7},{7,6},{8,9},{9,8},{10,11... | collective-permute-start | bytes 392 | tf_op jit(solution)/shard_map/ppermute | solution.py:358
  119.4 4.7 %collective-permute-start.9 = (f32[16,1536]{1,0:T(8,128)S(1)}, f32[16,1536]{1,0:T(8,128)S(1)}, u32[]{:S(2)}, u32[]{:S(2)}) collective-permute-start(f32[16,1536]{1,0:T(8,128)S(1)} %fusion.3), channel_id=1, source_target_pairs={{0,1},{1,0},{2,3},{3,2},{4,5},{5,4},{6,7},{7,6},{8,9},{9,8},{10,11... | collective-permute-start | bytes 294920 | tf_op jit(solution)/shard_map/ppermute | solution.py:357

commit v9 on v8

--- a/solution.py
+++ b/solution.py
@@ -20,7 +20,7 @@
 TALL = 768
 WIDE = 512
 SUB = 256
-UNROLL = 8
+UNROLL = 12
 LOG2E = math.log2(math.e)
 SHIFT = 1.5 * LOG2E
 OFFSET = 0.75 * LOG2E * LOG2E
@@ -214,8 +214,8 @@
     def both(ahead, ahead_hi, ahead_lo, now, hi, lo):
         subs = [(x, y) for x in range(0, WIDE, SUB) for y in range(0, TALL, SUB)]
         sides = ((hi, vectors), (lo, vectors8))
-        work = [(consume_rows, *side, y) for y in range(0, TALL, SUB) for side in sides]
-        work += [(consume_columns, *side, x) for x in range(0, WIDE, SUB) for side in sides]
+        work = [(consume_rows, *side, y) for side in sides for y in range(0, TALL, SUB)]
+        work += [(consume_columns, *side, x) for side in sides for x in range(0, WIDE, SUB)]
         done = 0
         for n, (x, y) in enumerate(subs):
             if ahead is not None:

time: 125 us -> 124 us (level)
  no operation moved by 1% of the time
where the time goes in v9:
time: 124 us
  Pallas kernels  74.4 us (60%)
  blocking collectives  19.2 us (15%)
  starting transfers between devices  16.7 us (13%)
  waiting for transfers between devices  8.14 us (7%)
  other arithmetic  2.45 us (2%)
  local copies, waits for them, and re-layouts  2.21 us (2%)
    pallas_call x2, Pallas kernels, run_tiles(): pl.pallas_call(functools.partial(tile_kernel, len(rows), places, begun),...  74.4 us
    all_to_all x1, blocking collectives, on_device(): lax.all_to_all(jnp.broadcast_to(scalars[None], (blocks, 2 * NVEC)), 'blk'...  19.2 us
    ppermute x1, starting transfers between devices, on_device(): first_column = lax.ppermute(shard, BOTH, column_route(0))  4.55 us
    ppermute x1, waiting for transfers between devices, on_device(): theirs = lax.ppermute(own, 'grp', [(0, 1), (1, 0)])  2.99 us
    ppermute x1, starting transfers between devices, on_device(): column_sums = lax.ppermute(column_sums, BOTH, backward(column_route(0)))  2.58 us
  transfers between devices with their start and end apart: 10, of which 5 were waited for; matrix products, arithmetic and copies ran while one was open for 2% of the time, Pallas kernels for 16%

profile of v9, /device:TPU:0, one launch (start us, length us, event | category | flops | bytes accessed | tf_op | source)
XLA Modules:
  0.0 123.9 jit_solution(11302893830600816689)
XLA Ops:
  0.6 0.1 pad.10.clone
  0.7 1.0 maximum_maximum_fusion.refs_2_
  1.7 1.7 %collective-permute-start.1 = (f32[24,1536]{1,0:T(8,128)S(1)}, f32[24,1536]{1,0:T(8,128)S(1)}, u32[]{:S(2)}, u32[]{:S(2)}) collective-permute-start(f32[24,1536]{1,0:T(8,128)S(1)} %maximum_maximum_fusion.refs_2_), channel_id=1, source_target_pairs={{0,4},{2,6},{4,0},{6,2},{8,12},{10,14},{12,8},{14,10},{16,20},{18,... | collective-permute-start | bytes 442376 | tf_op jit(solution)/shard_map/ppermute | solution.py:307
  3.4 0.0 collective-permute-start
  3.4 4.5 %collective-permute-start.4 = (f32[24,1536]{1,0:T(8,128)S(1)}, f32[24,1536]{1,0:T(8,128)S(1)}, u32[]{:S(2)}, u32[]{:S(2)}) collective-permute-start(f32[24,1536]{1,0:T(8,128)S(1)} %maximum_maximum_fusion.refs_2_), channel_id=1, source_target_pairs={{65,0},{29,1},{50,2},{15,3},{36,4},{57,5},{22,6},{43,7},{73,8},{37... | collective-permute-start | bytes 442376 | tf_op jit(solution)/shard_map/ppermute | solution.py:306
  7.9 0.0 copy-start.3
  7.9 0.0 copy-start.1
  7.9 0.7 copy-done.3
  8.6 0.7 constant_dynamic-slice_fusion
  9.3 0.0 copy-start.2
  9.3 0.7 dynamic-slice_bitcast_fusion.refs_0_
  10.0 0.0 copy-done.1
  10.0 0.0 copy-done.2
  10.0 0.1 select_reduce_fusion
  10.1 0.0 collective-permute-done
  10.1 0.0 collective-permute-done.1
  10.1 1.7 %collective-permute-start.2 = (f32[24,1536]{1,0:T(8,128)S(1)}, f32[24,1536]{1,0:T(8,128)S(1)}, u32[]{:S(2)}, u32[]{:S(2)}) collective-permute-start(f32[24,1536]{1,0:T(8,128)S(1)} %collective-permute-done.1), channel_id=1, source_target_pairs={{0,2},{2,0},{4,6},{6,4},{8,10},{10,8},{12,14},{14,12},{16,18},{18,... | collective-permute-start | bytes 442376 | tf_op jit(solution)/shard_map/ppermute | solution.py:309
  11.8 1.0 collective-permute-done.2
  12.8 2.4 %collective-permute-start.3 = (f32[72,1536]{1,0:T(8,128)S(1)}, f32[72,1536]{1,0:T(8,128)S(1)}, u32[]{:S(2)}, u32[]{:S(2)}) collective-permute-start(f32[72,1536]{1,0:T(8,128)S(1)} %constant_dynamic-update-slice_fusion.refs_3_), channel_id=1, source_target_pairs={{65,0},{29,1},{50,2},{15,3},{36,4},{57,5},{22,6},{43,7},{73,8},{37... | collective-permute-start | bytes 1327112 | tf_op jit(solution)/shard_map/ppermute | solution.py:311
  15.2 0.0 collective-permute-done.4.refs_4_
  15.2 19.8 %shard_map.86 = (f32[16,1536]{1,0:T(8,128)S(1)}, f32[16,1536]{1,0:T(8,128)S(1)}, f32[16,1536]{1,0:T(8,128)S(1)}, f32[16,1536]{1,0:T(8,128)S(1)}, f32[16,1536]{1,0:T(8,128)S(1)}, /*index=5*/f32[16,128]{1,0:T(8,128)S(1)}) custom-call(s32[73]{0:T(128)S(1)} %dynamic-slice_bitcast_fusion.refs_0_, f32[3]{0:T(128)S(1)} %broadcast_divide_fusion.refs_1_, ...), custom_call_target="tpu_custom_call" | custom-call | flops 24089999360 | bytes 2000000 | tf_op jit(solution)/shard_map/pallas_call | solution.py:275
  35.0 0.0 collective-permute-done.3.refs_4_
  35.0 54.6 %shard_map.87 = (f32[16,1536]{1,0:T(8,128)S(1)}, f32[16,1536]{1,0:T(8,128)S(1)}, f32[16,1536]{1,0:T(8,128)S(1)}, f32[16,1536]{1,0:T(8,128)S(1)}, f32[16,1536]{1,...) custom-call(s32[223]{0:T(256)S(1)} %bitcast.3, ...), custom_call_target="tpu_custom_call" | custom-call | flops 73589997568 | bytes 2000000 | tf_op jit(solution)/shard_map/pallas_call | solution.py:275
  89.6 0.0 copy-start
  89.6 2.6 %collective-permute-start.5 = (f32[64,1536]{1,0:T(8,128)S(1)}, f32[64,1536]{1,0:T(8,128)S(1)}, u32[]{:S(2)}, u32[]{:S(2)}) collective-permute-start(f32[64,1536]{1,0:T(8,128)S(1)} %pad_maximum_fusion), channel_id=1, source_target_pairs={{0,65},{1,29},{2,50},{3,15},{4,36},{5,57},{6,22},{7,43},{8,73},{9,... | collective-permute-start | bytes 1179656 | tf_op jit(solution)/shard_map/ppermute | solution.py:336
  92.2 0.0 copy-done
  92.2 0.1 multiply_reduce_fusion
  92.4 0.1 reduce_sum.46
  92.5 0.1 pad_maximum_fusion.2
  92.6 19.2 %all_to_all.6 = f32[64,1,32]{2,1,0:T(1,128)S(1)} all-to-all(f32[64,1,32]{2,1,0:T(1,128)S(1)} %broadcast_in_dim.29), channel_id=1, replica_groups=mesh['blk'=64,'grp'=2] {'blk'}, dimensions={0} | all-to-all | bytes 16384 | tf_op jit(solution)/shard_map/all_to_all | solution.py:347
  111.8 0.1 reduce_sum.49
  111.9 0.0 collective-permute-done.5
  112.0 0.1 collective-permute-start.7
  112.1 1.4 %collective-permute-done.7 = f32[32,1536]{1,0:T(8,128)S(1)} collective-permute-done((f32[32,1536]{1,0:T(8,128)S(1)}, f32[32,1536]{1,0:T(8,128)S(1)}, u32[]{:S(2)}, u32[]{:S(2)}) %collective-permute-start.7) | collective-permute-done | bytes 196640 | tf_op jit(solution)/shard_map/ppermute | solution.py:354
  113.5 0.7 collective-permute-start.8
  114.2 1.5 %collective-permute-start.6 = (f32[32]{0:T(128)S(1)}, f32[32]{0:T(128)S(1)}, u32[]{:S(2)}, u32[]{:S(2)}) collective-permute-start(f32[32]{0:T(128)S(1)} %reduce_sum.49), channel_id=1, source_target_pairs={{0,1},{1,0},{2,3},{3,2},{4,5},{5,4},{6,7},{7,6},{8,9},{9,8},{10,11... | collective-permute-start | bytes 392 | tf_op jit(solution)/shard_map/ppermute | solution.py:358
  115.7 2.0 %collective-permute-done.6 = f32[32]{0:T(128)S(1)} collective-permute-done((f32[32]{0:T(128)S(1)}, f32[32]{0:T(128)S(1)}, u32[]{:S(2)}, u32[]{:S(2)}) %collective-permute-start.6) | collective-permute-done | bytes 160 | tf_op jit(solution)/shard_map/ppermute | solution.py:358
  117.7 0.7 collective-permute-done.8
  118.5 1.6 %collective-permute-start.9 = (f32[16,1536]{1,0:T(8,128)S(1)}, f32[16,1536]{1,0:T(8,128)S(1)}, u32[]{:S(2)}, u32[]{:S(2)}) collective-permute-start(f32[16,1536]{1,0:T(8,128)S(1)} %fusion.3), channel_id=1, source_target_pairs={{0,1},{1,0},{2,3},{3,2},{4,5},{5,4},{6,7},{7,6},{8,9},{9,8},{10,11... | collective-permute-start | bytes 294920 | tf_op jit(solution)/shard_map/ppermute | solution.py:357
  120.1 0.1 slice_divide_fusion
  120.2 3.0 %collective-permute-done.9 = f32[16,1536]{1,0:T(8,128)S(1)} collective-permute-done((f32[16,1536]{1,0:T(8,128)S(1)}, f32[16,1536]{1,0:T(8,128)S(1)}, u32[]{:S(2)}, u32[]{:S(2)}) %collective-permute-start.9) | collective-permute-done | bytes 98336 | tf_op jit(solution)/shard_map/ppermute | solution.py:357
  123.2 0.8 fusion.2
  (13 shorter events, 0.2 us)
Async XLA Ops:
  1.7 8.4 %collective-permute-start.1 = (f32[24,1536]{1,0:T(8,128)S(1)}, f32[24,1536]{1,0:T(8,128)S(1)}, u32[]{:S(2)}, u32[]{:S(2)}) collective-permute-start(f32[24,1536]{1,0:T(8,128)S(1)} %maximum_maximum_fusion.refs_2_), channel_id=1, source_target_pairs={{0,4},{2,6},{4,0},{6,2},{8,12},{10,14},{12,8},{14,10},{16,20},{18,... | collective-permute-start | bytes 442376 | tf_op jit(solution)/shard_map/ppermute | solution.py:307
  3.4 6.7 %collective-permute-start = (f32[24,1536]{1,0:T(8,128)S(1)}, f32[24,1536]{1,0:T(8,128)S(1)}, u32[]{:S(2)}, u32[]{:S(2)}) collective-permute-start(f32[24,1536]{1,0:T(8,128)S(1)} %maximum_maximum_fusion.refs_2_), channel_id=1, source_target_pairs={{0,2},{2,0},{4,6},{6,4},{8,10},{10,8},{12,14},{14,12},{16,18},{18,... | collective-permute-start | bytes 442376 | tf_op jit(solution)/shard_map/ppermute | solution.py:308
  3.4 11.8 %collective-permute-start.4 = (f32[24,1536]{1,0:T(8,128)S(1)}, f32[24,1536]{1,0:T(8,128)S(1)}, u32[]{:S(2)}, u32[]{:S(2)}) collective-permute-start(f32[24,1536]{1,0:T(8,128)S(1)} %maximum_maximum_fusion.refs_2_), channel_id=1, source_target_pairs={{65,0},{29,1},{50,2},{15,3},{36,4},{57,5},{22,6},{43,7},{73,8},{37... | collective-permute-start | bytes 442376 | tf_op jit(solution)/shard_map/ppermute | solution.py:306
  7.9 0.7 copy-start.3
  7.9 2.1 %copy-start.1 = (s32[1536]{0:T(1024)S(1)}, s32[1536]{0:T(1024)}, u32[]{:S(2)}) copy-start(s32[1536]{0:T(1024)} %param.11) | copy-start | bytes 18436
  9.3 0.7 copy-start.2
  10.1 2.7 %collective-permute-start.2 = (f32[24,1536]{1,0:T(8,128)S(1)}, f32[24,1536]{1,0:T(8,128)S(1)}, u32[]{:S(2)}, u32[]{:S(2)}) collective-permute-start(f32[24,1536]{1,0:T(8,128)S(1)} %collective-permute-done.1), channel_id=1, source_target_pairs={{0,2},{2,0},{4,6},{6,4},{8,10},{10,8},{12,14},{14,12},{16,18},{18,... | collective-permute-start | bytes 442376 | tf_op jit(solution)/shard_map/ppermute | solution.py:309
  12.8 22.2 %collective-permute-start.3 = (f32[72,1536]{1,0:T(8,128)S(1)}, f32[72,1536]{1,0:T(8,128)S(1)}, u32[]{:S(2)}, u32[]{:S(2)}) collective-permute-start(f32[72,1536]{1,0:T(8,128)S(1)} %constant_dynamic-update-slice_fusion.refs_3_), channel_id=1, source_target_pairs={{65,0},{29,1},{50,2},{15,3},{36,4},{57,5},{22,6},{43,7},{73,8},{37... | collective-permute-start | bytes 1327112 | tf_op jit(solution)/shard_map/ppermute | solution.py:311
  89.6 2.6 %copy-start = (f32[16,1536]{1,0:T(8,128)S(1)}, f32[16,1536]{1,0:T(8,128)}, u32[]{:S(2)}) copy-start(f32[16,1536]{1,0:T(8,128)} %param.8) | copy-start | bytes 294916
  89.6 22.3 %collective-permute-start.5 = (f32[64,1536]{1,0:T(8,128)S(1)}, f32[64,1536]{1,0:T(8,128)S(1)}, u32[]{:S(2)}, u32[]{:S(2)}) collective-permute-start(f32[64,1536]{1,0:T(8,128)S(1)} %pad_maximum_fusion), channel_id=1, source_target_pairs={{0,65},{1,29},{2,50},{3,15},{4,36},{5,57},{6,22},{7,43},{8,73},{9,... | collective-permute-start | bytes 1179656 | tf_op jit(solution)/shard_map/ppermute | solution.py:336
  112.0 1.5 %collective-permute-start.7 = (f32[32,1536]{1,0:T(8,128)S(1)}, f32[32,1536]{1,0:T(8,128)S(1)}, u32[]{:S(2)}, u32[]{:S(2)}) collective-permute-start(f32[32,1536]{1,0:T(8,128)S(1)} %pad_maximum_fusion.1), channel_id=1, source_target_pairs={{0,2},{2,0},{4,6},{6,4},{8,10},{10,8},{12,14},{14,12},{16,18},{18,... | collective-permute-start | bytes 589832 | tf_op jit(solution)/shard_map/ppermute | solution.py:354
  113.5 4.9 %collective-permute-start.8 = (f32[16,1536]{1,0:T(8,128)S(1)}, f32[16,1536]{1,0:T(8,128)S(1)}, u32[]{:S(2)}, u32[]{:S(2)}) collective-permute-start(f32[16,1536]{1,0:T(8,128)S(1)} %slice_add_fusion), channel_id=1, source_target_pairs={{0,4},{2,6},{4,0},{6,2},{8,12},{10,14},{12,8},{14,10},{16,20},{18,... | collective-permute-start | bytes 294920 | tf_op jit(solution)/shard_map/ppermute | solution.py:355
  114.2 3.5 %collective-permute-start.6 = (f32[32]{0:T(128)S(1)}, f32[32]{0:T(128)S(1)}, u32[]{:S(2)}, u32[]{:S(2)}) collective-permute-start(f32[32]{0:T(128)S(1)} %reduce_sum.49), channel_id=1, source_target_pairs={{0,1},{1,0},{2,3},{3,2},{4,5},{5,4},{6,7},{7,6},{8,9},{9,8},{10,11... | collective-permute-start | bytes 392 | tf_op jit(solution)/shard_map/ppermute | solution.py:358
  118.5 4.7 %collective-permute-start.9 = (f32[16,1536]{1,0:T(8,128)S(1)}, f32[16,1536]{1,0:T(8,128)S(1)}, u32[]{:S(2)}, u32[]{:S(2)}) collective-permute-start(f32[16,1536]{1,0:T(8,128)S(1)} %fusion.3), channel_id=1, source_target_pairs={{0,1},{1,0},{2,3},{3,2},{4,5},{5,4},{6,7},{7,6},{8,9},{9,8},{10,11... | collective-permute-start | bytes 294920 | tf_op jit(solution)/shard_map/ppermute | solution.py:357
